TPU v7x, 256 devices: a whole 4x4x8 slice. The times are simulated.
256 devices in a mesh: azim: 32 (over z, x), rad: 4 (over y_hi, core), group: 2 (over y_lo).
Axes of the slice: x: 4, y: 4 (y_hi: 2, y_lo: 2; y = y_hi * 2 + y_lo), z: 8, core: 2. Of those that a mesh axis runs over, the one named last changes fastest.
Arguments:
- les_state: float32 [5, 320, 40, 1280], P(None, 'azim', 'rad', 'group'), may hold values from -1 to 6, as said below
- acoustic_state: float32 [4, 160, 20, 1280], P(None, 'azim', 'rad', 'group'), may hold values from -6 to 6
- mean_density: float32 [160, 20, 1280], P('azim', 'rad', 'group'), may hold values from 0.8 to 1.25
- mean_sound: float32 [160, 20, 1280], P('azim', 'rad', 'group'), may hold values from 0.8 to 1.2
- mean_velocity: float32 [3, 160, 20, 1280], P(None, 'azim', 'rad', 'group'), may hold values from -0.4 to 0.4
- projection: float32 [8, 125, 125], replicated, may hold values from -0.5 to 0.5
- intersection_counts: int32 [32, 4, 2, 128], P('azim', 'rad', 'group'), may hold values from 1 to 16, 768 in all within a row
- intersection_elem: int32 [32, 4, 2, 768], P('azim', 'rad', 'group'), may hold values from 0 to 767
- intersection_pattern: int32 [32, 4, 2, 768], P('azim', 'rad', 'group'), may hold values from 0 to 7
Outputs:
- les_next: float32 [5, 320, 40, 1280], P(None, 'azim', 'rad', 'group')
- acoustic_next: float32 [4, 160, 20, 1280], P(None, 'azim', 'rad', 'group')
Inputs may be any that keep to these rules, and one draw needn't show every extreme that they name: `les_state`: density lies in 0.7 to 1.4 and pressure 0.4 (E - |m|^2 / (2 rho)) in 0.5 to 2 at every node. `intersection_counts`: the counts of one block sum to 768.
All inputs are finite; a program needn't handle non-finite values.
Results may differ from a plain program's by a relative error of at most 0.0003.
Values sent between devices are 32-bit elements; how exact they have to be, the bound alone decides.
No kernel may reach another device: no remote copies, remote signals or barrier semaphores. Data moves between devices by JAX's collectives and lax.ppermute only.
A program may use at most 128 MiB of HBM per device.

v0:
```python
from functools import partial
import math

import jax
import jax.numpy as jnp
import numpy as np
from jax import lax
from jax.sharding import PartitionSpec as P

EA = 2
ER = 2
EX = 128
EL = 512
COL = 256
AA = 1
AR = 1
AEL = 128


HEAT_RATIO = 1.4
TIME_STEP = 0.05
EDGE_WEIGHT = 0.1


def with_halo(block, sides, width):
    for axis, dim in sides:
        count = lax.axis_size(axis)
        forward = [(i, i + 1) for i in range(count - 1)]
        forward.append((count - 1, 0))
        backward = [(target, source) for source, target in forward]
        low = lax.ppermute(
            lax.slice_in_dim(block, block.shape[dim] - width, None, axis=dim), axis, forward
        )
        high = lax.ppermute(lax.slice_in_dim(block, 0, width, axis=dim), axis, backward)
        block = jnp.concatenate([low, block, high], axis=dim)
    return block


def shifted(value, axis, steps):
    count = lax.axis_size(axis)
    pairs = [(source, (source + steps) % count) for source in range(count)]
    return lax.ppermute(value, axis, pairs)


def gll_derivative():
    points = np.array([-1.0, -math.sqrt(3.0 / 7.0), 0.0, math.sqrt(3.0 / 7.0), 1.0])
    barycentric = np.array(
        [1.0 / np.prod([points[j] - points[k] for k in range(5) if k != j]) for j in range(5)]
    )
    matrix = np.zeros((5, 5))
    for i in range(5):
        for j in range(5):
            if i != j:
                matrix[i, j] = barycentric[j] / barycentric[i] / (points[i] - points[j])
        matrix[i, i] = -np.sum(matrix[i])
    return jnp.asarray(matrix, jnp.float32)


def along_axis(values, matrix, axis_dim):
    extent = values.shape
    blocks = values.reshape(extent[:axis_dim] + (extent[axis_dim] // 5, 5) + extent[axis_dim + 1 :])
    letters = "abcdefg"[: blocks.ndim]
    summed_letter = letters[axis_dim + 1]
    formula = letters + ",z" + summed_letter + "->" + letters.replace(summed_letter, "z")
    result = jnp.einsum(formula, blocks, matrix, precision=lax.Precision.HIGHEST)
    return result.reshape(extent)


def line_term(interior, extended, flux_of, speed_of, solved, axis_dim, derivative):
    volume = along_axis(flux_of(interior), derivative, axis_dim)
    length = extended.shape[axis_dim]
    elements = (length - 2) // 5
    left_state = lax.slice_in_dim(extended, 0, length - 1, 5, axis_dim)
    right_state = lax.slice_in_dim(extended, 1, length, 5, axis_dim)
    flux_left = flux_of(left_state)
    flux_right = flux_of(right_state)
    wave_speed = jnp.maximum(speed_of(left_state), speed_of(right_state))
    state_jump = lax.slice_in_dim(right_state - left_state, 0, solved, 1, 0)
    common = 0.5 * (flux_left + flux_right) - 0.5 * wave_speed[None] * state_jump
    first_lift = (
        lax.slice_in_dim(common, 0, elements, 1, axis_dim)
        - lax.slice_in_dim(flux_right, 0, elements, 1, axis_dim)
    ) / EDGE_WEIGHT
    last_lift = (
        lax.slice_in_dim(flux_left, 1, elements + 1, 1, axis_dim)
        - lax.slice_in_dim(common, 1, elements + 1, 1, axis_dim)
    ) / EDGE_WEIGHT
    zero_lift = jnp.zeros_like(first_lift)
    surface = jnp.stack(
        [first_lift, zero_lift, zero_lift, zero_lift, last_lift], axis=axis_dim + 1
    ).reshape(volume.shape)
    return surface - volume


def euler_parts(state, direction):
    density = state[0]
    velocity = state[1 + direction] / density
    kinetic = 0.5 * (state[1] * state[1] + state[2] * state[2] + state[3] * state[3]) / density
    pressure = (HEAT_RATIO - 1.0) * (state[4] - kinetic)
    return (density, velocity, pressure)


def euler_flux(state, direction):
    density, velocity, pressure = euler_parts(state, direction)
    pieces = [state[1 + direction]]
    for k in range(3):
        if k == direction:
            pieces.append(state[1 + k] * velocity + pressure)
        else:
            pieces.append(state[1 + k] * velocity)
    pieces.append((state[4] + pressure) * velocity)
    return jnp.stack(pieces)


def euler_speed(state, direction):
    density, velocity, pressure = euler_parts(state, direction)
    return jnp.abs(velocity) + jnp.sqrt(HEAT_RATIO * pressure / density)


def ape_flux(state, direction):
    pressure = state[0]
    carried = state[6] * state[1] + state[7] * state[2] + state[8] * state[3] + pressure / state[4]
    leading = (
        state[5] * state[5] * state[4] * state[1 + direction] + state[6 + direction] * pressure
    )
    pieces = [leading]
    for k in range(3):
        if k == direction:
            pieces.append(carried)
        else:
            pieces.append(jnp.zeros_like(carried))
    return jnp.stack(pieces)


def ape_speed(state, direction):
    return jnp.abs(state[6 + direction]) + state[5]


def lamb_vector(state, derivative):
    density = state[0]
    velocity = [state[1 + k] / density for k in range(3)]
    omega_first = along_axis(velocity[2], derivative, 1) - along_axis(velocity[1], derivative, 2)
    omega_second = along_axis(velocity[0], derivative, 2) - along_axis(velocity[2], derivative, 0)
    omega_third = along_axis(velocity[1], derivative, 0) - along_axis(velocity[0], derivative, 1)
    return jnp.stack(
        [
            omega_second * velocity[2] - omega_third * velocity[1],
            omega_third * velocity[0] - omega_first * velocity[2],
            omega_first * velocity[1] - omega_second * velocity[0],
        ]
    )


def repeat_edges(padded, axis_dim, position, axis_count):
    extent = padded.shape[axis_dim]
    low_outer = jnp.where(
        position == 0,
        lax.slice_in_dim(padded, 1, 2, 1, axis_dim),
        lax.slice_in_dim(padded, 0, 1, 1, axis_dim),
    )
    high_outer = jnp.where(
        position == axis_count - 1,
        lax.slice_in_dim(padded, extent - 2, extent - 1, 1, axis_dim),
        lax.slice_in_dim(padded, extent - 1, extent, 1, axis_dim),
    )
    middle = lax.slice_in_dim(padded, 1, extent - 1, 1, axis_dim)
    return jnp.concatenate([low_outer, middle, high_outer], axis=axis_dim)


def keep_rim(padded, axis_dim):
    for other_dim in (1, 2, 3):
        if other_dim != axis_dim:
            padded = lax.slice_in_dim(padded, 1, padded.shape[other_dim] - 1, 1, other_dim)
    return padded


def all_lines(interior, padded, flux_fn, speed_fn, solved, derivative):
    total = None
    for direction in range(3):
        term = line_term(
            interior,
            keep_rim(padded, direction + 1),
            partial(flux_fn, direction=direction),
            partial(speed_fn, direction=direction),
            solved,
            direction + 1,
            derivative,
        )
        total = term if total is None else total + term
    return total


def intersection_owner(counts, intersections):
    running_ends = jnp.cumsum(counts)
    positions = jnp.arange(intersections, dtype=jnp.int32)
    return jnp.sum((positions[:, None] >= running_ends[None, :]).astype(jnp.int32), axis=1)


def project_block(rows_source, index, keep, owner, pattern, projection):
    patterns = projection.shape[0]
    gathered = jnp.take(rows_source, index, axis=0)
    segment = jnp.where(keep, owner * patterns + pattern, AEL * patterns)
    summed = jax.ops.segment_sum(gathered, segment, num_segments=AEL * patterns + 1)[
        : AEL * patterns
    ]
    summed = summed.reshape(AEL, patterns, 3, 125)
    return jnp.einsum("apcn,pmn->acm", summed, projection, precision=lax.Precision.HIGHEST)


def body(
    les_state,
    acoustic_state,
    mean_density,
    mean_sound,
    mean_velocity,
    projection,
    intersection_counts,
    intersection_elem,
    intersection_pattern,
):
    derivative = gll_derivative()
    les_padded = with_halo(les_state, (("azim", 1), ("rad", 2), ("group", 3)), 1)
    les_padded = repeat_edges(les_padded, 2, lax.axis_index("rad"), lax.axis_size("rad"))
    les_padded = repeat_edges(les_padded, 3, lax.axis_index("group"), lax.axis_size("group"))
    combined = jnp.concatenate(
        [acoustic_state, mean_density[None], mean_sound[None], mean_velocity], axis=0
    )
    ape_padded = with_halo(combined, (("azim", 1), ("rad", 2), ("group", 3)), 1)
    ape_padded = repeat_edges(ape_padded, 2, lax.axis_index("rad"), lax.axis_size("rad"))
    ape_padded = repeat_edges(ape_padded, 3, lax.axis_index("group"), lax.axis_size("group"))
    lamb = lamb_vector(les_state, derivative)
    rows = lamb.reshape(3, EA, 5, ER, 5, EX, 5).transpose(1, 3, 5, 0, 2, 4, 6).reshape(EL, 375)
    counts = intersection_counts.reshape(-1)
    elems = intersection_elem.reshape(-1)
    patterns_used = intersection_pattern.reshape(-1)
    intersections = elems.shape[0]
    column_rows = shifted(rows[:COL], "azim", -1)
    window = jnp.concatenate([rows, column_rows], axis=0)
    owner = intersection_owner(counts, intersections)
    projected = project_block(window, elems, elems >= 0, owner, patterns_used, projection)
    sources = (
        projected.reshape(AA, AR, EX, 3, 5, 5, 5)
        .transpose(3, 0, 4, 1, 5, 2, 6)
        .reshape(3, 5 * AA, 5 * AR, 5 * EX)
    )
    les_total = all_lines(les_state, les_padded, euler_flux, euler_speed, 5, derivative)
    les_next = les_state + TIME_STEP * les_total
    ape_total = all_lines(combined, ape_padded, ape_flux, ape_speed, 4, derivative)
    forcing = jnp.concatenate([jnp.zeros_like(sources[:1]), sources], axis=0)
    acoustic_next = acoustic_state + TIME_STEP * (ape_total - forcing)
    return (les_next, acoustic_next)


def solution(mesh):
    return jax.shard_map(
        body,
        mesh=mesh,
        in_specs=(
            P(None, "azim", "rad", "group"),
            P(None, "azim", "rad", "group"),
            P("azim", "rad", "group"),
            P("azim", "rad", "group"),
            P(None, "azim", "rad", "group"),
            P(),
            P("azim", "rad", "group", None),
            P("azim", "rad", "group", None),
            P("azim", "rad", "group", None),
        ),
        out_specs=(P(None, "azim", "rad", "group"), P(None, "azim", "rad", "group")),
        check_vma=False,
    )
```

profile of v0, /device:TPU:1, one launch (start us, length us, event | category | flops | bytes accessed | tf_op | source)
XLA Modules:
  0.0 423.6 jit_solution(9476994710057352252)
XLA Ops:
  7.1 2.0 collective-permute-start.6
  9.2 6.6 %collective-permute-start.7 = (f32[9,1,5,640]{3,1,0,2:T(1,128)}, f32[9,1,5,640]{3,1,0,2:T(1,128)}, u32[]{:S(2)}, u32[]{:S(2)}) collective-permute-start(f32[9,1,5,640]{3,1,0,2:T(1,128)} %get-tuple-element.74), channel_id=1, source_target_pairs={{8,0},{16,8},{24,16},{32,24},{40,32},{48,40},{56,48},{64,56},{72,6... | collective-permute-start | bytes 345608 | tf_op jit(solution)/shard_map/ppermute | solution.py:34
  21.7 8.4 %div.291 = f32[10,10,128,5]{3,2,1,0:T(8,128)} reshape(f32[1,10,10,640]{3,2,1,0:T(8,128)S(1)} %get-tuple-element.23) | data formatting | bytes 512000 | tf_op jit(solution)/shard_map/div | solution.py:97
  30.1 8.2 %div.296 = f32[10,10,128,5]{3,2,1,0:T(8,128)} reshape(f32[1,10,10,640]{3,2,1,0:T(8,128)S(1)} %get-tuple-element.15) | data formatting | bytes 512000 | tf_op jit(solution)/shard_map/div | solution.py:97
  44.0 7.2 %fusion.117 = f32[10,10,128,5]{3,2,1,0:T(8,128)} fusion(f32[10,10,128,5]{3,2,1,0:T(8,128)S(1)} %copy-done.2, f32[5,5,1,1]{1,0,3,2:T(8,128)S(1)} %copy-done.40), kind=kOutput, calls=%fused_computation.309 | convolution fusion | flops 3840000 | bytes 512100 | tf_op jit(solution)/shard_map/abcd,zd->abcz/dot_general | solution.py:65
  51.2 5.7 %reshape.292 = f32[1,10,10,640]{3,2,1,0:T(8,128)} reshape(f32[10,10,128,5]{3,2,1,0:T(8,128)} %fusion.117) | data formatting | bytes 512000 | tf_op jit(solution)/shard_map/reshape | solution.py:66
  56.9 9.5 %fusion.118 = f32[10,10,128,5]{3,2,1,0:T(8,128)} fusion(f32[10,10,128,5]{3,2,1,0:T(8,128)} %div.296, f32[5,5,1,1]{1,0,3,2:T(8,128)S(1)} %copy-done.40), kind=kOutput, calls=%fused_computation.310 | convolution fusion | flops 3840000 | bytes 512100 | tf_op jit(solution)/shard_map/abcd,zd->abcz/dot_general | solution.py:65
  66.4 5.7 %reshape.297 = f32[1,10,10,640]{3,2,1,0:T(8,128)} reshape(f32[10,10,128,5]{3,2,1,0:T(8,128)} %fusion.118) | data formatting | bytes 512000 | tf_op jit(solution)/shard_map/reshape | solution.py:66
  72.1 2.9 multiply_subtract_fusion.5
  75.0 8.4 %stack.297 = f32[1,2,5,2,5,128,5]{6,5,0,4,3,2,1:T(8,128)} reshape(f32[1,10,10,640]{3,2,1,0:T(8,128)} %get-tuple-element.68) | data formatting | bytes 512000 | tf_op jit(solution)/shard_map/stack | solution.py:145
  83.4 5.3 %copy.389 = f32[1,2,5,2,5,128,5]{5,3,6,4,2,1,0:T(2,128)} copy(f32[1,2,5,2,5,128,5]{6,5,0,4,3,2,1:T(8,128)} %stack.297) | data formatting | bytes 512000 | tf_op jit(solution)/shard_map/stack | solution.py:145
  88.7 8.4 %stack.298 = f32[1,2,5,2,5,128,5]{6,5,0,4,3,2,1:T(8,128)} reshape(f32[1,10,10,640]{3,2,1,0:T(8,128)} %get-tuple-element.69) | data formatting | bytes 512000 | tf_op jit(solution)/shard_map/stack | solution.py:145
  97.0 5.3 %copy.390 = f32[1,2,5,2,5,128,5]{5,3,6,4,2,1,0:T(2,128)} copy(f32[1,2,5,2,5,128,5]{6,5,0,4,3,2,1:T(8,128)} %stack.298) | data formatting | bytes 512000 | tf_op jit(solution)/shard_map/stack | solution.py:145
  102.3 8.4 %stack.299 = f32[1,2,5,2,5,128,5]{6,5,0,4,3,2,1:T(8,128)} reshape(f32[1,10,10,640]{3,2,1,0:T(8,128)} %get-tuple-element.70) | data formatting | bytes 512000 | tf_op jit(solution)/shard_map/stack | solution.py:145
  110.6 5.3 %copy.391 = f32[1,2,5,2,5,128,5]{5,3,6,4,2,1,0:T(2,128)} copy(f32[1,2,5,2,5,128,5]{6,5,0,4,3,2,1:T(8,128)} %stack.299) | data formatting | bytes 512000 | tf_op jit(solution)/shard_map/stack | solution.py:145
  119.3 1.9 copy.393
  121.2 4.8 %collective-permute-start.12 = (f32[256,375]{1,0:T(8,128)}, f32[256,375]{1,0:T(8,128)}, u32[]{:S(2)}, u32[]{:S(2)}) collective-permute-start(f32[256,375]{1,0:T(8,128)} %copy.393), channel_id=1, source_target_pairs={{0,248},{8,0},{16,8},{24,16},{32,24},{40,32},{48,40},{56,48},{64,5... | collective-permute-start | bytes 1152008 | tf_op jit(solution)/shard_map/ppermute | solution.py:42
  126.0 3.3 slice_multiply_fusion.12
  134.5 5.1 %copy.337 = f32[1,10,10,640]{2,0,3,1:T(1,128)S(1)} copy(f32[1,10,10,640]{3,2,1,0:T(8,128)} %get-tuple-element.49) | data formatting | bytes 512000 | tf_op jit(solution)/shard_map/mul | solution.py:111
  139.6 4.3 %copy.342 = f32[1,10,10,128,5]{3,4,2,1,0:T(8,128)} copy(f32[1,10,10,128,5]{2,0,4,3,1:T(1,128)S(1)} %bitcast.275) | data formatting | bytes 512000 | tf_op jit(solution)/shard_map/stack | solution.py:112
  144.0 1.9 stack.304
  145.9 2.0 stack.241
  147.9 1.9 stack.243
  154.3 5.0 %copy.336 = f32[1,10,10,640]{2,0,3,1:T(1,128)S(1)} copy(f32[1,10,10,640]{3,2,1,0:T(8,128)} %get-tuple-element.42) | data formatting | bytes 512000 | tf_op jit(solution)/shard_map/add | solution.py:108
  159.3 4.4 %copy.341 = f32[1,10,10,128,5]{3,4,2,1,0:T(8,128)} copy(f32[1,10,10,128,5]{2,0,4,3,1:T(1,128)S(1)} %bitcast.276) | data formatting | bytes 512000 | tf_op jit(solution)/shard_map/stack | solution.py:112
  163.6 5.0 %copy.335 = f32[1,10,10,640]{2,0,3,1:T(1,128)S(1)} copy(f32[1,10,10,640]{3,2,1,0:T(8,128)} %get-tuple-element.43) | data formatting | bytes 512000 | tf_op jit(solution)/shard_map/mul | solution.py:110
  168.6 4.4 %copy.340 = f32[1,10,10,128,5]{3,4,2,1,0:T(8,128)} copy(f32[1,10,10,128,5]{2,0,4,3,1:T(1,128)S(1)} %bitcast.277) | data formatting | bytes 512000 | tf_op jit(solution)/shard_map/stack | solution.py:112
  173.0 5.0 %copy.334 = f32[1,10,10,640]{2,0,3,1:T(1,128)S(1)} copy(f32[1,10,10,640]{3,2,1,0:T(8,128)} %get-tuple-element.47) | data formatting | bytes 512000 | tf_op jit(solution)/shard_map/mul | solution.py:110
  177.9 4.4 %copy.339 = f32[1,10,10,128,5]{3,4,2,1,0:T(8,128)} copy(f32[1,10,10,128,5]{2,0,4,3,1:T(1,128)S(1)} %bitcast.278) | data formatting | bytes 512000 | tf_op jit(solution)/shard_map/stack | solution.py:112
  182.3 5.0 %copy.333 = f32[1,10,10,640]{2,0,3,1:T(1,128)S(1)} copy(f32[1,10,10,640]{3,2,1,0:T(8,128)} %get-tuple-element.57) | data formatting | bytes 512000 | tf_op jit(solution)/shard_map/slice | solution.py:98
  187.3 4.4 %copy.338 = f32[1,10,10,128,5]{3,4,2,1,0:T(8,128)} copy(f32[1,10,10,128,5]{2,0,4,3,1:T(1,128)S(1)} %bitcast.279) | data formatting | bytes 512000 | tf_op jit(solution)/shard_map/stack | solution.py:112
  191.7 1.9 constant_dynamic-update-slice_fusion.14
  205.9 2.4 reshape.323
  209.7 2.4 reshape.322
  221.3 5.0 %collective-permute-start.8 = (f32[9,7,1,640]{3,1,0,2:T(8,128)S(1)}, f32[9,7,1,640]{3,1,0,2:T(8,128)S(1)}, u32[]{:S(2)}, u32[]{:S(2)}) collective-permute-start(f32[9,7,1,640]{3,1,0,2:T(8,128)S(1)} %get-tuple-element.71), channel_id=1, source_target_pairs={{0,2},{2,4},{4,6},{6,0},{1,3},{3,5},{5,7},{7,1},{8,10},{10,12},{12... | collective-permute-start | bytes 483848 | tf_op jit(solution)/shard_map/ppermute | solution.py:31
  231.0 3.3 collective-permute-start.2
  239.0 2.4 maximum_subtract_fusion
  243.0 1.9 collective-permute-done.10
  244.8 5.5 %collective-permute-done.11 = f32[9,7,7,1]{3,1,0,2:T(8,128)S(1)} collective-permute-done((f32[9,7,7,1]{3,1,0,2:T(8,128)S(1)}, f32[9,7,7,1]{3,1,0,2:T(8,128)S(1)}, u32[]{:S(2)}, u32[]{:S(2)}) %collective-permute-start.11) | collective-permute-done | bytes 1796 | tf_op jit(solution)/shard_map/ppermute | solution.py:34
  250.4 2.1 pad_maximum_fusion.4
  256.4 4.6 %slice.911 = f32[9,5,5,129]{3,1,0,2:T(8,128)S(1)} slice(f32[9,5,5,642]{3,1,0,2:T(8,128)} %pad_maximum_fusion.8), slice={[0:9:1], [0:5:1], [0:5:1], [1:642:5]} | slice | bytes 232200 | tf_op jit(solution)/shard_map/slice | solution.py:74
  261.0 4.5 %slice.901 = f32[9,5,5,129]{3,1,0,2:T(8,128)S(1)} slice(f32[9,5,5,642]{3,1,0,2:T(8,128)} %pad_maximum_fusion.8), slice={[0:9:1], [0:5:1], [0:5:1], [0:641:5]} | slice | bytes 232200 | tf_op jit(solution)/shard_map/slice | solution.py:73
  269.1 2.1 pad_maximum_fusion.13
  273.7 5.0 %copy.417 = f32[4,5,5,128,5]{4,3,1,2,0:T(8,128)} copy(f32[4,5,5,128,5]{3,4,2,1,0:T(8,128)} %convolution_subtract_fusion) | data formatting | bytes 512000 | tf_op jit(solution)/shard_map/sub | solution.py:92
  278.8 6.1 %reshape.324 = f32[4,5,5,640]{3,1,2,0:T(8,128)} reshape(f32[4,5,5,128,5]{4,3,1,2,0:T(8,128)} %copy.417) | data formatting | bytes 512000 | tf_op jit(solution)/shard_map/sub | solution.py:92
  284.9 8.5 %collective-permute-done.5 = f32[5,12,12,1]{3,2,1,0:T(8,128)S(1)} collective-permute-done((f32[5,12,12,1]{3,2,1,0:T(8,128)}, f32[5,12,12,1]{3,2,1,0:T(8,128)S(1)}, u32[]{:S(2)}, u32[]{:S(2)}) %collective-permute-start.5) | collective-permute-done | bytes 2912 | tf_op jit(solution)/shard_map/ppermute | solution.py:34
  293.4 3.1 pad_maximum_fusion
  296.9 2.9 broadcast_select_fusion.1
  299.8 3.1 broadcast_select_fusion
  307.4 5.0 %slice.794 = f32[5,10,3,640]{3,2,1,0:T(4,128)S(1)} slice(f32[5,10,12,640]{3,2,1,0:T(8,128)} %slice.948), slice={[0:5:1], [0:10:1], [1:12:5], [0:640:1]} | slice | bytes 768000 | tf_op jit(solution)/shard_map/slice | solution.py:74
  312.4 5.2 %slice.788 = f32[5,10,3,640]{3,2,1,0:T(4,128)S(1)} slice(f32[5,10,12,640]{3,2,1,0:T(8,128)} %slice.948), slice={[0:5:1], [0:10:1], [0:11:5], [0:640:1]} | slice | bytes 768000 | tf_op jit(solution)/shard_map/slice | solution.py:73
  317.6 3.5 pad_maximum_fusion.2
  321.1 8.5 %slice.810 = f32[5,10,10,129]{3,2,1,0:T(8,128)S(1)} slice(f32[5,10,10,642]{3,2,1,0:T(8,128)} %pad_maximum_fusion.2), slice={[0:5:1], [0:10:1], [0:10:1], [0:641:5]} | slice | bytes 516000 | tf_op jit(solution)/shard_map/slice | solution.py:73
  329.6 8.6 %slice.816 = f32[5,10,10,129]{3,2,1,0:T(8,128)S(1)} slice(f32[5,10,10,642]{3,2,1,0:T(8,128)} %pad_maximum_fusion.2), slice={[0:5:1], [0:10:1], [0:10:1], [1:642:5]} | slice | bytes 516000 | tf_op jit(solution)/shard_map/slice | solution.py:74
  342.6 2.4 maximum_subtract_fusion.1
  346.8 4.0 maximum_subtract_fusion.2
  350.8 17.4 %copy.343 = f32[5,10,10,128,5]{4,3,2,1,0:T(8,128)} copy(f32[5,10,10,128,5]{3,4,2,1,0:T(8,128)S(1)} %maximum_subtract_fusion.2) | data formatting | bytes 2560000 | tf_op jit(solution)/shard_map/sub | solution.py:92
  368.1 21.8 %sub.233 = f32[5,10,10,640]{3,2,1,0:T(8,128)} reshape(f32[5,10,10,128,5]{4,3,2,1,0:T(8,128)} %copy.343) | data formatting | bytes 2560000 | tf_op jit(solution)/shard_map/sub | solution.py:92
  389.9 4.9 %fusion.2 = f32[5,10,10,640]{3,2,1,0:T(8,128)} fusion(f32[5,10,10,640]{3,2,1,0:T(8,128)S(1)} %copy-done.1, f32[5,10,10,640]{3,2,1,0:T(8,128)} %sub.233, f32[5,10,10,640]{3,2,1,0:T(8,128)} %bitcast.282, f32[5,10,10,640]{3,1,2,0:T(8,128)} %bitcast.283), kind=kLoop, calls=%fused_computation.12 | loop fusion | flops 1280000 | bytes 6400000 | tf_op jit(solution)/shard_map/add | solution.py:247
  395.9 11.3 %scatter_custom_fusion = f32[1025,375]{1,0:T(8,128)S(1)} fusion(s32[768]{0:T(1024)} %get-tuple-element.13, f32[]{:T(128)} %constant.34.clone.1, f32[]{:T(128)} %constant.45.clone.1, pred[768]{0:T(1024)(128)(4,1)S(1)} %copy-done.48, f32[768,375]{1,0:T(8,128)S(1)} %pad_maximum_fusion.7, s32[1024]{0:T(1024)S(1)} %pad_clamp_fusion), kind=kCustom, calls=%fused_computation.34 | custom fusion | flops 576000 | bytes 2695388 | tf_op jit(solution)/shard_map/scatter-add | solution.py:203
  407.4 2.3 reshape.299
  409.6 4.4 %fusion.13 = f32[3,1,5,1,5,128,5]{5,6,4,2,0,3,1:T(8,128)S(1)} fusion(f32[128,8,3,125]{3,2,1,0:T(4,128)} %reshape.299, f32[5,5,5,125,8]{3,4,2,1,0:T(8,128)S(1)} %bitcast.296), kind=kOutput, calls=%fused_computation.32 | convolution fusion | flops 576000000 | bytes 2228000 | tf_op jit(solution)/shard_map/apcn,pmn->acm/dot_general | solution.py:207
  414.0 3.2 copy.418
  417.2 4.4 %reshape.325 = f32[3,5,5,640]{3,1,2,0:T(8,128)S(1)} reshape(f32[3,1,5,1,5,128,5]{6,5,2,4,0,3,1:T(8,128)} %copy.418) | data formatting | bytes 384000 | tf_op jit(solution)/shard_map/reshape | solution.py:244
  (278 shorter events, 88.0 us)
Async XLA Ops:
  0.6 4.8 %copy-start.43 = (f32[5,5,640]{2,1,0:T(8,128)S(1)}, f32[5,5,640]{2,1,0:T(8,128)}, u32[]{:S(2)}) copy-start(f32[5,5,640]{2,1,0:T(8,128)} %param.13) | copy-start | bytes 192004
  0.6 4.8 %copy-start.42 = (f32[5,5,640]{2,1,0:T(8,128)S(1)}, f32[5,5,640]{2,1,0:T(8,128)}, u32[]{:S(2)}) copy-start(f32[5,5,640]{2,1,0:T(8,128)} %param.12) | copy-start | bytes 192004
  3.1 13.5 %copy-start.5 = (f32[3,5,5,640]{3,1,0,2:T(8,128)}, f32[3,5,5,640]{3,1,0,2:T(8,128)S(1)}, u32[]{:S(2)}) copy-start(f32[3,5,5,640]{3,1,0,2:T(8,128)S(1)} %copy.347) | copy-start | bytes 576004
  3.1 12.7 %copy-start = (f32[5,10,10,640]{3,2,1,0:T(8,128)S(1)}, f32[5,10,10,640]{3,2,1,0:T(8,128)}, u32[]{:S(2)}) copy-start(f32[5,10,10,640]{3,2,1,0:T(8,128)} %param.10) | copy-start | bytes 3840004
  4.2 14.9 %copy-start.3 = (f32[4,5,5,640]{3,1,0,2:T(8,128)}, f32[4,5,5,640]{3,1,0,2:T(8,128)S(1)}, u32[]{:S(2)}) copy-start(f32[4,5,5,640]{3,1,0,2:T(8,128)S(1)} %copy.346) | copy-start | bytes 768004
  7.1 209.1 %collective-permute-start.6 = (f32[9,1,5,640]{3,1,0,2:T(1,128)}, f32[9,1,5,640]{3,1,0,2:T(1,128)}, u32[]{:S(2)}, u32[]{:S(2)}) collective-permute-start(f32[9,1,5,640]{3,1,0,2:T(1,128)} %get-tuple-element.73), channel_id=1, source_target_pairs={{0,8},{8,16},{16,24},{24,32},{32,40},{40,48},{48,56},{56,64},{64,7... | collective-permute-start | bytes 345608 | tf_op jit(solution)/shard_map/ppermute | solution.py:31
  9.2 207.1 %collective-permute-start.7 = (f32[9,1,5,640]{3,1,0,2:T(1,128)}, f32[9,1,5,640]{3,1,0,2:T(1,128)}, u32[]{:S(2)}, u32[]{:S(2)}) collective-permute-start(f32[9,1,5,640]{3,1,0,2:T(1,128)} %get-tuple-element.74), channel_id=1, source_target_pairs={{8,0},{16,8},{24,16},{32,24},{40,32},{48,40},{56,48},{64,56},{72,6... | collective-permute-start | bytes 345608 | tf_op jit(solution)/shard_map/ppermute | solution.py:34
  16.6 212.4 %collective-permute-start.1 = (f32[5,1,10,640]{3,2,1,0:T(8,128)}, f32[5,1,10,640]{3,2,1,0:T(8,128)}, u32[]{:S(2)}, u32[]{:S(2)}) collective-permute-start(f32[5,1,10,640]{3,2,1,0:T(8,128)} %get-tuple-element.58), channel_id=1, source_target_pairs={{8,0},{16,8},{24,16},{32,24},{40,32},{48,40},{56,48},{64,56},{72,6... | collective-permute-start | bytes 384008 | tf_op jit(solution)/shard_map/ppermute | solution.py:34
  18.0 208.3 %collective-permute-start = (f32[5,1,10,640]{3,2,1,0:T(8,128)}, f32[5,1,10,640]{3,2,1,0:T(8,128)}, u32[]{:S(2)}, u32[]{:S(2)}) collective-permute-start(f32[5,1,10,640]{3,2,1,0:T(8,128)} %get-tuple-element.59), channel_id=1, source_target_pairs={{0,8},{8,16},{16,24},{24,32},{32,40},{40,48},{48,56},{56,64},{64,7... | collective-permute-start | bytes 384008 | tf_op jit(solution)/shard_map/ppermute | solution.py:31
  30.1 8.3 %copy-start.40 = (f32[5,5,1,1]{1,0,3,2:T(8,128)S(1)}, f32[5,5,1,1]{1,0,3,2:T(8,128)}, u32[]{:S(2)}) copy-start(f32[5,5,1,1]{1,0,3,2:T(8,128)} %constant.58) | copy-start | bytes 304
  38.4 2.9 copy-start.25
  38.9 5.1 %copy-start.2 = (f32[10,10,128,5]{3,2,1,0:T(8,128)S(1)}, f32[10,10,128,5]{3,2,1,0:T(8,128)}, u32[]{:S(2)}) copy-start(f32[10,10,128,5]{3,2,1,0:T(8,128)} %div.291) | copy-start | bytes 768004
  121.2 8.0 %copy-start.47 = (s32[1,1,1,768]{3,2,1,0:T(1,128)S(1)}, s32[1,1,1,768]{3,2,1,0:T(1,128)}, u32[]{:S(2)}) copy-start(s32[1,1,1,768]{3,2,1,0:T(1,128)} %param.17) | copy-start | bytes 9220
  121.2 8.7 %copy-start.53 = (s32[1,1,1,128]{3,2,1,0:T(1,128)S(1)}, s32[1,1,1,128]{3,2,1,0:T(1,128)}, u32[]{:S(2)}) copy-start(s32[1,1,1,128]{3,2,1,0:T(1,128)} %param.16) | copy-start | bytes 1540
  121.2 273.6 %collective-permute-start.12 = (f32[256,375]{1,0:T(8,128)}, f32[256,375]{1,0:T(8,128)}, u32[]{:S(2)}, u32[]{:S(2)}) collective-permute-start(f32[256,375]{1,0:T(8,128)} %copy.393), channel_id=1, source_target_pairs={{0,248},{8,0},{16,8},{24,16},{32,24},{40,32},{48,40},{56,48},{64,5... | collective-permute-start | bytes 1152008 | tf_op jit(solution)/shard_map/ppermute | solution.py:42
  129.2 3.5 copy-start.18
  129.3 4.3 %copy-start.23 = (f32[1,10,10,640]{3,2,1,0:T(8,128)S(1)}, f32[1,10,10,640]{3,2,1,0:T(8,128)}, u32[]{:S(2)}) copy-start(f32[1,10,10,640]{3,2,1,0:T(8,128)} %get-tuple-element.22) | copy-start | bytes 768004
  144.0 5.9 %copy-start.32 = (f32[1,10,10,640]{3,2,1,0:T(8,128)S(1)}, f32[1,10,10,640]{3,2,1,0:T(8,128)}, u32[]{:S(2)}) copy-start(f32[1,10,10,640]{3,2,1,0:T(8,128)} %get-tuple-element.46) | copy-start | bytes 768004
  144.0 6.9 %copy-start.31 = (f32[1,10,10,640]{3,2,1,0:T(8,128)S(1)}, f32[1,10,10,640]{3,2,1,0:T(8,128)}, u32[]{:S(2)}) copy-start(f32[1,10,10,640]{3,2,1,0:T(8,128)} %get-tuple-element.56) | copy-start | bytes 768004
  144.0 7.1 %copy-start.30 = (f32[1,10,10,640]{3,2,1,0:T(8,128)S(1)}, f32[1,10,10,640]{3,2,1,0:T(8,128)}, u32[]{:S(2)}) copy-start(f32[1,10,10,640]{3,2,1,0:T(8,128)} %get-tuple-element.41) | copy-start | bytes 768004
  144.0 7.9 %copy-start.29 = (f32[1,10,10,640]{3,2,1,0:T(8,128)S(1)}, f32[1,10,10,640]{3,2,1,0:T(8,128)}, u32[]{:S(2)}) copy-start(f32[1,10,10,640]{3,2,1,0:T(8,128)} %get-tuple-element.48) | copy-start | bytes 768004
  145.9 6.8 %copy-start.28 = (f32[1,10,10,640]{3,2,1,0:T(8,128)S(1)}, f32[1,10,10,640]{3,2,1,0:T(8,128)}, u32[]{:S(2)}) copy-start(f32[1,10,10,640]{3,2,1,0:T(8,128)} %get-tuple-element.55) | copy-start | bytes 768004
  187.3 6.3 %copy-start.49 = (s32[1,1,1,768]{3,2,1,0:T(1,128)S(1)}, s32[1,1,1,768]{3,2,1,0:T(1,128)}, u32[]{:S(2)}) copy-start(s32[1,1,1,768]{3,2,1,0:T(1,128)} %param.18) | copy-start | bytes 9220
  191.7 8.2 %copy-start.24 = (f32[1,10,2,5,640]{4,3,2,1,0:T(8,128)S(1)}, f32[1,10,2,5,640]{4,3,2,1,0:T(8,128)}, u32[]{:S(2)}) copy-start(f32[1,10,2,5,640]{4,3,2,1,0:T(8,128)} %stack.305) | copy-start | bytes 768004
  191.7 8.9 %copy-start.13 = (f32[5,2,5,10,640]{4,2,3,1,0:T(8,128)S(1)}, f32[5,2,5,10,640]{4,2,3,1,0:T(8,128)}, u32[]{:S(2)}) copy-start(f32[5,2,5,10,640]{4,2,3,1,0:T(8,128)} %copy_dynamic-update-slice_fusion.4) | copy-start | bytes 3840004
  191.7 8.9 %copy-start.35 = (f32[1,2,5,10,640]{4,0,3,2,1:T(1,128)S(1)}, f32[1,2,5,10,640]{4,0,3,2,1:T(1,128)}, u32[]{:S(2)}) copy-start(f32[1,2,5,10,640]{4,0,3,2,1:T(1,128)} %stack.241) | copy-start | bytes 768004
  193.6 7.1 %copy-start.36 = (f32[1,2,5,10,640]{4,0,3,2,1:T(1,128)S(1)}, f32[1,2,5,10,640]{4,0,3,2,1:T(1,128)}, u32[]{:S(2)}) copy-start(f32[1,2,5,10,640]{4,0,3,2,1:T(1,128)} %stack.242) | copy-start | bytes 768004
  196.1 4.7 %copy-start.34 = (f32[1,2,5,10,640]{4,0,3,2,1:T(1,128)S(1)}, f32[1,2,5,10,640]{4,0,3,2,1:T(1,128)}, u32[]{:S(2)}) copy-start(f32[1,2,5,10,640]{4,0,3,2,1:T(1,128)} %stack.243) | copy-start | bytes 768004
  196.1 4.7 %copy-start.33 = (f32[1,2,5,10,640]{4,0,3,2,1:T(1,128)S(1)}, f32[1,2,5,10,640]{4,0,3,2,1:T(1,128)}, u32[]{:S(2)}) copy-start(f32[1,2,5,10,640]{4,0,3,2,1:T(1,128)} %stack.244) | copy-start | bytes 768004
  198.0 4.2 copy-start.22
  199.8 3.1 copy-start.21
  200.6 3.1 copy-start.20
  200.7 3.8 copy-start.19
  200.9 1.3 copy-start.14
  202.9 5.5 %copy-start.8 = (f32[2,2,128,3,5,5,5]{2,1,6,5,4,0,3:T(2,128)S(1)}, f32[2,2,128,3,5,5,5]{2,1,6,5,4,0,3:T(2,128)}, u32[]{:S(2)}) copy-start(f32[2,2,128,3,5,5,5]{2,1,6,5,4,0,3:T(2,128)} %copy-done.7) | copy-start | bytes 2304004
  205.9 14.2 %copy-start.50 = (f32[4]{0:T(128)}, f32[4]{0:T(128)S(1)}, u32[]{:S(2)}) copy-start(f32[4]{0:T(128)S(1)} %get-tuple-element.126) | copy-start | bytes 52
  213.3 1.1 copy-start.12
  213.3 3.0 copy-start.4
  213.3 3.0 copy-start.6
  221.3 14.5 %collective-permute-start.8 = (f32[9,7,1,640]{3,1,0,2:T(8,128)S(1)}, f32[9,7,1,640]{3,1,0,2:T(8,128)S(1)}, u32[]{:S(2)}, u32[]{:S(2)}) collective-permute-start(f32[9,7,1,640]{3,1,0,2:T(8,128)S(1)} %get-tuple-element.71), channel_id=1, source_target_pairs={{0,2},{2,4},{4,6},{6,0},{1,3},{3,5},{5,7},{7,1},{8,10},{10,12},{12... | collective-permute-start | bytes 483848 | tf_op jit(solution)/shard_map/ppermute | solution.py:31
  226.3 9.6 %collective-permute-start.9 = (f32[9,7,1,640]{3,1,0,2:T(8,128)S(1)}, f32[9,7,1,640]{3,1,0,2:T(8,128)S(1)}, u32[]{:S(2)}, u32[]{:S(2)}) collective-permute-start(f32[9,7,1,640]{3,1,0,2:T(8,128)S(1)} %get-tuple-element.72), channel_id=1, source_target_pairs={{2,0},{4,2},{6,4},{0,6},{3,1},{5,3},{7,5},{1,7},{10,8},{12,10},{14... | collective-permute-start | bytes 483848 | tf_op jit(solution)/shard_map/ppermute | solution.py:34
  231.0 38.2 %collective-permute-start.2 = (f32[5,12,1,640]{3,2,1,0:T(1,128)}, f32[5,12,1,640]{3,2,1,0:T(1,128)}, u32[]{:S(2)}, u32[]{:S(2)}) collective-permute-start(f32[5,12,1,640]{3,2,1,0:T(1,128)} %get-tuple-element.53), channel_id=1, source_target_pairs={{0,2},{2,4},{4,6},{6,0},{1,3},{3,5},{5,7},{7,1},{8,10},{10,12},{12... | collective-permute-start | bytes 460808 | tf_op jit(solution)/shard_map/ppermute | solution.py:31
  234.3 34.8 %collective-permute-start.3 = (f32[5,12,1,640]{3,2,1,0:T(1,128)}, f32[5,12,1,640]{3,2,1,0:T(1,128)}, u32[]{:S(2)}, u32[]{:S(2)}) collective-permute-start(f32[5,12,1,640]{3,2,1,0:T(1,128)} %get-tuple-element.54), channel_id=1, source_target_pairs={{2,0},{4,2},{6,4},{0,6},{3,1},{5,3},{7,5},{1,7},{10,8},{12,10},{14... | collective-permute-start | bytes 460808 | tf_op jit(solution)/shard_map/ppermute | solution.py:34
  235.8 3.2 copy-start.15
  235.8 3.2 copy-start.46
  237.4 7.4 %collective-permute-start.10 = (f32[9,7,7,1]{3,1,0,2:T(8,128)S(1)}, f32[9,7,7,1]{3,1,0,2:T(8,128)S(1)}, u32[]{:S(2)}, u32[]{:S(2)}) collective-permute-start(f32[9,7,7,1]{3,1,0,2:T(8,128)S(1)} %get-tuple-element.66), channel_id=1, source_target_pairs={{0,1},{1,0},{2,3},{3,2},{4,5},{5,4},{6,7},{7,6},{8,9},{9,8},{10,11... | collective-permute-start | bytes 5300 | tf_op jit(solution)/shard_map/ppermute | solution.py:31
  237.9 12.5 %collective-permute-start.11 = (f32[9,7,7,1]{3,1,0,2:T(8,128)S(1)}, f32[9,7,7,1]{3,1,0,2:T(8,128)S(1)}, u32[]{:S(2)}, u32[]{:S(2)}) collective-permute-start(f32[9,7,7,1]{3,1,0,2:T(8,128)S(1)} %get-tuple-element.67), channel_id=1, source_target_pairs={{1,0},{0,1},{3,2},{2,3},{5,4},{4,5},{7,6},{6,7},{9,8},{8,9},{11,10... | collective-permute-start | bytes 5300 | tf_op jit(solution)/shard_map/ppermute | solution.py:34
  265.6 1.3 copy-start.52
  271.2 13.7 %collective-permute-start.4 = (f32[5,12,12,1]{3,2,1,0:T(8,128)}, f32[5,12,12,1]{3,2,1,0:T(8,128)S(1)}, u32[]{:S(2)}, u32[]{:S(2)}) collective-permute-start(f32[5,12,12,1]{3,2,1,0:T(8,128)} %get-tuple-element.38), channel_id=1, source_target_pairs={{0,1},{1,0},{2,3},{3,2},{4,5},{5,4},{6,7},{7,6},{8,9},{9,8},{10,11... | collective-permute-start | bytes 8648 | tf_op jit(solution)/shard_map/ppermute | solution.py:31
  271.2 22.2 %collective-permute-start.5 = (f32[5,12,12,1]{3,2,1,0:T(8,128)}, f32[5,12,12,1]{3,2,1,0:T(8,128)S(1)}, u32[]{:S(2)}, u32[]{:S(2)}) collective-permute-start(f32[5,12,12,1]{3,2,1,0:T(8,128)} %get-tuple-element.39), channel_id=1, source_target_pairs={{1,0},{0,1},{3,2},{2,3},{5,4},{4,5},{7,6},{6,7},{9,8},{8,9},{11,10... | collective-permute-start | bytes 8648 | tf_op jit(solution)/shard_map/ppermute | solution.py:34
  341.1 1.6 copy-start.16
  368.1 21.8 %copy-start.1 = (f32[5,10,10,640]{3,2,1,0:T(8,128)S(1)}, f32[5,10,10,640]{3,2,1,0:T(8,128)}, u32[]{:S(2)}) copy-start(f32[5,10,10,640]{3,2,1,0:T(8,128)} %param.10) | copy-start | bytes 3840004
  389.9 4.9 %copy-start.11 = (f32[512,375]{1,0:T(8,128)S(1)}, f32[512,375]{1,0:T(8,128)}, u32[]{:S(2)}) copy-start(f32[512,375]{1,0:T(8,128)} %copy.394) | copy-start | bytes 2304004
  394.8 1.1 copy-start.48
  407.3 2.3 copy-start.54
  417.2 4.5 %copy-start.10 = (f32[4,5,5,640]{3,0,2,1:T(4,128)S(1)}, f32[4,5,5,640]{3,0,2,1:T(4,128)}, u32[]{:S(2)}) copy-start(f32[4,5,5,640]{3,0,2,1:T(4,128)} %param.11) | copy-start | bytes 768004
  417.2 4.5 %copy-start.17 = (f32[5,4,5,640]{3,0,2,1:T(8,128)S(1)}, f32[5,4,5,640]{3,0,2,1:T(8,128)}, u32[]{:S(2)}) copy-start(f32[5,4,5,640]{3,0,2,1:T(8,128)} %fusion.44) | copy-start | bytes 768004
  417.2 4.5 %copy-start.26 = (f32[4,5,5,640]{3,1,2,0:T(8,128)S(1)}, f32[4,5,5,640]{3,1,2,0:T(8,128)}, u32[]{:S(2)}) copy-start(f32[4,5,5,640]{3,1,2,0:T(8,128)} %reshape.324) | copy-start | bytes 768004
  417.2 4.5 %copy-start.27 = (f32[5,5,640]{2,0,1:T(8,128)S(1)}, f32[5,5,640]{2,0,1:T(8,128)}, u32[]{:S(2)}) copy-start(f32[5,5,640]{2,0,1:T(8,128)} %get-tuple-element.81) | copy-start | bytes 192004
  417.2 4.5 %copy-start.37 = (f32[1,5,5,640]{3,1,2,0:T(8,128)S(1)}, f32[1,5,5,640]{3,1,2,0:T(8,128)}, u32[]{:S(2)}) copy-start(f32[1,5,5,640]{3,1,2,0:T(8,128)} %get-tuple-element.80) | copy-start | bytes 192004
  417.2 4.5 %copy-start.38 = (f32[4,5,1,1,640]{4,1,3,0,2:T(8,128)S(1)}, f32[4,5,1,1,640]{4,1,3,0,2:T(8,128)}, u32[]{:S(2)}) copy-start(f32[4,5,1,1,640]{4,1,3,0,2:T(8,128)} %get-tuple-element.109) | copy-start | bytes 153604
  417.2 4.5 %copy-start.39 = (f32[4,5,1,1,640]{4,1,3,0,2:T(8,128)S(1)}, f32[4,5,1,1,640]{4,1,3,0,2:T(8,128)}, u32[]{:S(2)}) copy-start(f32[4,5,1,1,640]{4,1,3,0,2:T(8,128)} %get-tuple-element.110) | copy-start | bytes 153604
  417.2 4.5 %copy-start.41 = (f32[4,1,1,5,640]{4,2,3,0,1:T(1,128)S(1)}, f32[4,1,1,5,640]{4,2,3,0,1:T(1,128)}, u32[]{:S(2)}) copy-start(f32[4,1,1,5,640]{4,2,3,0,1:T(1,128)} %copy.348) | copy-start | bytes 153604
  417.2 4.5 %copy-start.51 = (f32[4]{0:T(128)S(1)}, f32[4]{0:T(128)}, u32[]{:S(2)}) copy-start(f32[4]{0:T(128)} %copy-done.50) | copy-start | bytes 52
  (4 other events, 3.5 us)
where the time goes:
time: 431 us; the launch traced here: 424 us
  local copies, waits for them, and re-layouts  284 us (66%)
  other arithmetic  59.5 us (14%)
  matrix products  35.4 us (8%)
  starting transfers between devices  26.9 us (6%)
  waiting for transfers between devices  15.9 us (4%)
    sub x6, local copies, waits for them, and re-layouts, line_term(): return surface - volume  53.7 us
    another operation x6, local copies, waits for them, and re-layouts, lamb_vector(): jnp.stack([omega_second * velocity[2] - omega_third * velocity[1], omega_...  40.9 us
    another operation x18, local copies, waits for them, and re-layouts, euler_flux(): return jnp.stack(pieces)  33.9 us
    dot_general x12, matrix products, along_axis(): jnp.einsum(formula, blocks, matrix, precision=lax.Precision.HIGHEST)  31 us
    unnamed x131, local copies, waits for them, and re-layouts  23.5 us
    slice x6, local copies, waits for them, and re-layouts, line_term(): right_state = lax.slice_in_dim(extended, 1, length, 5, axis_dim)  20.7 us
    slice x4, local copies, waits for them, and re-layouts, line_term(): left_state = lax.slice_in_dim(extended, 0, length - 1, 5, axis_dim)  19.4 us
    div x4, local copies, waits for them, and re-layouts, euler_parts(): velocity = state[1 + direction] / density  17.5 us
  transfers between devices with their start and end apart: 13, of which 3 were waited for; matrix products, arithmetic and copies ran while one was open for 80% of the time, Pallas kernels for 0%

commit v1 on v0

v1 whole, which is shorter than its diff:
```python
import functools
import math

import jax
import jax.numpy as jnp
import numpy as np
from jax import lax
from jax.experimental import pallas as pl
from jax.experimental.pallas import tpu as pltpu
from jax.sharding import PartitionSpec as P

GAMMA = 1.4
DT = 0.05
LIFT = 10.0
F32 = jnp.float32
BF16 = jnp.bfloat16
NX = 640
NE = 128
VMEM_LIMIT = 48 * 1024 * 1024


def derivative_matrix():
    points = np.array([-1.0, -math.sqrt(3.0 / 7.0), 0.0, math.sqrt(3.0 / 7.0), 1.0])
    weights = np.array([1.0 / np.prod([points[j] - points[k] for k in range(5) if k != j]) for j in range(5)])
    matrix = np.zeros((5, 5))
    for i in range(5):
        for j in range(5):
            if i != j:
                matrix[i, j] = weights[j] / weights[i] / (points[i] - points[j])
        matrix[i, i] = -np.sum(matrix[i])
    return matrix


D = derivative_matrix()
T = -D.copy()
T[0, 0] -= LIFT
T[4, 4] += LIFT


def lane_split():
    p = np.zeros((NX, NX), np.float32)
    for e in range(NE):
        for j in range(5):
            p[5 * e + j, NE * j + e] = 1.0
    return p


def radial_coefs():
    inner, outer = T.copy(), T.copy()
    inner[0, 0] += LIFT
    outer[4, 4] -= LIFT
    out = np.zeros((4, 5, 8, 128), np.float32)
    for kind, m in enumerate((inner, outer, D, -D)):
        for k in range(5):
            out[kind, k, :5, :] = m[:, k][:, None]
    return out


def apply5(f, m):
    s = [f[0] + f[4], f[1] + f[3]]
    d = [f[0] - f[4], f[1] - f[3]]
    out = [None] * 5
    for i in range(2):
        even = (0.5 * (m[i, 0] + m[i, 4])) * s[0] + (0.5 * (m[i, 1] + m[i, 3])) * s[1] + m[i, 2] * f[2]
        odd = (0.5 * (m[i, 0] - m[i, 4])) * d[0] + (0.5 * (m[i, 1] - m[i, 3])) * d[1]
        out[i] = odd + even
        out[4 - i] = odd - even
    out[2] = (0.5 * (m[2, 0] - m[2, 4])) * d[0] + (0.5 * (m[2, 1] - m[2, 3])) * d[1]
    return out


def radial(f, coefs):
    total = coefs[0] * f[0:1, :]
    for k in range(1, 5):
        total = total + coefs[k] * f[k : k + 1, :]
    return total


def tile(j):
    return slice(NE * j, NE * j + NE)


def wide(ref):
    return jnp.concatenate([ref[j] for j in range(ref.shape[0])], axis=1)


def split(x):
    hi = x.astype(BF16)
    return hi, (x - hi.astype(F32)).astype(BF16)


def dot(a, b):
    return jnp.dot(a, b, preferred_element_type=F32)


def relane(x, matrix):
    rows = x.shape[0]
    y = dot(jnp.concatenate(split(x), axis=0), matrix)
    return y[:rows] + y[rows:]


def les_prims(q):
    rec = 1.0 / q[0]
    v = [q[1] * rec, q[2] * rec, q[3] * rec]
    p = 0.4 * (q[4] - 0.5 * (q[1] * v[0] + q[2] * v[1] + q[3] * v[2]))
    return rec, v, p


def les_flux(q, v, p, k):
    out = [q[1 + k]]
    for j in range(3):
        out.append(q[1 + j] * v[k] + p if j == k else q[1 + j] * v[k])
    out.append((q[4] + p) * v[k])
    return out


def les_speed(rec, v, p, k):
    return jnp.abs(v[k]) + jnp.sqrt(GAMMA * p * rec)


def common(fl, fr, sl, sr, ql, qr):
    half = 0.5 * jnp.maximum(sl, sr)
    return [0.5 * (fl[n] + fr[n]) - half * (qr[n] - ql[n]) for n in range(len(fl))]


def ape_carried(s):
    return s[6] * s[1] + s[7] * s[2] + s[8] * s[3] + s[0] / s[4]


def ape_leading(s, k):
    return s[5] * s[5] * s[4] * s[1 + k] + s[6 + k] * s[0]


def ape_common(l, r, k, fl=None, fr=None):
    if fl is None:
        fl = (ape_leading(l, k), ape_carried(l))
    if fr is None:
        fr = (ape_leading(r, k), ape_carried(r))
    half = 0.5 * jnp.maximum(jnp.abs(l[6 + k]) + l[5], jnp.abs(r[6 + k]) + r[5])
    out = []
    for n in range(4):
        value = -half * (r[n] - l[n])
        if n == 0:
            value = value + 0.5 * (fl[0] + fr[0])
        elif n == 1 + k:
            value = value + 0.5 * (fl[1] + fr[1])
        out.append(value)
    return out, fl, fr


B_ROWS, F_ROWS, G_ROWS = 224, 96, 160
B_APE = 176
F_APE = 50


def pack_kernel(les, ac, den, snd, mv, back, fwd, low, high, axial):
    for a in range(5):
        rec = 1.0 / les[0, a]
        for c in range(3):
            v = les[1 + c, a] * rec
            for j in range(5):
                back[j, c * 50 + a * 10 : c * 50 + a * 10 + 10, :] = v[:, tile(j)]
    for j in range(5):
        back[j, 150:160, :] = les[0, 0, :, tile(j)]
        back[j, 160:170, :] = les[4, 0, :, tile(j)]
        back[j, 170:176, :] = jnp.zeros((6, 128), F32)
        back[j, 221:224, :] = jnp.zeros((3, 128), F32)
        for buf, a, base in ((back, 0, B_APE), (fwd, 4, F_APE)):
            for r in range(5):
                buf[j, pl.ds(base + r, 4, stride=5), :] = ac[a, r, :, tile(j)]
                buf[j, pl.ds(base + 30 + r, 3, stride=5), :] = mv[a, r, :, tile(j)]
            buf[j, base + 20 : base + 25, :] = den[a, :, tile(j)]
            buf[j, base + 25 : base + 30, :] = snd[a, :, tile(j)]
        for c in range(5):
            fwd[j, c * 10 : c * 10 + 10, :] = les[c, 9, :, tile(j)]
        for buf, r, ra in ((low, 0, 0), (high, 9, 4)):
            for c in range(5):
                for a in range(10):
                    buf[j, c * 10 + a : c * 10 + a + 1, :] = les[c, a, r : r + 1, tile(j)]
            for a in range(5):
                buf[j, pl.ds(F_APE + a, 4, stride=5), :] = ac[a, ra, :, tile(j)]
                buf[j, pl.ds(F_APE + 30 + a, 3, stride=5), :] = mv[a, ra, :, tile(j)]
                buf[j, F_APE + 20 + a : F_APE + 21 + a, :] = den[a, ra : ra + 1, tile(j)]
                buf[j, F_APE + 25 + a : F_APE + 26 + a, :] = snd[a, ra : ra + 1, tile(j)]
        for buf in (fwd, low, high):
            buf[j, 95:96, :] = jnp.zeros((1, 128), F32)
    first = lax.axis_index("group") == 0

    def end(ref, *at):
        return jnp.where(first, ref[(*at, slice(None), slice(NX - 1, NX))], ref[(*at, slice(None), slice(0, 1))])

    def gather(columns, rows):
        lane = lax.broadcasted_iota(jnp.int32, (rows, 128), 1)
        value = jnp.broadcast_to(columns[0], (rows, 128))
        for i in range(1, len(columns)):
            value = jnp.where(lane == i, jnp.broadcast_to(columns[i], (rows, 128)), value)
        return value

    for c in range(5):
        axial[16 * c : 16 * c + 10, :] = gather([end(les, c, a) for a in range(10)], 10)
        axial[16 * c + 10 : 16 * c + 16, :] = jnp.ones((6, 128), F32)
    axial[80:84, :] = gather([end(ac, a, r) for a in range(5) for r in range(5)], 4)
    axial[84:87, :] = gather([end(mv, a, r) for a in range(5) for r in range(5)], 3)
    axial[87:88, :] = jnp.zeros((1, 128), F32)
    axial[88:93, :] = gather([end(den, a) for a in range(5)], 5)
    axial[93:96, :] = jnp.zeros((3, 128), F32)
    axial[96:101, :] = gather([end(snd, a) for a in range(5)], 5)
    axial[101:160, :] = jnp.zeros((59, 128), F32)


def project(s, pp_hi, pp_lo, rhs_hi, rhs_lo, osc):
    for p in range(8):
        for c in range(3):
            hi, lo = split(s[c * 128 : c * 128 + 128, tile(p)])
            rhs_hi[p * 128 : p * 128 + 128, tile(c)] = hi
            rhs_lo[p * 128 : p * 128 + 128, tile(c)] = lo
    hi = rhs_hi[...]
    out = dot(pp_hi[...], hi) + (dot(pp_lo[...], hi) + dot(pp_hi[...], rhs_lo[...]))
    for c in range(3):
        osc[c] = out[:, tile(c)]


def interior_kernel(
    les, ac, den, snd, mv, proj, counts, elem, pattern, perm, perm_t, coef,
    les_out, ac_out, mn_out, pp_hi, pp_lo,
    y, acc, vel, omega, rt, m_own, one_hot, owned, s_own, rhs_hi, rhs_lo, osc, la, ya, da, flat,
):
    upper = lax.broadcasted_iota(jnp.int32, (NE, NE), 1)
    lower = lax.broadcasted_iota(jnp.int32, (NE, NE), 0)
    row = jnp.broadcast_to(counts[...], (NE, NE)).astype(F32)
    ends = jnp.sum(jnp.where(upper <= lower, row, 0.0), axis=1, keepdims=True)
    starts = jnp.sum(jnp.where(upper < lower, row, 0.0), axis=1, keepdims=True)
    position = lax.broadcasted_iota(jnp.int32, (NE, 768), 1).astype(F32)
    mine = jnp.where((position >= starts) & (position < ends), jnp.broadcast_to(pattern[...], (NE, 768)), -1)
    for p in range(8):
        owned[p * NE : p * NE + NE, :] = jnp.where(mine == p, 1.0, 0.0).astype(BF16)
    source = jnp.broadcast_to(elem[...], (NE, 768))
    for i in range(6):
        which = lax.broadcasted_iota(jnp.int32, (NE, 768), 0) + i * NE
        one_hot[i * NE : i * NE + NE, :] = jnp.where(which == source, 1.0, 0.0).astype(BF16)

    @pl.loop(0, 4)
    def _(i):
        rows = pl.ds(pl.multiple_of(i * NE, NE), NE)
        m_own[rows, :] = lax.dot_general(
            one_hot[rows, :], owned[...], (((1,), (1,)), ((), ())), preferred_element_type=F32
        ).astype(BF16)

    for i in range(2):
        mn_out[i * NE : i * NE + NE, :] = lax.dot_general(
            one_hot[(4 + i) * NE : (5 + i) * NE, :], owned[...], (((1,), (1,)), ((), ())), preferred_element_type=F32
        ).astype(BF16)

    flat[...] = jnp.zeros((1024, 128), F32)
    flat[0:1000, 0:125] = proj[...]
    for p in range(8):
        hi, lo = split(flat[pl.ds(p, 128, stride=8), :])
        pp_hi[:, tile(p)] = hi
        pp_lo[:, tile(p)] = lo

    @pl.loop(0, 5)
    def _(c):
        x0 = les[c, :, 0:8, :].reshape(80, NX)
        x1 = pltpu.roll(les[c, :, 2:10, :], 5, 1).reshape(80, NX)
        value = relane(jnp.concatenate([x0, x1], axis=0), perm[...])
        for j in range(5):
            y[c, j] = value[:, tile(j)]

    lane = lax.broadcasted_iota(jnp.int32, (8, 128), 1)

    @pl.loop(0, 20)
    def _(t):
        er = t // 10
        rows = pl.ds(pl.multiple_of(t * 8, 8), 8)
        q = [[y[c, j, rows, :] for j in range(5)] for c in range(5)]
        rec, v, p = [], [[], [], []], []
        for j in range(5):
            rec_j, v_j, p_j = les_prims([q[c][j] for c in range(5)])
            rec.append(rec_j)
            p.append(p_j)
            for k in range(3):
                v[k].append(v_j[k])
                vel[k, j, rows, :] = v_j[k]
            vel[3, j, rows, :] = p_j
        coefs = [coef[er, k] for k in range(5)]
        flux = [les_flux([q[c][j] for c in range(5)], [v[k][j] for k in range(3)], p[j], 2) for j in range(5)]
        s_left = les_speed(rec[4], [v[k][4] for k in range(3)], p[4], 2)
        s_right = pltpu.roll(les_speed(rec[0], [v[k][0] for k in range(3)], p[0], 2), 127, 1)
        half = 0.5 * jnp.maximum(s_left, s_right)
        for n in range(5):
            fr = pltpu.roll(flux[0][n], 127, 1)
            qr = pltpu.roll(q[n][0], 127, 1)
            h = 0.5 * (flux[4][n] + fr) - half * (qr - q[n][4])
            out = apply5([flux[j][n] for j in range(5)], T)
            out[4] = out[4] - LIFT * jnp.where(lane < 127, h, flux[4][n])
            out[0] = out[0] + LIFT * jnp.where(lane > 0, pltpu.roll(h, 1, 1), flux[0][n])
            for j in range(5):
                f = les_flux([q[c][j] for c in range(5)], [v[k][j] for k in range(3)], p[j], 1)[n]
                acc[n, j, rows, :] = out[j] + radial(f, coefs)
        dcoefs = [coef[2, k] for k in range(5)]
        d2v0 = apply5(v[0], D)
        d2v1 = apply5(v[1], D)
        for j in range(5):
            omega[0, j, rows, :] = radial(v[2][j], dcoefs) - d2v1[j]
            omega[1, j, rows, :] = d2v0[j]
            omega[2, j, rows, :] = -radial(v[0][j], dcoefs)

    for c in range(3):
        for i in range(4):
            rt[i, c * 128 + 120 : c * 128 + 128, :] = jnp.zeros((8, 128), F32)

    @pl.loop(0, 2)
    def _(er):
        for j in range(5):
            at = [pl.ds(pl.multiple_of(er * 80 + a * 8, 8), 8) for a in range(10)]
            q = [[y[c, j, at[a], :] for a in range(10)] for c in range(5)]
            v = [[vel[k, j, at[a], :] for a in range(10)] for k in range(3)]
            p = [vel[3, j, at[a], :] for a in range(10)]
            flux = [les_flux([q[c][a] for c in range(5)], [v[k][a] for k in range(3)], p[a], 0) for a in range(10)]
            speed = [
                jnp.abs(v[0][a]) + jnp.sqrt(GAMMA * p[a] / q[0][a]) for a in (4, 5)
            ]
            h = common(flux[4], flux[5], speed[0], speed[1], [q[c][4] for c in range(5)], [q[c][5] for c in range(5)])
            for n in range(5):
                low = apply5([flux[a][n] for a in range(5)], T)
                low[0] = low[0] + LIFT * flux[0][n]
                low[4] = low[4] - LIFT * h[n]
                top = apply5([flux[5 + a][n] for a in range(5)], T)
                top[0] = top[0] + LIFT * h[n]
                top[4] = top[4] - LIFT * flux[9][n]
                for a, value in enumerate(low + top):
                    acc[n, j, at[a], :] = acc[n, j, at[a], :] + value
            for ea in range(2):
                d0v1 = apply5([v[1][5 * ea + i] for i in range(5)], D)
                d0v2 = apply5([v[2][5 * ea + i] for i in range(5)], D)
                for i in range(5):
                    a = 5 * ea + i
                    w0 = omega[0, j, at[a], :]
                    w1 = omega[1, j, at[a], :] - d0v2[i]
                    w2 = omega[2, j, at[a], :] + d0v1[i]
                    lamb = [
                        w1 * v[2][a] - w2 * v[1][a],
                        w2 * v[0][a] - w0 * v[2][a],
                        w0 * v[1][a] - w1 * v[0][a],
                    ]
                    for c in range(3):
                        rt[2 * ea + er, pl.ds(c * 128 + i * 25 + j, 5, stride=5), :] = lamb[c][0:5]

    for j in range(5):
        left, right = pl.ds(4, 10, stride=8), pl.ds(80, 10, stride=8)
        ql = [y[c, j, left, :] for c in range(5)]
        qr = [y[c, j, right, :] for c in range(5)]
        rl, vl, pl_ = les_prims(ql)
        rr, vr, pr = les_prims(qr)
        h = common(
            les_flux(ql, vl, pl_, 1), les_flux(qr, vr, pr, 1),
            les_speed(rl, vl, pl_, 1), les_speed(rr, vr, pr, 1), ql, qr,
        )
        for n in range(5):
            acc[n, j, left, :] = acc[n, j, left, :] - LIFT * h[n]
            acc[n, j, right, :] = acc[n, j, right, :] + LIFT * h[n]

    @pl.loop(0, 5)
    def _(c):
        delta = relane(jnp.concatenate([acc[c, j] for j in range(5)], axis=1), perm_t[...]).reshape(2, 10, 8, NX)
        les_out[c, :, 0:5, :] = les[c, :, 0:5, :] + DT * delta[0, :, 0:5, :]
        les_out[c, :, 5:10, :] = les[c, :, 5:10, :] + DT * delta[1, :, 0:5, :]

    hi, lo = split(wide(rt))
    m = m_own[...]
    s_own[...] = dot(hi, m) + dot(lo, m)
    project(s_own, pp_hi, pp_lo, rhs_hi, rhs_lo, osc)

    for a in range(5):
        for r in range(5):
            la[a * 20 + r * 4 : a * 20 + r * 4 + 4, :] = ac[a, r]
            la[104 + a * 15 + r * 3 : 104 + a * 15 + r * 3 + 3, :] = mv[a, r]
        la[184 + a * 8 : 184 + a * 8 + 5, :] = den[a]
        la[224 + a * 8 : 224 + a * 8 + 5, :] = snd[a]
    value = relane(la[...], perm[...])
    for j in range(5):
        ya[j] = value[:, tile(j)]
    lane5 = lax.broadcasted_iota(jnp.int32, (5, 128), 1)
    state = [[None] * 5 for _ in range(5)]
    for a in range(5):
        for j in range(5):
            state[a][j] = (
                [ya[j, pl.ds(a * 20 + c, 5, stride=4), :] for c in range(4)]
                + [ya[j, 184 + a * 8 : 189 + a * 8, :], ya[j, 224 + a * 8 : 229 + a * 8, :]]
                + [ya[j, pl.ds(104 + a * 15 + k, 5, stride=3), :] for k in range(3)]
            )
    carried = [[ape_carried(state[a][j]) for j in range(5)] for a in range(5)]
    lead = [[[ape_leading(state[a][j], k) for j in range(5)] for a in range(5)] for k in range(3)]
    total = [[[None] * 5 for _ in range(5)] for _ in range(4)]
    minus = -D
    mcoefs = [coef[3, k, 0:5] for k in range(5)]
    for j in range(5):
        first = apply5([lead[0][a][j] for a in range(5)], minus)
        other = apply5([carried[a][j] for a in range(5)], minus)
        for a in range(5):
            total[0][a][j] = first[a] + radial(lead[1][a][j], mcoefs)
            total[1][a][j] = other[a]
            total[2][a][j] = radial(carried[a][j], mcoefs)
    for a in range(5):
        first = apply5(lead[2][a], T)
        other = apply5(carried[a], T)
        shift = [pltpu.roll(jnp.pad(x, ((0, 3), (0, 0))), 127, 1)[0:5] for x in state[a][0]]
        h, fl, fr = ape_common(state[a][4], shift, 2)
        for n in range(4):
            own4 = lead[2][a][4] if n == 0 else carried[a][4] if n == 3 else jnp.zeros_like(carried[a][4])
            own0 = lead[2][a][0] if n == 0 else carried[a][0] if n == 3 else jnp.zeros_like(carried[a][0])
            back = pltpu.roll(jnp.pad(h[n], ((0, 3), (0, 0))), 1, 1)[0:5]
            lift4 = -LIFT * jnp.where(lane5 < 127, h[n], own4)
            lift0 = LIFT * jnp.where(lane5 > 0, back, own0)
            for j in range(5):
                value = total[n][a][j]
                if n in (0, 3):
                    extra = first[j] if n == 0 else other[j]
                    value = extra if value is None else value + extra
                if j == 4:
                    value = value + lift4
                if j == 0:
                    value = value + lift0
                if n > 0:
                    value = value - osc[n - 1, pl.ds(a * 25 + j, 5, stride=5), :]
                da[j, pl.ds(a * 20 + n, 5, stride=4), :] = value
    for j in range(5):
        da[j, 100:104, :] = jnp.zeros((4, 128), F32)
    delta = relane(wide(da), perm_t[...])
    for a in range(5):
        for r in range(5):
            i = (a * 5 + r) * 4
            ac_out[a, r] = ac[a, r] + DT * delta[i : i + 4]


def ape_face(buf, base, j):
    return [buf[j, base + 5 * n : base + 5 * n + 5, :] for n in range(9)]


def back_face(buf, j):
    rho = buf[j, 150:160, :]
    return [rho] + [rho * buf[j, c * 50 : c * 50 + 10, :] for c in range(3)] + [buf[j, 160:170, :]]


def les_rows(buf, j):
    return [buf[j, c * 10 : c * 10 + 10, :] for c in range(5)]


def les_common(ql, qr, k):
    rl, vl, pl_ = les_prims(ql)
    rr, vr, pr = les_prims(qr)
    fl, fr = les_flux(ql, vl, pl_, k), les_flux(qr, vr, pr, k)
    return common(fl, fr, les_speed(rl, vl, pl_, k), les_speed(rr, vr, pr, k), ql, qr), fl, fr


def faces_kernel(
    les_in, ac_in, back, fwd, low, high, axial, fwd_in, low_in, high_in, axial_in, les_out, ac_out, sub, azim, aub,
):
    rad = lax.axis_index("rad")
    first_half = lax.axis_index("group") == 0
    at_low, at_high = rad == 0, rad == lax.axis_size("rad") - 1
    for j in range(5):
        own_low, own_high = les_rows(low, j), les_rows(high, j)
        nbr_low = [jnp.where(at_low, o, n) for o, n in zip(own_low, les_rows(low_in, j))]
        nbr_high = [jnp.where(at_high, o, n) for o, n in zip(own_high, les_rows(high_in, j))]
        h, _, fr = les_common(nbr_low, own_low, 1)
        g, fl, _ = les_common(own_high, nbr_high, 1)
        for n in range(5):
            sub[n * 24 : n * 24 + 10, tile(j)] = DT * LIFT * (h[n] - fr[n])
            sub[n * 24 + 10 : n * 24 + 20, tile(j)] = DT * LIFT * (fl[n] - g[n])
        h, _, fr = les_common(les_rows(fwd_in, j), back_face(back, j), 0)
        for n in range(5):
            azim[n * 16 : n * 16 + 10, tile(j)] = DT * LIFT * (h[n] - fr[n])
    own = [axial[16 * c : 16 * c + 16, :] for c in range(5)]
    nbr = [axial_in[16 * c : 16 * c + 16, :] for c in range(5)]
    ql = [jnp.where(first_half, o, n) for o, n in zip(own, nbr)]
    qr = [jnp.where(first_half, n, o) for o, n in zip(own, nbr)]
    h, fl, fr = les_common(ql, qr, 2)
    axis = [DT * LIFT * jnp.where(first_half, fl[n] - h[n], h[n] - fr[n]) for n in range(5)]
    lane = lax.broadcasted_iota(jnp.int32, (10, 128), 1)
    on_last = (lane == 127) & first_half
    on_first = (lane == 0) & jnp.logical_not(first_half)
    for n in range(5):
        for a in range(10):
            value = les_in[n, a]
            column = jnp.broadcast_to(axis[n][0:10, a : a + 1], (10, 128))
            head = value[:, 0:128] + jnp.where(on_first, column, 0.0)
            tail = value[:, 512:640] + jnp.where(on_last, column, 0.0)
            value = jnp.concatenate([head, value[:, 128:512], tail], axis=1)
            if a == 0:
                value = value + azim[n * 16 : n * 16 + 10, :]
            les_out[n, a] = value
            les_out[n, a, 0:1, :] = les_out[n, a, 0:1, :] + sub[n * 24 + a : n * 24 + a + 1, :]
            les_out[n, a, 9:10, :] = les_out[n, a, 9:10, :] + sub[n * 24 + 10 + a : n * 24 + 11 + a, :]

    for j in range(5):
        aub[j] = jnp.zeros((104, 128), F32)
        h, _, fr = ape_common(ape_face(fwd_in, F_APE, j), ape_face(back, B_APE, j), 0)
        for n in range(4):
            own_flux = fr[0] if n == 0 else fr[1] if n == 1 else 0.0
            aub[j, pl.ds(n, 5, stride=4), :] = DT * LIFT * (h[n] - own_flux)
        own_l, own_h = ape_face(low, F_APE, j), ape_face(high, F_APE, j)
        nbr_l = [jnp.where(at_low, o, n) for o, n in zip(own_l, ape_face(low_in, F_APE, j))]
        nbr_h = [jnp.where(at_high, o, n) for o, n in zip(own_h, ape_face(high_in, F_APE, j))]
        h, _, fr = ape_common(nbr_l, own_l, 1)
        g, fl, _ = ape_common(own_h, nbr_h, 1)
        for n in range(4):
            fr_n = fr[0] if n == 0 else fr[1] if n == 2 else 0.0
            fl_n = fl[0] if n == 0 else fl[1] if n == 2 else 0.0
            at = pl.ds(n, 5, stride=20)
            aub[j, at, :] = aub[j, at, :] + DT * LIFT * (h[n] - fr_n)
            at = pl.ds(16 + n, 5, stride=20)
            aub[j, at, :] = aub[j, at, :] + DT * LIFT * (fl_n - g[n])

    def axial_state(buf):
        def spread(base):
            rows = buf[base : base + 8, :]
            row = lax.broadcasted_iota(jnp.int32, (8, 128), 0)
            lanes = lax.broadcasted_iota(jnp.int32, (8, 128), 1)
            wide = jnp.zeros((8, 128), F32)
            for a in range(5):
                wide = jnp.where((lanes == a * 5 + row) & (row < 5), jnp.broadcast_to(rows[:, a : a + 1], (8, 128)), wide)
            return jnp.sum(wide, axis=0, keepdims=True)

        ones = lax.broadcasted_iota(jnp.int32, (1, 128), 1) < 25
        return (
            [buf[80 + c : 81 + c, :] for c in range(4)]
            + [jnp.where(ones, spread(88), 1.0), spread(96)]
            + [buf[84 + k : 85 + k, :] for k in range(3)]
        )

    own, nbr = axial_state(axial), axial_state(axial_in)
    ql = [jnp.where(first_half, o, n) for o, n in zip(own, nbr)]
    qr = [jnp.where(first_half, n, o) for o, n in zip(own, nbr)]
    h, fl, fr = ape_common(ql, qr, 2)
    rows = []
    for n in range(4):
        fl_n = fl[0] if n == 0 else fl[1] if n == 3 else 0.0
        fr_n = fr[0] if n == 0 else fr[1] if n == 3 else 0.0
        rows.append(DT * LIFT * jnp.where(first_half, fl_n - h[n], h[n] - fr_n))
    axis = jnp.concatenate(rows, axis=0)
    lane4 = lax.broadcasted_iota(jnp.int32, (4, 128), 1)
    on_last = (lane4 == 127) & first_half
    on_first = (lane4 == 0) & jnp.logical_not(first_half)
    for a in range(5):
        for r in range(5):
            i = a * 5 + r
            value = ac_in[a, r] + jnp.concatenate([aub[j, 4 * i : 4 * i + 4, :] for j in range(5)], axis=1)
            column = jnp.broadcast_to(axis[:, i : i + 1], (4, 128))
            head = value[:, 0:128] + jnp.where(on_first, column, 0.0)
            tail = value[:, 512:640] + jnp.where(on_last, column, 0.0)
            ac_out[a, r] = jnp.concatenate([head, value[:, 128:512], tail], axis=1)


def finish_kernel(
    les_in, ac_in, back_in, fwd, mn, pp_hi, pp_lo, perm, perm_t, coef,
    les_out, ac_out, yn, rt, s_nbr, rhs_hi, rhs_lo, osc, da,
):
    yn[...] = relane(jnp.concatenate([back_in[j, 0:160, :] for j in range(5)], axis=1), perm[...])
    for c in range(3):
        for i in range(2):
            rt[i, c * 128 + 120 : c * 128 + 128, :] = jnp.zeros((8, 128), F32)
    dcoefs = [coef[2, k] for k in range(5)]
    for er in range(2):
        v = [
            [[yn[c * 50 + a * 10 + er * 5 : c * 50 + a * 10 + er * 5 + 8, tile(j)] for j in range(5)] for a in range(5)]
            for c in range(3)
        ]
        d2v0 = [apply5(v[0][a], D) for a in range(5)]
        d2v1 = [apply5(v[1][a], D) for a in range(5)]
        for j in range(5):
            d0v1 = apply5([v[1][a][j] for a in range(5)], D)
            d0v2 = apply5([v[2][a][j] for a in range(5)], D)
            for a in range(5):
                w0 = radial(v[2][a][j], dcoefs) - d2v1[a][j]
                w1 = d2v0[a][j] - d0v2[a]
                w2 = d0v1[a] - radial(v[0][a][j], dcoefs)
                lamb = [
                    w1 * v[2][a][j] - w2 * v[1][a][j],
                    w2 * v[0][a][j] - w0 * v[2][a][j],
                    w0 * v[1][a][j] - w1 * v[0][a][j],
                ]
                for c in range(3):
                    rt[er, pl.ds(c * 128 + a * 25 + j, 5, stride=5), :] = lamb[c][0:5]
    hi, lo = split(wide(rt))
    m = mn[...]
    s_nbr[...] = dot(hi, m) + dot(lo, m)
    project(s_nbr, pp_hi, pp_lo, rhs_hi, rhs_lo, osc)
    for j in range(5):
        da[j] = jnp.zeros((104, 128), F32)
        for a in range(5):
            for n in range(1, 4):
                da[j, pl.ds(a * 20 + n, 5, stride=4), :] = osc[n - 1, pl.ds(a * 25 + j, 5, stride=5), :]
    delta = relane(wide(da), perm_t[...])
    for j in range(5):
        h, fl, _ = les_common(les_rows(fwd, j), back_face(back_in, j), 0)
        for n in range(5):
            les_out[n, 0, :, tile(j)] = les_in[n, 0, :, tile(j)] + DT * LIFT * (fl[n] - h[n])
        da[j] = delta[:, tile(j)]
        h, fl, _ = ape_common(ape_face(fwd, F_APE, j), ape_face(back_in, B_APE, j), 0)
        for n in range(4):
            own_flux = fl[0] if n == 0 else fl[1] if n == 1 else 0.0
            at = pl.ds(80 + n, 5, stride=4)
            da[j, at, :] = da[j, at, :] - LIFT * (own_flux - h[n])
        for a in range(5):
            for r in range(5):
                i = (a * 5 + r) * 4
                ac_out[a, r, :, tile(j)] = ac_in[a, r, :, tile(j)] - DT * da[j, i : i + 4, :]


def shape(*dims, dtype=F32):
    return jax.ShapeDtypeStruct(dims, dtype)


def cost(flops, size):
    return pl.CostEstimate(flops=flops, bytes_accessed=size, transcendentals=0)


def params():
    return pltpu.CompilerParams(vmem_limit_bytes=VMEM_LIMIT)


def body(les, ac, den, snd, mv, proj, counts, elem, pattern):
    vmem = pl.BlockSpec(memory_space=pltpu.VMEM)
    ac = jnp.transpose(ac, (1, 2, 0, 3))
    mv = jnp.transpose(mv, (1, 2, 0, 3))
    proj = jnp.transpose(proj, (1, 0, 2)).reshape(1000, 125)
    counts, elem, pattern = counts.reshape(1, 128), elem.reshape(1, 768), pattern.reshape(1, 768)
    perm = jnp.asarray(lane_split(), BF16)
    perm_t = jnp.asarray(lane_split().T, BF16)
    coef = jnp.asarray(radial_coefs(), F32)

    back, fwd, low, high, axial = pl.pallas_call(
        pack_kernel,
        out_shape=[shape(5, B_ROWS, 128)] + [shape(5, F_ROWS, 128)] * 3 + [shape(G_ROWS, 128)],
        in_specs=[vmem] * 5,
        out_specs=[vmem] * 5,
        compiler_params=params(),
        cost_estimate=cost(1_000_000, 5_000_000),
        name="pack",
    )(les, ac, den, snd, mv)

    azim, radc = lax.axis_size("azim"), lax.axis_size("rad")
    back_in = lax.ppermute(back, "azim", [(i, (i - 1) % azim) for i in range(azim)])
    fwd_in = lax.ppermute(fwd, "azim", [(i, (i + 1) % azim) for i in range(azim)])
    high_in = lax.ppermute(low, "rad", [(i, i - 1) for i in range(1, radc)])
    low_in = lax.ppermute(high, "rad", [(i, i + 1) for i in range(radc - 1)])
    axial_in = lax.ppermute(axial, "group", [(0, 1), (1, 0)])

    les_part, ac_part, mn, pp_hi, pp_lo = pl.pallas_call(
        interior_kernel,
        out_shape=[
            shape(5, 10, 10, NX), shape(5, 5, 4, NX), shape(256, 1024, dtype=BF16),
            shape(128, 1024, dtype=BF16), shape(128, 1024, dtype=BF16),
        ],
        in_specs=[vmem] * 12,
        out_specs=[vmem] * 5,
        scratch_shapes=[
            pltpu.VMEM((5, 5, 160, 128), F32),
            pltpu.VMEM((5, 5, 160, 128), F32),
            pltpu.VMEM((4, 5, 160, 128), F32),
            pltpu.VMEM((3, 5, 160, 128), F32),
            pltpu.VMEM((4, 384, 128), F32),
            pltpu.VMEM((512, 1024), BF16),
            pltpu.VMEM((768, 768), BF16),
            pltpu.VMEM((1024, 768), BF16),
            pltpu.VMEM((384, 1024), F32),
            pltpu.VMEM((1024, 384), BF16),
            pltpu.VMEM((1024, 384), BF16),
            pltpu.VMEM((3, 128, 128), F32),
            pltpu.VMEM((264, NX), F32),
            pltpu.VMEM((5, 264, 128), F32),
            pltpu.VMEM((5, 104, 128), F32),
            pltpu.VMEM((1024, 128), F32),
        ],
        compiler_params=params(),
        cost_estimate=cost(5_000_000_000, 10_000_000),
        name="interior",
    )(les, ac, den, snd, mv, proj, counts, elem, pattern, perm, perm_t, coef)

    les_part, ac_part = pl.pallas_call(
        faces_kernel,
        out_shape=[shape(5, 10, 10, NX), shape(5, 5, 4, NX)],
        in_specs=[vmem] * 11,
        out_specs=[vmem] * 2,
        scratch_shapes=[pltpu.VMEM((120, NX), F32), pltpu.VMEM((80, NX), F32), pltpu.VMEM((5, 104, 128), F32)],
        input_output_aliases={0: 0, 1: 1},
        compiler_params=params(),
        cost_estimate=cost(1_000_000, 5_000_000),
        name="faces",
    )(les_part, ac_part, back, fwd, low, high, axial, fwd_in, low_in, high_in, axial_in)

    plane = pl.BlockSpec((5, 1, 10, NX), lambda i: (0, 9, 0, 0))

    def whole(*dims):
        return pl.BlockSpec(dims, lambda i: (0,) * len(dims))

    les_next, ac_next = pl.pallas_call(
        finish_kernel,
        grid=(1,),
        out_shape=[shape(5, 10, 10, NX), shape(5, 5, 4, NX)],
        in_specs=[
            plane, whole(5, 5, 4, NX), whole(5, B_ROWS, 128), whole(5, F_ROWS, 128), whole(256, 1024), whole(128, 1024),
            whole(128, 1024), whole(NX, NX), whole(NX, NX), whole(4, 5, 8, 128),
        ],
        out_specs=[plane, whole(5, 5, 4, NX)],
        scratch_shapes=[
            pltpu.VMEM((160, NX), F32),
            pltpu.VMEM((2, 384, 128), F32),
            pltpu.VMEM((384, 1024), F32),
            pltpu.VMEM((1024, 384), BF16),
            pltpu.VMEM((1024, 384), BF16),
            pltpu.VMEM((3, 128, 128), F32),
            pltpu.VMEM((5, 104, 128), F32),
        ],
        input_output_aliases={0: 0, 1: 1},
        compiler_params=params(),
        cost_estimate=cost(500_000_000, 4_000_000),
        name="finish",
    )(les_part, ac_part, back_in, fwd, mn, pp_hi, pp_lo, perm, perm_t, coef)
    return les_next, jnp.transpose(ac_next, (2, 0, 1, 3))


def solution(mesh):
    field = P(None, "azim", "rad", "group")
    node = P("azim", "rad", "group")
    lists = P("azim", "rad", "group", None)
    return jax.shard_map(
        body,
        mesh=mesh,
        in_specs=(field, field, node, node, field, P(), lists, lists, lists),
        out_specs=(field, field),
        check_vma=False,
    )
```

time: 431 us -> 51.5 us (0.12); the launches traced: 424 us -> 51.1 us
  local copies, waits for them, and re-layouts: 284 us -> 5.29 us
  other arithmetic: 59.5 us -> 0 us
  matrix products: 35.4 us -> 0 us
  Pallas kernels: 0 us -> 28.2 us
  waiting for transfers between devices: 15.9 us -> 0.01 us
  starting transfers between devices: 26.9 us -> 16.9 us
    another operation x45 -> x0, local copies, waits for them, and re-layouts: 85.2 us -> none  [the longest x6 40.9 us: lamb_vector(): jnp.stack([omega_second * velocity[2] - omega_third * velocity[1], omega_...]
    slice x25 -> x0, local copies, waits for them, and re-layouts: 55.4 us -> none  [the longest x6 20.7 us: line_term(): right_state = lax.slice_in_dim(extended, 1, length, 5, axis_dim)]
    sub x6 -> x0, local copies, waits for them, and re-layouts: 53.7 us -> none  [line_term(): return surface - volume]
    dot_general x13 -> x0, matrix products: 35.4 us -> none  [the longest x12 31 us: along_axis(): jnp.einsum(formula, blocks, matrix, precision=lax.Precision.HIGHEST)]
    pallas_call x0 -> x4, Pallas kernels: none -> 28.2 us  [the longest x1 18.4 us: body(): pl.pallas_call(interior_kernel, out_shape=[shape(5, 10, 10, NX), shape(5,...]
    reshape x7 -> x0, local copies, waits for them, and re-layouts: 23 us -> none  [the longest x2 11.4 us: along_axis(): return result.reshape(extent)]
    unnamed x131 -> x24, local copies, waits for them, and re-layouts: 23.5 us -> 5.29 us
    div x4 -> x0, local copies, waits for them, and re-layouts: 17.5 us -> none  [euler_parts(): velocity = state[1 + direction] / density]
  transfers between devices with their start and end apart: 13 -> 5, of which waited for: 3 -> 0; matrix products, arithmetic and copies ran while one was open for 80% -> 0% of each run, Pallas kernels for 0% -> 44%
where the time goes in v1:
time: 51.5 us; the launch traced here: 51.1 us
  Pallas kernels  28.2 us (55%)
  starting transfers between devices  16.9 us (33%)
  local copies, waits for them, and re-layouts  5.29 us (10%)
  between operations  0.74 us (1%)
    pallas_call x1, Pallas kernels, body(): pl.pallas_call(interior_kernel, out_shape=[shape(5, 10, 10, NX), shape(5,...  18.4 us
    ppermute x1, starting transfers between devices, body(): lax.ppermute(back, 'azim', [(i, (i - 1) % azim) for i in range(azim)])  8.68 us
    ppermute x1, starting transfers between devices, body(): low_in = lax.ppermute(high, 'rad', [(i, i + 1) for i in range(radc - 1)])  5.65 us
    unnamed x24, local copies, waits for them, and re-layouts  5.29 us
    pallas_call x1, Pallas kernels, body(): pl.pallas_call(finish_kernel, grid=(1,), out_shape=[shape(5, 10, 10, NX),...  5.04 us
    pallas_call x1, Pallas kernels, body(): pl.pallas_call(faces_kernel, out_shape=[shape(5, 10, 10, NX), shape(5, 5,...  3.84 us
    ppermute x1, starting transfers between devices, body(): high_in = lax.ppermute(low, 'rad', [(i, i - 1) for i in range(1, radc)])  1.92 us
  transfers between devices with their start and end apart: 5, of which 0 were waited for; matrix products, arithmetic and copies ran while one was open for 0% of the time, Pallas kernels for 44%

profile of v1, /device:TPU:1, one launch (start us, length us, event | category | flops | bytes accessed | tf_op | source)
XLA Modules:
  0.0 51.1 jit_solution(5203497241964742494)
XLA Ops:
  0.6 0.0 copy-start.11
  0.6 0.0 copy-start.9
  0.7 0.0 copy-start
  0.7 1.6 %copy-done = f32[5,10,10,640]{3,2,1,0:T(8,128)S(1)} copy-done((f32[5,10,10,640]{3,2,1,0:T(8,128)S(1)}, f32[5,10,10,640]{3,2,1,0:T(8,128)}, u32[]{:S(2)}) %copy-start) | copy-done | bytes 1280024
  2.2 0.0 copy-start.3
  2.2 0.9 %copy-done.3 = f32[4,5,5,640]{3,0,2,1:T(4,128)S(1)} copy-done((f32[4,5,5,640]{3,0,2,1:T(4,128)S(1)}, f32[4,5,5,640]{3,0,2,1:T(4,128)}, u32[]{:S(2)}) %copy-start.3) | copy-done | bytes 256024
  3.2 0.0 copy-start.4
  3.2 0.9 %copy-done.4 = f32[3,5,5,640]{3,0,2,1:T(4,128)S(1)} copy-done((f32[3,5,5,640]{3,0,2,1:T(4,128)S(1)}, f32[3,5,5,640]{3,0,2,1:T(4,128)}, u32[]{:S(2)}) %copy-start.4) | copy-done | bytes 192024
  4.1 0.0 copy-start.5
  4.1 0.9 %copy-done.5 = f32[5,5,640]{2,1,0:T(8,128)S(1)} copy-done((f32[5,5,640]{2,1,0:T(8,128)S(1)}, f32[5,5,640]{2,1,0:T(8,128)}, u32[]{:S(2)}) %copy-start.5) | copy-done | bytes 64024
  5.0 0.0 copy-start.6
  5.0 0.9 %copy-done.6 = f32[5,5,640]{2,1,0:T(8,128)S(1)} copy-done((f32[5,5,640]{2,1,0:T(8,128)S(1)}, f32[5,5,640]{2,1,0:T(8,128)}, u32[]{:S(2)}) %copy-start.6) | copy-done | bytes 64024
  5.9 0.0 copy-start.1
  5.9 0.0 copy-start.2
  5.9 0.0 copy-start.7
  5.9 0.0 copy-start.8
  5.9 0.0 copy-start.10
  5.9 0.9 %pack.1 = (f32[5,224,128]{2,1,0:T(8,128)S(1)}, f32[5,96,128]{2,1,0:T(8,128)S(1)}, f32[5,96,128]{2,1,0:T(8,128)S(1)}, f32[5,96,128]{2,1,0:T(8,128)S(1)}, f32[160,128]{1,0:T(8,128)S(1)}) custom-call(f32[5,10,10,640]{3,2,1,0:T(8,128)S(1)} %copy-done, f32[5,5,4,640]{3,2,1,0:T(4,128)S(1)} %bitcast.9, f32[5,5,640]{2,1,0:T(8,128)S(1)} %copy-done.5, ...), custom_call_target="tpu_custom_call" | custom-call | flops 1000000 | bytes 5000000 | tf_op jit(solution)/shard_map/pack/pallas_call | solution.py:633
  6.8 8.7 %collective-permute-start.4 = (f32[5,224,128]{2,1,0:T(8,128)S(1)}, f32[5,224,128]{2,1,0:T(8,128)S(1)}, u32[]{:S(2)}, u32[]{:S(2)}) collective-permute-start(f32[5,224,128]{2,1,0:T(8,128)S(1)} %get-tuple-element.18.back), channel_id=1, source_target_pairs={{0,248},{8,0},{16,8},{24,16},{32,24},{40,32},{48,40},{56,48},{64,5... | collective-permute-start | bytes 1720328 | tf_op jit(solution)/shard_map/ppermute | solution.py:644
  15.5 0.0 collective-permute-start
  15.5 5.7 %collective-permute-start.1 = (f32[5,96,128]{2,1,0:T(8,128)S(1)}, f32[5,96,128]{2,1,0:T(8,128)S(1)}, u32[]{:S(2)}, u32[]{:S(2)}) collective-permute-start(f32[5,96,128]{2,1,0:T(8,128)S(1)} %get-tuple-element.21.high), channel_id=1, source_target_pairs={{0,2},{2,4},{4,6},{1,3},{3,5},{5,7},{8,10},{10,12},{12,14},{9,11},... | collective-permute-start | bytes 737288 | tf_op jit(solution)/shard_map/ppermute | solution.py:647
  21.1 1.9 %collective-permute-start.2 = (f32[5,96,128]{2,1,0:T(8,128)S(1)}, f32[5,96,128]{2,1,0:T(8,128)S(1)}, u32[]{:S(2)}, u32[]{:S(2)}) collective-permute-start(f32[5,96,128]{2,1,0:T(8,128)S(1)} %get-tuple-element.20.low), channel_id=1, source_target_pairs={{2,0},{4,2},{6,4},{3,1},{5,3},{7,5},{10,8},{12,10},{14,12},{11,9},... | collective-permute-start | bytes 737288 | tf_op jit(solution)/shard_map/ppermute | solution.py:646
  23.1 0.7 %collective-permute-start.3 = (f32[160,128]{1,0:T(8,128)S(1)}, f32[160,128]{1,0:T(8,128)S(1)}, u32[]{:S(2)}, u32[]{:S(2)}) collective-permute-start(f32[160,128]{1,0:T(8,128)S(1)} %get-tuple-element.22.axial), channel_id=1, source_target_pairs={{0,1},{1,0},{2,3},{3,2},{4,5},{5,4},{6,7},{7,6},{8,9},{9,8},{10,11... | collective-permute-start | bytes 245768 | tf_op jit(solution)/shard_map/ppermute | solution.py:648
  23.7 0.0 copy-done.11
  23.7 0.0 copy-done.9
  23.7 0.0 copy-done.1
  23.7 0.0 copy-done.2
  23.8 0.0 copy-done.7
  23.8 0.0 copy-done.8
  23.8 0.0 copy-done.10
  23.8 18.4 %interior.1 = (f32[5,10,10,640]{3,2,1,0:T(8,128)}, f32[5,5,4,640]{3,2,1,0:T(4,128)}, bf16[256,1024]{1,0:T(8,128)(2,1)S(1)}, bf16[128,1024]{1,0:T(8,128)(2,1)S(1)}, bf16[128,1024]{1,0:T(8,128)(2,1)S(1)}) custom-call(f32[5,10,10,640]{3,2,1,0:T(8,128)S(1)} %copy-done, f32[5,5,4,640]{3,2,1,0:T(4,128)S(1)} %bitcast.10, f32[5,5,640]{2,1,0:T(8,128)S(1)} %copy-done.5, ...), custom_call_target="tpu_custom_call" | custom-call | flops 5000000000 | bytes 10000000 | tf_op jit(solution)/shard_map/interior/pallas_call | solution.py:650
  42.2 0.0 collective-permute-done.3.axial_in
  42.2 0.0 collective-permute-done.fwd_in
  42.2 0.0 collective-permute-done.1.low_in
  42.2 0.0 collective-permute-done.2.high_in
  42.3 3.8 %faces.1 = (f32[5,10,10,640]{3,2,1,0:T(8,128)}, f32[5,5,4,640]{3,2,1,0:T(4,128)}) custom-call(f32[5,10,10,640]{3,2,1,0:T(8,128)} %get-tuple-element.16.les_in, f32[5,5,4,640]{3,2,1,0:T(4,128)} %get-tuple-element.17.ac_in, f32[5,224,128]{2,1,0:T(8,128)S(1)} %get-tuple-element.18.back, ...), custom_call_target="tpu_custom_call", output_to_operand_aliasing={{0}: (0, {}), {1}: (1, {})} | custom-call | flops 1000000 | bytes 5000000 | tf_op jit(solution)/shard_map/faces/pallas_call | solution.py:681
  46.1 0.0 collective-permute-done.4.back_in
  46.1 5.0 %finish.1 = (f32[5,10,10,640]{3,2,1,0:T(8,128)}, f32[5,5,4,640]{3,2,1,0:T(4,128)}) custom-call(f32[5,10,10,640]{3,2,1,0:T(8,128)} %get-tuple-element.23.les_in, f32[5,5,4,640]{3,2,1,0:T(4,128)} %get-tuple-element.24.ac_in, f32[5,224,128]{2,1,0:T(8,128)S(1)} %collective-permute-done.4.back_in, ...), custom_call_target="tpu_custom_call", output_to_operand_aliasing={{0}: (0, {}), {1}: (1, {})} | custom-call | flops 500000000 | bytes 4000000 | tf_op jit(solution)/shard_map/finish/pallas_call | solution.py:698
Async XLA Ops:
  0.6 23.1 %copy-start.11 = (s32[1,1,1,128]{3,2,1,0:T(1,128)S(1)}, s32[1,1,1,128]{3,2,1,0:T(1,128)}, u32[]{:S(2)}) copy-start(s32[1,1,1,128]{3,2,1,0:T(1,128)} %param.18) | copy-start | bytes 1540
  0.6 23.1 %copy-start.9 = (s32[1,1,1,768]{3,2,1,0:T(1,128)S(1)}, s32[1,1,1,768]{3,2,1,0:T(1,128)}, u32[]{:S(2)}) copy-start(s32[1,1,1,768]{3,2,1,0:T(1,128)} %param.19) | copy-start | bytes 9220
  0.7 1.6 %copy-start = (f32[5,10,10,640]{3,2,1,0:T(8,128)S(1)}, f32[5,10,10,640]{3,2,1,0:T(8,128)}, u32[]{:S(2)}) copy-start(f32[5,10,10,640]{3,2,1,0:T(8,128)} %les.3) | copy-start | bytes 3840004
  2.2 0.9 %copy-start.3 = (f32[4,5,5,640]{3,0,2,1:T(4,128)S(1)}, f32[4,5,5,640]{3,0,2,1:T(4,128)}, u32[]{:S(2)}) copy-start(f32[4,5,5,640]{3,0,2,1:T(4,128)} %param.13) | copy-start | bytes 768004
  3.2 0.9 %copy-start.4 = (f32[3,5,5,640]{3,0,2,1:T(4,128)S(1)}, f32[3,5,5,640]{3,0,2,1:T(4,128)}, u32[]{:S(2)}) copy-start(f32[3,5,5,640]{3,0,2,1:T(4,128)} %param.16) | copy-start | bytes 576004
  4.1 0.9 %copy-start.5 = (f32[5,5,640]{2,1,0:T(8,128)S(1)}, f32[5,5,640]{2,1,0:T(8,128)}, u32[]{:S(2)}) copy-start(f32[5,5,640]{2,1,0:T(8,128)} %den.3) | copy-start | bytes 192004
  5.0 0.9 %copy-start.6 = (f32[5,5,640]{2,1,0:T(8,128)S(1)}, f32[5,5,640]{2,1,0:T(8,128)}, u32[]{:S(2)}) copy-start(f32[5,5,640]{2,1,0:T(8,128)} %snd.3) | copy-start | bytes 192004
  5.9 17.8 %copy-start.1 = (bf16[640,640]{1,0:T(8,128)(2,1)S(1)}, bf16[640,640]{1,0:T(8,128)(2,1)}, u32[]{:S(2)}) copy-start(bf16[640,640]{1,0:T(8,128)(2,1)} %constant.6.clone.perm) | copy-start | bytes 2457604
  5.9 17.8 %copy-start.2 = (bf16[640,640]{1,0:T(8,128)(2,1)S(1)}, bf16[640,640]{1,0:T(8,128)(2,1)}, u32[]{:S(2)}) copy-start(bf16[640,640]{1,0:T(8,128)(2,1)} %constant.7.clone.perm_t) | copy-start | bytes 2457604
  5.9 17.8 %copy-start.7 = (f32[4,5,8,128]{3,2,1,0:T(8,128)S(1)}, f32[4,5,8,128]{3,2,1,0:T(8,128)}, u32[]{:S(2)}) copy-start(f32[4,5,8,128]{3,2,1,0:T(8,128)} %constant.8.clone.coef) | copy-start | bytes 245764
  5.9 17.8 %copy-start.8 = (f32[8,125,125]{2,0,1:T(8,128)S(1)}, f32[8,125,125]{2,0,1:T(8,128)}, u32[]{:S(2)}) copy-start(f32[8,125,125]{2,0,1:T(8,128)} %param.17) | copy-start | bytes 1500004
  5.9 17.8 %copy-start.10 = (s32[1,1,1,768]{3,2,1,0:T(1,128)S(1)}, s32[1,1,1,768]{3,2,1,0:T(1,128)}, u32[]{:S(2)}) copy-start(s32[1,1,1,768]{3,2,1,0:T(1,128)} %param.20) | copy-start | bytes 9220
  6.8 39.3 %collective-permute-start.4 = (f32[5,224,128]{2,1,0:T(8,128)S(1)}, f32[5,224,128]{2,1,0:T(8,128)S(1)}, u32[]{:S(2)}, u32[]{:S(2)}) collective-permute-start(f32[5,224,128]{2,1,0:T(8,128)S(1)} %get-tuple-element.18.back), channel_id=1, source_target_pairs={{0,248},{8,0},{16,8},{24,16},{32,24},{40,32},{48,40},{56,48},{64,5... | collective-permute-start | bytes 1720328 | tf_op jit(solution)/shard_map/ppermute | solution.py:644
  15.5 26.8 %collective-permute-start = (f32[5,96,128]{2,1,0:T(8,128)S(1)}, f32[5,96,128]{2,1,0:T(8,128)S(1)}, u32[]{:S(2)}, u32[]{:S(2)}) collective-permute-start(f32[5,96,128]{2,1,0:T(8,128)S(1)} %get-tuple-element.19.fwd), channel_id=1, source_target_pairs={{0,8},{8,16},{16,24},{24,32},{32,40},{40,48},{48,56},{56,64},{64,7... | collective-permute-start | bytes 737288 | tf_op jit(solution)/shard_map/ppermute | solution.py:645
  15.5 26.8 %collective-permute-start.1 = (f32[5,96,128]{2,1,0:T(8,128)S(1)}, f32[5,96,128]{2,1,0:T(8,128)S(1)}, u32[]{:S(2)}, u32[]{:S(2)}) collective-permute-start(f32[5,96,128]{2,1,0:T(8,128)S(1)} %get-tuple-element.21.high), channel_id=1, source_target_pairs={{0,2},{2,4},{4,6},{1,3},{3,5},{5,7},{8,10},{10,12},{12,14},{9,11},... | collective-permute-start | bytes 737288 | tf_op jit(solution)/shard_map/ppermute | solution.py:647
  21.1 21.1 %collective-permute-start.2 = (f32[5,96,128]{2,1,0:T(8,128)S(1)}, f32[5,96,128]{2,1,0:T(8,128)S(1)}, u32[]{:S(2)}, u32[]{:S(2)}) collective-permute-start(f32[5,96,128]{2,1,0:T(8,128)S(1)} %get-tuple-element.20.low), channel_id=1, source_target_pairs={{2,0},{4,2},{6,4},{3,1},{5,3},{7,5},{10,8},{12,10},{14,12},{11,9},... | collective-permute-start | bytes 737288 | tf_op jit(solution)/shard_map/ppermute | solution.py:646
  23.1 19.2 %collective-permute-start.3 = (f32[160,128]{1,0:T(8,128)S(1)}, f32[160,128]{1,0:T(8,128)S(1)}, u32[]{:S(2)}, u32[]{:S(2)}) collective-permute-start(f32[160,128]{1,0:T(8,128)S(1)} %get-tuple-element.22.axial), channel_id=1, source_target_pairs={{0,1},{1,0},{2,3},{3,2},{4,5},{5,4},{6,7},{7,6},{8,9},{9,8},{10,11... | collective-permute-start | bytes 245768 | tf_op jit(solution)/shard_map/ppermute | solution.py:648

commit v2 on v1

v2 whole, which is shorter than its diff:
```python
import functools
import math

import jax
import jax.numpy as jnp
import numpy as np
from jax import lax
from jax.experimental import pallas as pl
from jax.experimental.pallas import tpu as pltpu
from jax.sharding import PartitionSpec as P

GAMMA = 1.4
DT = 0.05
LIFT = 10.0
F32 = jnp.float32
BF16 = jnp.bfloat16
NX = 640
NE = 128
VMEM_LIMIT = 40 * 1024 * 1024


def derivative_matrix():
    points = np.array([-1.0, -math.sqrt(3.0 / 7.0), 0.0, math.sqrt(3.0 / 7.0), 1.0])
    weights = np.array([1.0 / np.prod([points[j] - points[k] for k in range(5) if k != j]) for j in range(5)])
    matrix = np.zeros((5, 5))
    for i in range(5):
        for j in range(5):
            if i != j:
                matrix[i, j] = weights[j] / weights[i] / (points[i] - points[j])
        matrix[i, i] = -np.sum(matrix[i])
    return matrix


D = derivative_matrix()
T = -D.copy()
T[0, 0] -= LIFT
T[4, 4] += LIFT


def lane_split():
    p = np.zeros((NX, NX), np.float32)
    for e in range(NE):
        for j in range(5):
            p[5 * e + j, NE * j + e] = 1.0
    return p


def radial_coefs():
    inner, outer = T.copy(), T.copy()
    inner[0, 0] += LIFT
    outer[4, 4] -= LIFT
    out = np.zeros((4, 5, 8, 128), np.float32)
    for kind, m in enumerate((inner, outer, D, -D)):
        for k in range(5):
            out[kind, k, :5, :] = m[:, k][:, None]
    return out


def apply5(f, m):
    s = [f[0] + f[4], f[1] + f[3]]
    d = [f[0] - f[4], f[1] - f[3]]
    out = [None] * 5
    for i in range(2):
        even = (0.5 * (m[i, 0] + m[i, 4])) * s[0] + (0.5 * (m[i, 1] + m[i, 3])) * s[1] + m[i, 2] * f[2]
        odd = (0.5 * (m[i, 0] - m[i, 4])) * d[0] + (0.5 * (m[i, 1] - m[i, 3])) * d[1]
        out[i] = odd + even
        out[4 - i] = odd - even
    out[2] = (0.5 * (m[2, 0] - m[2, 4])) * d[0] + (0.5 * (m[2, 1] - m[2, 3])) * d[1]
    return out


def radial(f, coefs):
    total = coefs[0] * f[0:1, :]
    for k in range(1, 5):
        total = total + coefs[k] * f[k : k + 1, :]
    return total


def tile(j):
    return slice(NE * j, NE * j + NE)


def wide(ref):
    return jnp.concatenate([ref[j] for j in range(ref.shape[0])], axis=1)


def split(x):
    hi = x.astype(BF16)
    return hi, (x - hi.astype(F32)).astype(BF16)


def dot(a, b):
    return jnp.dot(a, b, preferred_element_type=F32)


def relane(x, matrix):
    rows = x.shape[0]
    y = dot(jnp.concatenate(split(x), axis=0), matrix)
    return y[:rows] + y[rows:]


def les_prims(q):
    rec = 1.0 / q[0]
    v = [q[1] * rec, q[2] * rec, q[3] * rec]
    p = 0.4 * (q[4] - 0.5 * (q[1] * v[0] + q[2] * v[1] + q[3] * v[2]))
    return rec, v, p


def les_flux(q, v, p, k):
    out = [q[1 + k]]
    for j in range(3):
        out.append(q[1 + j] * v[k] + p if j == k else q[1 + j] * v[k])
    out.append((q[4] + p) * v[k])
    return out


def les_speed(rec, v, p, k):
    return jnp.abs(v[k]) + jnp.sqrt(GAMMA * p * rec)


def common(fl, fr, sl, sr, ql, qr):
    half = 0.5 * jnp.maximum(sl, sr)
    return [0.5 * (fl[n] + fr[n]) - half * (qr[n] - ql[n]) for n in range(len(fl))]


def ape_carried(s):
    return s[6] * s[1] + s[7] * s[2] + s[8] * s[3] + s[0] / s[4]


def ape_leading(s, k):
    return s[5] * s[5] * s[4] * s[1 + k] + s[6 + k] * s[0]


def ape_common(l, r, k, fl=None, fr=None):
    if fl is None:
        fl = (ape_leading(l, k), ape_carried(l))
    if fr is None:
        fr = (ape_leading(r, k), ape_carried(r))
    half = 0.5 * jnp.maximum(jnp.abs(l[6 + k]) + l[5], jnp.abs(r[6 + k]) + r[5])
    out = []
    for n in range(4):
        value = -half * (r[n] - l[n])
        if n == 0:
            value = value + 0.5 * (fl[0] + fr[0])
        elif n == 1 + k:
            value = value + 0.5 * (fl[1] + fr[1])
        out.append(value)
    return out, fl, fr


B_ROWS, F_ROWS, G_ROWS = 224, 96, 160
B_APE = 176
F_APE = 50


def pack_kernel(
    les_h, ac_h, den_h, snd_h, mv_h, back, fwd, low, high, axial, les, ac, den, snd, mv, sems,
):
    copies = [pltpu.make_async_copy(les_h.at[c], les.at[c], sems.at[c]) for c in range(5)]
    for i, (src, dst) in enumerate(((ac_h, ac), (den_h, den), (snd_h, snd), (mv_h, mv))):
        copies.append(pltpu.make_async_copy(src, dst, sems.at[5 + i]))
    for copy in copies:
        copy.start()
    for copy in copies:
        copy.wait()
    for a in range(5):
        rec = 1.0 / les[0, a]
        for c in range(3):
            v = les[1 + c, a] * rec
            for j in range(5):
                back[j, c * 50 + a * 10 : c * 50 + a * 10 + 10, :] = v[:, tile(j)]
    for j in range(5):
        back[j, 150:160, :] = les[0, 0, :, tile(j)]
        back[j, 160:170, :] = les[4, 0, :, tile(j)]
        back[j, 170:176, :] = jnp.zeros((6, 128), F32)
        back[j, 221:224, :] = jnp.zeros((3, 128), F32)
        for buf, a, base in ((back, 0, B_APE), (fwd, 4, F_APE)):
            for r in range(5):
                buf[j, pl.ds(base + r, 4, stride=5), :] = ac[a, r, :, tile(j)]
                buf[j, pl.ds(base + 30 + r, 3, stride=5), :] = mv[a, r, :, tile(j)]
            buf[j, base + 20 : base + 25, :] = den[a, :, tile(j)]
            buf[j, base + 25 : base + 30, :] = snd[a, :, tile(j)]
        for c in range(5):
            fwd[j, c * 10 : c * 10 + 10, :] = les[c, 9, :, tile(j)]
        for buf, r, ra in ((low, 0, 0), (high, 9, 4)):
            for c in range(5):
                for a in range(10):
                    buf[j, c * 10 + a : c * 10 + a + 1, :] = les[c, a, r : r + 1, tile(j)]
            for a in range(5):
                buf[j, pl.ds(F_APE + a, 4, stride=5), :] = ac[a, ra, :, tile(j)]
                buf[j, pl.ds(F_APE + 30 + a, 3, stride=5), :] = mv[a, ra, :, tile(j)]
                buf[j, F_APE + 20 + a : F_APE + 21 + a, :] = den[a, ra : ra + 1, tile(j)]
                buf[j, F_APE + 25 + a : F_APE + 26 + a, :] = snd[a, ra : ra + 1, tile(j)]
        for buf in (fwd, low, high):
            buf[j, 95:96, :] = jnp.zeros((1, 128), F32)
    first = lax.axis_index("group") == 0

    def end(ref, *at):
        return jnp.where(first, ref[(*at, slice(None), slice(NX - 1, NX))], ref[(*at, slice(None), slice(0, 1))])

    def gather(columns, rows):
        lane = lax.broadcasted_iota(jnp.int32, (rows, 128), 1)
        value = jnp.broadcast_to(columns[0], (rows, 128))
        for i in range(1, len(columns)):
            value = jnp.where(lane == i, jnp.broadcast_to(columns[i], (rows, 128)), value)
        return value

    for c in range(5):
        axial[16 * c : 16 * c + 10, :] = gather([end(les, c, a) for a in range(10)], 10)
        axial[16 * c + 10 : 16 * c + 16, :] = jnp.ones((6, 128), F32)
    axial[80:84, :] = gather([end(ac, a, r) for a in range(5) for r in range(5)], 4)
    axial[84:87, :] = gather([end(mv, a, r) for a in range(5) for r in range(5)], 3)
    axial[87:88, :] = jnp.zeros((1, 128), F32)
    axial[88:93, :] = gather([end(den, a) for a in range(5)], 5)
    axial[93:96, :] = jnp.zeros((3, 128), F32)
    axial[96:101, :] = gather([end(snd, a) for a in range(5)], 5)
    axial[101:160, :] = jnp.zeros((59, 128), F32)


ROWS = 768
APE, APE_MV, APE_DEN, APE_SND = 504, 608, 688, 728


def interior_kernel(
    les, ac, den, snd, mv, proj, counts, elem, pattern, perm, coef,
    acc, da, lamb_out, m_out, pp_hi, pp_lo,
    x, y, vel, omega, rt, one_hot, owned, flat,
):
    def list_matrices():
        upper = lax.broadcasted_iota(jnp.int32, (NE, NE), 1)
        lower = lax.broadcasted_iota(jnp.int32, (NE, NE), 0)
        row = jnp.broadcast_to(counts[...], (NE, NE)).astype(F32)
        ends = jnp.sum(jnp.where(upper <= lower, row, 0.0), axis=1, keepdims=True)
        starts = jnp.sum(jnp.where(upper < lower, row, 0.0), axis=1, keepdims=True)
        position = lax.broadcasted_iota(jnp.int32, (NE, 768), 1).astype(F32)
        mine = jnp.where((position >= starts) & (position < ends), jnp.broadcast_to(pattern[...], (NE, 768)), -1)
        for p in range(8):
            owned[p * NE : p * NE + NE, :] = jnp.where(mine == p, 1.0, 0.0).astype(BF16)
        source = jnp.broadcast_to(elem[...], (NE, 768))
        for i in range(6):
            which = lax.broadcasted_iota(jnp.int32, (NE, 768), 0) + i * NE
            one_hot[i * NE : i * NE + NE, :] = jnp.where(which == source, 1.0, 0.0).astype(BF16)
        m_out[...] = lax.dot_general(
            one_hot[...], owned[...], (((1,), (1,)), ((), ())), preferred_element_type=F32
        ).astype(BF16)

    def projection_matrices():
        flat[...] = jnp.zeros((1024, 128), F32)
        flat[0:1000, 0:125] = proj[...]
        for p in range(8):
            hi, lo = split(flat[pl.ds(p, 128, stride=8), :])
            pp_hi[:, tile(p)] = hi
            pp_lo[:, tile(p)] = lo

    def lane_splitting():
        for j in range(5):
            for c in range(5):
                for a in range(10):
                    x[j, c * 100 + a * 10 : c * 100 + a * 10 + 10, :] = les[c, a, :, tile(j)]
            for a in range(5):
                for r in range(5):
                    i = a * 5 + r
                    x[j, APE + 4 * i : APE + 4 * i + 4, :] = ac[a, r, :, tile(j)]
                    x[j, APE_MV + 3 * i : APE_MV + 3 * i + 3, :] = mv[a, r, :, tile(j)]
                x[j, APE_DEN + 8 * a : APE_DEN + 8 * a + 5, :] = den[a, :, tile(j)]
                x[j, APE_SND + 8 * a : APE_SND + 8 * a + 5, :] = snd[a, :, tile(j)]
        value = relane(wide(x), perm[...])
        for j in range(5):
            y[j] = value[:, tile(j)]

    def les_rows_pass():
        lane = lax.broadcasted_iota(jnp.int32, (8, 128), 1)

        @pl.loop(0, 20)
        def _(t):
            er = t // 10
            base = (t - er * 10) * 10 + er * 5
            rows = pl.ds(pl.multiple_of(t * 8, 8), 8)
            q = [[y[j, pl.ds(c * 100 + base, 8), :] for j in range(5)] for c in range(5)]
            rec, v, p = [], [[], [], []], []
            for j in range(5):
                rec_j, v_j, p_j = les_prims([q[c][j] for c in range(5)])
                rec.append(rec_j)
                p.append(p_j)
                for k in range(3):
                    v[k].append(v_j[k])
                    vel[k, j, rows, :] = v_j[k]
                vel[3, j, rows, :] = p_j
            coefs = [coef[er, k] for k in range(5)]
            flux = [les_flux([q[c][j] for c in range(5)], [v[k][j] for k in range(3)], p[j], 2) for j in range(5)]
            s_left = les_speed(rec[4], [v[k][4] for k in range(3)], p[4], 2)
            s_right = pltpu.roll(les_speed(rec[0], [v[k][0] for k in range(3)], p[0], 2), 127, 1)
            half = 0.5 * jnp.maximum(s_left, s_right)
            for n in range(5):
                fr = pltpu.roll(flux[0][n], 127, 1)
                qr = pltpu.roll(q[n][0], 127, 1)
                h = 0.5 * (flux[4][n] + fr) - half * (qr - q[n][4])
                out = apply5([flux[j][n] for j in range(5)], T)
                out[4] = out[4] - LIFT * jnp.where(lane < 127, h, flux[4][n])
                out[0] = out[0] + LIFT * jnp.where(lane > 0, pltpu.roll(h, 1, 1), flux[0][n])
                for j in range(5):
                    f = les_flux([q[c][j] for c in range(5)], [v[k][j] for k in range(3)], p[j], 1)[n]
                    acc[j, pl.ds(n * 100 + base, 5), :] = (out[j] + radial(f, coefs))[0:5]
            dcoefs = [coef[2, k] for k in range(5)]
            d2v0 = apply5(v[0], D)
            d2v1 = apply5(v[1], D)
            for j in range(5):
                omega[0, j, rows, :] = radial(v[2][j], dcoefs) - d2v1[j]
                omega[1, j, rows, :] = d2v0[j]
                omega[2, j, rows, :] = -radial(v[0][j], dcoefs)

    def les_azimuth_pass():
        for c in range(3):
            for i in range(4):
                rt[i, c * 128 + 120 : c * 128 + 128, :] = jnp.zeros((8, 128), F32)

        @pl.loop(0, 2)
        def _(er):
            for j in range(5):
                at = [pl.ds(pl.multiple_of(er * 80 + a * 8, 8), 8) for a in range(10)]
                q = [[y[j, pl.ds(c * 100 + a * 10 + er * 5, 8), :] for a in range(10)] for c in range(5)]
                v = [[vel[k, j, at[a], :] for a in range(10)] for k in range(3)]
                p = [vel[3, j, at[a], :] for a in range(10)]
                flux = [les_flux([q[c][a] for c in range(5)], [v[k][a] for k in range(3)], p[a], 0) for a in range(10)]
                speed = [jnp.abs(v[0][a]) + jnp.sqrt(GAMMA * p[a] / q[0][a]) for a in (4, 5)]
                h = common(flux[4], flux[5], speed[0], speed[1], [q[c][4] for c in range(5)], [q[c][5] for c in range(5)])
                for n in range(5):
                    low = apply5([flux[a][n] for a in range(5)], T)
                    low[0] = low[0] + LIFT * flux[0][n]
                    low[4] = low[4] - LIFT * h[n]
                    top = apply5([flux[5 + a][n] for a in range(5)], T)
                    top[0] = top[0] + LIFT * h[n]
                    top[4] = top[4] - LIFT * flux[9][n]
                    for a, value in enumerate(low + top):
                        to = pl.ds(n * 100 + a * 10 + er * 5, 5)
                        acc[j, to, :] = acc[j, to, :] + value[0:5]
                for ea in range(2):
                    d0v1 = apply5([v[1][5 * ea + i] for i in range(5)], D)
                    d0v2 = apply5([v[2][5 * ea + i] for i in range(5)], D)
                    for i in range(5):
                        a = 5 * ea + i
                        w0 = omega[0, j, at[a], :]
                        w1 = omega[1, j, at[a], :] - d0v2[i]
                        w2 = omega[2, j, at[a], :] + d0v1[i]
                        lamb = [
                            w1 * v[2][a] - w2 * v[1][a],
                            w2 * v[0][a] - w0 * v[2][a],
                            w0 * v[1][a] - w1 * v[0][a],
                        ]
                        for c in range(3):
                            rt[2 * ea + er, pl.ds(c * 128 + i * 25 + j, 5, stride=5), :] = lamb[c][0:5]
        for i in range(4):
            hi, lo = split(rt[i])
            lamb_out[0:384, tile(i)] = hi
            lamb_out[384:768, tile(i)] = lo

    def les_radial_face():
        for j in range(5):
            left = [pl.ds(c * 100 + 4, 10, stride=10) for c in range(5)]
            right = [pl.ds(c * 100 + 5, 10, stride=10) for c in range(5)]
            h, _, _ = les_common([y[j, at, :] for at in left], [y[j, at, :] for at in right], 1)
            for n in range(5):
                acc[j, left[n], :] = acc[j, left[n], :] - LIFT * h[n]
                acc[j, right[n], :] = acc[j, right[n], :] + LIFT * h[n]
            acc[j, 500:512, :] = jnp.zeros((12, 128), F32)

    def acoustic():
        lane5 = lax.broadcasted_iota(jnp.int32, (5, 128), 1)
        state = [[None] * 5 for _ in range(5)]
        for a in range(5):
            for j in range(5):
                state[a][j] = (
                    [y[j, pl.ds(APE + a * 20 + c, 5, stride=4), :] for c in range(4)]
                    + [y[j, base + a * 8 : base + a * 8 + 5, :] for base in (APE_DEN, APE_SND)]
                    + [y[j, pl.ds(APE_MV + a * 15 + k, 5, stride=3), :] for k in range(3)]
                )
        carried = [[ape_carried(state[a][j]) for j in range(5)] for a in range(5)]
        lead = [[[ape_leading(state[a][j], k) for j in range(5)] for a in range(5)] for k in range(3)]
        total = [[[None] * 5 for _ in range(5)] for _ in range(4)]
        minus = -D
        mcoefs = [coef[3, k, 0:5] for k in range(5)]
        for j in range(5):
            first = apply5([lead[0][a][j] for a in range(5)], minus)
            other = apply5([carried[a][j] for a in range(5)], minus)
            for a in range(5):
                total[0][a][j] = first[a] + radial(lead[1][a][j], mcoefs)
                total[1][a][j] = other[a]
                total[2][a][j] = radial(carried[a][j], mcoefs)
        for a in range(5):
            first = apply5(lead[2][a], T)
            other = apply5(carried[a], T)
            shift = [pltpu.roll(jnp.pad(v, ((0, 3), (0, 0))), 127, 1)[0:5] for v in state[a][0]]
            h, fl, fr = ape_common(state[a][4], shift, 2)
            for n in range(4):
                own4 = lead[2][a][4] if n == 0 else carried[a][4] if n == 3 else jnp.zeros_like(carried[a][4])
                own0 = lead[2][a][0] if n == 0 else carried[a][0] if n == 3 else jnp.zeros_like(carried[a][0])
                back = pltpu.roll(jnp.pad(h[n], ((0, 3), (0, 0))), 1, 1)[0:5]
                lift4 = -LIFT * jnp.where(lane5 < 127, h[n], own4)
                lift0 = LIFT * jnp.where(lane5 > 0, back, own0)
                for j in range(5):
                    value = total[n][a][j]
                    if n in (0, 3):
                        extra = first[j] if n == 0 else other[j]
                        value = extra if value is None else value + extra
                    if j == 4:
                        value = value + lift4
                    if j == 0:
                        value = value + lift0
                    if value is None:
                        value = jnp.zeros((5, 128), F32)
                    da[j, pl.ds(a * 20 + n, 5, stride=4), :] = value
        for j in range(5):
            da[j, 100:104, :] = jnp.zeros((4, 128), F32)

    for part in (
        list_matrices, projection_matrices, lane_splitting, les_rows_pass, les_azimuth_pass, les_radial_face, acoustic,
    ):
        part()


def ape_face(buf, base, j):
    return [buf[j, base + 5 * n : base + 5 * n + 5, :] for n in range(9)]


def back_face(buf, j):
    rho = buf[j, 150:160, :]
    return [rho] + [rho * buf[j, c * 50 : c * 50 + 10, :] for c in range(3)] + [buf[j, 160:170, :]]


def les_rows(buf, j):
    return [buf[j, c * 10 : c * 10 + 10, :] for c in range(5)]


def les_common(ql, qr, k):
    rl, vl, pl_ = les_prims(ql)
    rr, vr, pr = les_prims(qr)
    fl, fr = les_flux(ql, vl, pl_, k), les_flux(qr, vr, pr, k)
    return common(fl, fr, les_speed(rl, vl, pl_, k), les_speed(rr, vr, pr, k), ql, qr), fl, fr


def finish_kernel(
    les, ac, acc, da_in, lamb_own, m, pp_hi, pp_lo, back, fwd, low, high, axial,
    fwd_in, low_in, high_in, axial_in, back_in, perm, perm_t, coef,
    les_out, ac_out, delta, result, yn, rt, rhs_hi, rhs_lo, osc, da, sem,
):
    rad = lax.axis_index("rad")
    first_half = lax.axis_index("group") == 0
    at_low, at_high = rad == 0, rad == lax.axis_size("rad") - 1

    def les_faces():
        value = relane(wide(acc), perm_t[...])
        for j in range(5):
            delta[j] = value[:, tile(j)]
        for j in range(5):
            own_low, own_high = les_rows(low, j), les_rows(high, j)
            nbr_low = [jnp.where(at_low, o, n) for o, n in zip(own_low, les_rows(low_in, j))]
            nbr_high = [jnp.where(at_high, o, n) for o, n in zip(own_high, les_rows(high_in, j))]
            h, _, fr = les_common(nbr_low, own_low, 1)
            g, fl, _ = les_common(own_high, nbr_high, 1)
            for n in range(5):
                at = pl.ds(n * 100, 10, stride=10)
                delta[j, at, :] = delta[j, at, :] + LIFT * (h[n] - fr[n])
                at = pl.ds(n * 100 + 9, 10, stride=10)
                delta[j, at, :] = delta[j, at, :] + LIFT * (fl[n] - g[n])
            h, _, fr = les_common(les_rows(fwd_in, j), back_face(back, j), 0)
            g, fl, _ = les_common(les_rows(fwd, j), back_face(back_in, j), 0)
            for n in range(5):
                at = slice(n * 100, n * 100 + 10)
                delta[j, at, :] = delta[j, at, :] + LIFT * (h[n] - fr[n])
                at = slice(n * 100 + 90, n * 100 + 100)
                delta[j, at, :] = delta[j, at, :] + LIFT * (fl[n] - g[n])
        own = [axial[16 * c : 16 * c + 16, :] for c in range(5)]
        nbr = [axial_in[16 * c : 16 * c + 16, :] for c in range(5)]
        ql = [jnp.where(first_half, o, n) for o, n in zip(own, nbr)]
        qr = [jnp.where(first_half, n, o) for o, n in zip(own, nbr)]
        h, fl, fr = les_common(ql, qr, 2)
        lane = lax.broadcasted_iota(jnp.int32, (10, 128), 1)
        on_last = (lane == 127) & first_half
        on_first = (lane == 0) & jnp.logical_not(first_half)
        for n in range(5):
            axis = LIFT * jnp.where(first_half, fl[n] - h[n], h[n] - fr[n])
            for a in range(10):
                column = jnp.broadcast_to(axis[0:10, a : a + 1], (10, 128))
                at = slice(n * 100 + a * 10, n * 100 + a * 10 + 10)
                for j in range(5):
                    value = delta[j, at, :]
                    if j == 0:
                        value = value + jnp.where(on_first, column, 0.0)
                    if j == 4:
                        value = value + jnp.where(on_last, column, 0.0)
                    result[n, a, :, tile(j)] = les[n, a, :, tile(j)] + DT * value
        pltpu.make_async_copy(result, les_out, sem).start()

    def sources():
        value = relane(jnp.concatenate([back_in[j, 0:160, :] for j in range(5)], axis=1), perm[...])
        for j in range(5):
            yn[j] = value[:, tile(j)]
        for c in range(3):
            for i in range(2):
                rt[i, c * 128 + 120 : c * 128 + 128, :] = jnp.zeros((8, 128), F32)
        dcoefs = [coef[2, k] for k in range(5)]
        for er in range(2):
            v = [[[None] * 5 for _ in range(5)] for _ in range(3)]
            for c in range(3):
                for a in range(5):
                    at = c * 50 + a * 10 + er * 5
                    v[c][a] = [yn[j, at : at + 8, :] for j in range(5)]
            d2v0 = [apply5(v[0][a], D) for a in range(5)]
            d2v1 = [apply5(v[1][a], D) for a in range(5)]
            for j in range(5):
                d0v1 = apply5([v[1][a][j] for a in range(5)], D)
                d0v2 = apply5([v[2][a][j] for a in range(5)], D)
                for a in range(5):
                    w0 = radial(v[2][a][j], dcoefs) - d2v1[a][j]
                    w1 = d2v0[a][j] - d0v2[a]
                    w2 = d0v1[a] - radial(v[0][a][j], dcoefs)
                    lamb = [
                        w1 * v[2][a][j] - w2 * v[1][a][j],
                        w2 * v[0][a][j] - w0 * v[2][a][j],
                        w0 * v[1][a][j] - w1 * v[0][a][j],
                    ]
                    for c in range(3):
                        rt[er, pl.ds(c * 128 + a * 25 + j, 5, stride=5), :] = lamb[c][0:5]
        near = jnp.concatenate(split(wide(rt)), axis=0)
        s = dot(jnp.concatenate([lamb_own[...], near], axis=1), m[...])
        s = s[0:384] + s[384:768]
        for p in range(8):
            for c in range(3):
                hi, lo = split(s[c * 128 : c * 128 + 128, tile(p)])
                rhs_hi[p * 128 : p * 128 + 128, tile(c)] = hi
                rhs_lo[p * 128 : p * 128 + 128, tile(c)] = lo
        hi = rhs_hi[...]
        out = dot(pp_hi[...], hi) + (dot(pp_lo[...], hi) + dot(pp_hi[...], rhs_lo[...]))
        for c in range(3):
            osc[c] = out[:, tile(c)]

    def acoustic():
        for j in range(5):
            da[j] = da_in[j]
            for a in range(5):
                for n in range(1, 4):
                    at = pl.ds(a * 20 + n, 5, stride=4)
                    da[j, at, :] = da[j, at, :] - osc[n - 1, pl.ds(a * 25 + j, 5, stride=5), :]
        value = relane(wide(da), perm_t[...])

        def axial_state(buf):
            def spread(base):
                rows = buf[base : base + 8, :]
                row = lax.broadcasted_iota(jnp.int32, (8, 128), 0)
                lanes = lax.broadcasted_iota(jnp.int32, (8, 128), 1)
                out = jnp.zeros((8, 128), F32)
                for a in range(5):
                    here = (lanes == a * 5 + row) & (row < 5)
                    out = jnp.where(here, jnp.broadcast_to(rows[:, a : a + 1], (8, 128)), out)
                return jnp.sum(out, axis=0, keepdims=True)

            used = lax.broadcasted_iota(jnp.int32, (1, 128), 1) < 25
            return (
                [buf[80 + c : 81 + c, :] for c in range(4)]
                + [jnp.where(used, spread(88), 1.0), spread(96)]
                + [buf[84 + k : 85 + k, :] for k in range(3)]
            )

        own, nbr = axial_state(axial), axial_state(axial_in)
        ql = [jnp.where(first_half, o, n) for o, n in zip(own, nbr)]
        qr = [jnp.where(first_half, n, o) for o, n in zip(own, nbr)]
        h, fl, fr = ape_common(ql, qr, 2)
        rows = []
        for n in range(4):
            fl_n = fl[0] if n == 0 else fl[1] if n == 3 else 0.0
            fr_n = fr[0] if n == 0 else fr[1] if n == 3 else 0.0
            rows.append(LIFT * jnp.where(first_half, fl_n - h[n], h[n] - fr_n))
        axis = jnp.concatenate(rows, axis=0)
        lane4 = lax.broadcasted_iota(jnp.int32, (4, 128), 1)
        on_last = (lane4 == 127) & first_half
        on_first = (lane4 == 0) & jnp.logical_not(first_half)
        for j in range(5):
            da[j] = value[:, tile(j)]

            def add(start, stride, h, own, k, sign):
                for n in range(4):
                    own_n = own[0] if n == 0 else own[1] if n == 1 + k else 0.0
                    at = pl.ds(start + n, 5, stride=stride)
                    da[j, at, :] = da[j, at, :] + sign * LIFT * (h[n] - own_n)

            h, _, fr = ape_common(ape_face(fwd_in, F_APE, j), ape_face(back, B_APE, j), 0)
            add(0, 4, h, fr, 0, 1.0)
            h, fl, _ = ape_common(ape_face(fwd, F_APE, j), ape_face(back_in, B_APE, j), 0)
            add(80, 4, h, fl, 0, -1.0)
            own_l, own_h = ape_face(low, F_APE, j), ape_face(high, F_APE, j)
            nbr_l = [jnp.where(at_low, o, n) for o, n in zip(own_l, ape_face(low_in, F_APE, j))]
            nbr_h = [jnp.where(at_high, o, n) for o, n in zip(own_h, ape_face(high_in, F_APE, j))]
            h, _, fr = ape_common(nbr_l, own_l, 1)
            add(0, 20, h, fr, 1, 1.0)
            h, fl, _ = ape_common(own_h, nbr_h, 1)
            add(16, 20, h, fl, 1, -1.0)
            for a in range(5):
                for r in range(5):
                    i = a * 5 + r
                    change = da[j, 4 * i : 4 * i + 4, :]
                    if j == 0 or j == 4:
                        column = jnp.broadcast_to(axis[:, i : i + 1], (4, 128))
                        change = change + jnp.where(on_last if j == 4 else on_first, column, 0.0)
                    ac_out[a, r, :, tile(j)] = ac[a, r, :, tile(j)] + DT * change

    les_faces()
    sources()
    acoustic()
    pltpu.make_async_copy(result, les_out, sem).wait()


def shape(*dims, dtype=F32):
    return jax.ShapeDtypeStruct(dims, dtype)


def cost(flops, size):
    return pl.CostEstimate(flops=flops, bytes_accessed=size, transcendentals=0)


def params():
    return pltpu.CompilerParams(vmem_limit_bytes=VMEM_LIMIT)


def body(les, ac, den, snd, mv, proj, counts, elem, pattern):
    vmem = pl.BlockSpec(memory_space=pltpu.VMEM)
    ac = jnp.transpose(ac, (1, 2, 0, 3))
    mv = jnp.transpose(mv, (1, 2, 0, 3))
    proj = jnp.transpose(proj, (1, 0, 2)).reshape(1000, 125)
    counts, elem, pattern = counts.reshape(1, 128), elem.reshape(1, 768), pattern.reshape(1, 768)
    perm = jnp.asarray(lane_split(), BF16)
    perm_t = jnp.asarray(lane_split().T, BF16)
    coef = jnp.asarray(radial_coefs(), F32)

    hbm = pl.BlockSpec(memory_space=pltpu.HBM)
    held = [pltpu.VMEM(a.shape, F32) for a in (les, ac, den, snd, mv)]
    back, fwd, low, high, axial, les, ac, den, snd, mv = pl.pallas_call(
        pack_kernel,
        out_shape=[pltpu.VMEM((5, n, 128), F32) for n in (B_ROWS, F_ROWS, F_ROWS, F_ROWS)]
        + [pltpu.VMEM((G_ROWS, 128), F32)]
        + held,
        in_specs=[hbm] * 5,
        out_specs=[vmem] * 10,
        scratch_shapes=[pltpu.SemaphoreType.DMA((9,))],
        compiler_params=params(),
        cost_estimate=cost(1_000_000, 5_000_000),
        name="pack",
    )(*[pltpu.with_memory_space_constraint(a, pltpu.HBM) for a in (les, ac, den, snd, mv)])

    azim, radc = lax.axis_size("azim"), lax.axis_size("rad")
    back_in = lax.ppermute(back, "azim", [(i, (i - 1) % azim) for i in range(azim)])
    fwd_in = lax.ppermute(fwd, "azim", [(i, (i + 1) % azim) for i in range(azim)])
    high_in = lax.ppermute(low, "rad", [(i, i - 1) for i in range(1, radc)])
    low_in = lax.ppermute(high, "rad", [(i, i + 1) for i in range(radc - 1)])
    axial_in = lax.ppermute(axial, "group", [(0, 1), (1, 0)])

    acc, da, lamb, m, pp_hi, pp_lo = pl.pallas_call(
        interior_kernel,
        out_shape=[
            shape(5, 512, 128), shape(5, 104, 128), shape(768, 512, dtype=BF16), shape(768, 1024, dtype=BF16),
            shape(128, 1024, dtype=BF16), shape(128, 1024, dtype=BF16),
        ],
        in_specs=[vmem] * 11,
        out_specs=[vmem] * 6,
        scratch_shapes=[
            pltpu.VMEM((5, ROWS, 128), F32),
            pltpu.VMEM((5, ROWS, 128), F32),
            pltpu.VMEM((4, 5, 160, 128), F32),
            pltpu.VMEM((3, 5, 160, 128), F32),
            pltpu.VMEM((4, 384, 128), F32),
            pltpu.VMEM((768, 768), BF16),
            pltpu.VMEM((1024, 768), BF16),
            pltpu.VMEM((1024, 128), F32),
        ],
        compiler_params=params(),
        cost_estimate=cost(5_000_000_000, 10_000_000),
        name="interior",
    )(les, ac, den, snd, mv, proj, counts, elem, pattern, perm, coef)

    les_next, ac_next = pl.pallas_call(
        finish_kernel,
        out_shape=[shape(5, 10, 10, NX), shape(5, 5, 4, NX)],
        in_specs=[vmem] * 21,
        out_specs=[hbm, vmem],
        scratch_shapes=[
            pltpu.VMEM((5, 512, 128), F32),
            pltpu.VMEM((5, 10, 10, NX), F32),
            pltpu.VMEM((5, 160, 128), F32),
            pltpu.VMEM((2, 384, 128), F32),
            pltpu.VMEM((1024, 384), BF16),
            pltpu.VMEM((1024, 384), BF16),
            pltpu.VMEM((3, 128, 128), F32),
            pltpu.VMEM((5, 104, 128), F32),
            pltpu.SemaphoreType.DMA(()),
        ],
        compiler_params=params(),
        cost_estimate=cost(500_000_000, 4_000_000),
        name="finish",
    )(
        les, ac, acc, da, lamb, m, pp_hi, pp_lo, back, fwd, low, high, axial,
        fwd_in, low_in, high_in, axial_in, back_in, perm, perm_t, coef,
    )
    return les_next, jnp.transpose(ac_next, (2, 0, 1, 3))


def solution(mesh):
    field = P(None, "azim", "rad", "group")
    node = P("azim", "rad", "group")
    lists = P("azim", "rad", "group", None)
    return jax.shard_map(
        body,
        mesh=mesh,
        in_specs=(field, field, node, node, field, P(), lists, lists, lists),
        out_specs=(field, field),
        check_vma=False,
    )
```

time: 51.5 us -> 35.6 us (0.69)
  Pallas kernels: 28.2 us -> 17.1 us
  local copies, waits for them, and re-layouts: 5.29 us -> 0.04 us
  starting transfers between devices: 16.9 us -> 17.5 us
    pallas_call x4 -> x3, Pallas kernels: 28.2 us -> 17.1 us  [the longest x1 8.55 us: body(): pl.pallas_call(interior_kernel, out_shape=[shape(5, 512, 128), shape(5, 1...]
    unnamed x24 -> x14, local copies, waits for them, and re-layouts: 5.29 us -> 0.04 us
    ppermute x1, starting transfers between devices: 5.65 us -> 4.43 us  [body(): low_in = lax.ppermute(high, 'rad', [(i, i + 1) for i in range(radc - 1)])]
    ppermute x1, starting transfers between devices: 1.92 us -> 3.13 us  [body(): high_in = lax.ppermute(low, 'rad', [(i, i - 1) for i in range(1, radc)])]
    ppermute x1, starting transfers between devices: 0.66 us -> 1.3 us  [body(): axial_in = lax.ppermute(axial, 'group', [(0, 1), (1, 0)])]
  transfers between devices with their start and end apart: 5 -> 5, of which waited for: 0 -> 0; matrix products, arithmetic and copies ran while one was open for 0% -> 0% of each run, Pallas kernels for 44% -> 24%
where the time goes in v2:
time: 35.6 us; the launch traced here: 35.5 us
  starting transfers between devices  17.5 us (49%)
  Pallas kernels  17.1 us (48%)
  between operations  0.82 us (2%)
    ppermute x1, starting transfers between devices, body(): lax.ppermute(back, 'azim', [(i, (i - 1) % azim) for i in range(azim)])  8.68 us
    pallas_call x1, Pallas kernels, body(): pl.pallas_call(interior_kernel, out_shape=[shape(5, 512, 128), shape(5, 1...  8.55 us
    pallas_call x1, Pallas kernels, body(): pl.pallas_call(finish_kernel, out_shape=[shape(5, 10, 10, NX), shape(5, 5...  5.53 us
    ppermute x1, starting transfers between devices, body(): low_in = lax.ppermute(high, 'rad', [(i, i + 1) for i in range(radc - 1)])  4.43 us
    ppermute x1, starting transfers between devices, body(): high_in = lax.ppermute(low, 'rad', [(i, i - 1) for i in range(1, radc)])  3.13 us
    pallas_call x1, Pallas kernels, body(): pl.pallas_call(pack_kernel, out_shape=[pltpu.VMEM((5, n, 128), F32) for n...  2.98 us
    ppermute x1, starting transfers between devices, body(): axial_in = lax.ppermute(axial, 'group', [(0, 1), (1, 0)])  1.3 us
  transfers between devices with their start and end apart: 5, of which 0 were waited for; matrix products, arithmetic and copies ran while one was open for 0% of the time, Pallas kernels for 24%

profile of v2, /device:TPU:1, one launch (start us, length us, event | category | flops | bytes accessed | tf_op | source)
XLA Modules:
  0.0 35.5 jit_solution(13244514718869535205)
XLA Ops:
  0.6 0.0 copy-start.2
  0.6 0.0 copy-start
  0.7 0.0 copy-start.5
  0.7 0.0 copy-start.4
  0.7 0.0 copy-start.6
  0.7 0.0 copy-start.3
  0.7 3.0 %pack.1 = (f32[5,224,128]{2,1,0:T(8,128)S(1)}, f32[5,96,128]{2,1,0:T(8,128)S(1)}, f32[5,96,128]{2,1,0:T(8,128)S(1)}, f32[5,96,128]{2,1,0:T(8,128)S(1)}, f32[160,...) custom-call(f32[5,10,10,640]{3,2,1,0:T(8,128)} %les_h.1, ...), custom_call_target="tpu_custom_call" | custom-call | flops 1000000 | bytes 5000000 | tf_op jit(solution)/shard_map/pack/pallas_call | solution.py:636
  3.7 8.7 %collective-permute-start.4 = (f32[5,224,128]{2,1,0:T(8,128)S(1)}, f32[5,224,128]{2,1,0:T(8,128)S(1)}, u32[]{:S(2)}, u32[]{:S(2)}) collective-permute-start(f32[5,224,128]{2,1,0:T(8,128)S(1)} %get-tuple-element.31.back), channel_id=1, source_target_pairs={{0,248},{8,0},{16,8},{24,16},{32,24},{40,32},{48,40},{56,48},{64,5... | collective-permute-start | bytes 1720328 | tf_op jit(solution)/shard_map/ppermute | solution.py:650
  12.4 1.3 %collective-permute-start.3 = (f32[160,128]{1,0:T(8,128)S(1)}, f32[160,128]{1,0:T(8,128)S(1)}, u32[]{:S(2)}, u32[]{:S(2)}) collective-permute-start(f32[160,128]{1,0:T(8,128)S(1)} %get-tuple-element.35.axial), channel_id=1, source_target_pairs={{0,1},{1,0},{2,3},{3,2},{4,5},{5,4},{6,7},{7,6},{8,9},{9,8},{10,11... | collective-permute-start | bytes 245768 | tf_op jit(solution)/shard_map/ppermute | solution.py:654
  13.7 0.0 collective-permute-start
  13.7 3.1 %collective-permute-start.2 = (f32[5,96,128]{2,1,0:T(8,128)S(1)}, f32[5,96,128]{2,1,0:T(8,128)S(1)}, u32[]{:S(2)}, u32[]{:S(2)}) collective-permute-start(f32[5,96,128]{2,1,0:T(8,128)S(1)} %get-tuple-element.33.low), channel_id=1, source_target_pairs={{2,0},{4,2},{6,4},{3,1},{5,3},{7,5},{10,8},{12,10},{14,12},{11,9},... | collective-permute-start | bytes 737288 | tf_op jit(solution)/shard_map/ppermute | solution.py:652
  16.8 4.4 %collective-permute-start.1 = (f32[5,96,128]{2,1,0:T(8,128)S(1)}, f32[5,96,128]{2,1,0:T(8,128)S(1)}, u32[]{:S(2)}, u32[]{:S(2)}) collective-permute-start(f32[5,96,128]{2,1,0:T(8,128)S(1)} %get-tuple-element.34.high), channel_id=1, source_target_pairs={{0,2},{2,4},{4,6},{1,3},{3,5},{5,7},{8,10},{10,12},{12,14},{9,11},... | collective-permute-start | bytes 737288 | tf_op jit(solution)/shard_map/ppermute | solution.py:653
  21.2 0.0 copy-done.2
  21.2 0.0 copy-done
  21.3 0.0 copy-done.5
  21.3 0.0 copy-done.4
  21.3 0.0 copy-done.6
  21.3 0.0 copy-done.3
  21.3 0.0 copy-start.1
  21.3 8.5 %interior.1 = (f32[5,512,128]{2,1,0:T(8,128)S(1)}, f32[5,104,128]{2,1,0:T(8,128)S(1)}, bf16[768,512]{1,0:T(8,128)(2,1)S(1)}, bf16[768,1024]{1,0:T(8,128)(2,1)S(1...) custom-call(f32[5,10,10,640]{3,2,1,0:T(8,128)S(1)} %get-tuple-element.20.les, ...), custom_call_target="tpu_custom_call" | custom-call | flops 5000000000 | bytes 10000000 | tf_op jit(solution)/shard_map/interior/pallas_call | solution.py:656
  29.9 0.0 collective-permute-done.3.axial_in
  29.9 0.0 collective-permute-done.fwd_in
  29.9 0.0 collective-permute-done.2.high_in
  29.9 0.0 collective-permute-done.1.low_in
  29.9 0.0 collective-permute-done.4.back_in
  29.9 0.0 copy-done.1
  29.9 5.5 %finish.1 = (f32[5,10,10,640]{3,2,1,0:T(8,128)}, f32[5,5,4,640]{3,2,1,0:T(4,128)}) custom-call(f32[5,10,10,640]{3,2,1,0:T(8,128)S(1)} %get-tuple-element.20.les, f32[5,5,4,640]{3,2,1,0:T(4,128)S(1)} %get-tuple-element.21.ac, f32[5,512,128]{2,1,0:T(8,128)S(1)} %get-tuple-element.25.acc, f32[5,104,128]{2,1,0:T(8,128)S(1)} %get-tuple-element.26.da_in, ...), custom_call_target="tpu_custom_call" | custom-call | flops 500000000 | bytes 4000000 | tf_op jit(solution)/shard_map/finish/pallas_call | solution.py:679
Async XLA Ops:
  0.6 20.6 %copy-start.2 = (f32[4,5,8,128]{3,2,1,0:T(8,128)S(1)}, f32[4,5,8,128]{3,2,1,0:T(8,128)}, u32[]{:S(2)}) copy-start(f32[4,5,8,128]{3,2,1,0:T(8,128)} %constant.8.clone.coef) | copy-start | bytes 245764
  0.6 20.6 %copy-start = (bf16[640,640]{1,0:T(8,128)(2,1)S(1)}, bf16[640,640]{1,0:T(8,128)(2,1)}, u32[]{:S(2)}) copy-start(bf16[640,640]{1,0:T(8,128)(2,1)} %constant.6.clone.perm) | copy-start | bytes 2457604
  0.7 20.6 %copy-start.5 = (s32[1,1,1,768]{3,2,1,0:T(1,128)S(1)}, s32[1,1,1,768]{3,2,1,0:T(1,128)}, u32[]{:S(2)}) copy-start(s32[1,1,1,768]{3,2,1,0:T(1,128)} %param.20) | copy-start | bytes 9220
  0.7 20.6 %copy-start.4 = (s32[1,1,1,768]{3,2,1,0:T(1,128)S(1)}, s32[1,1,1,768]{3,2,1,0:T(1,128)}, u32[]{:S(2)}) copy-start(s32[1,1,1,768]{3,2,1,0:T(1,128)} %param.19) | copy-start | bytes 9220
  0.7 20.6 %copy-start.6 = (s32[1,1,1,128]{3,2,1,0:T(1,128)S(1)}, s32[1,1,1,128]{3,2,1,0:T(1,128)}, u32[]{:S(2)}) copy-start(s32[1,1,1,128]{3,2,1,0:T(1,128)} %param.18) | copy-start | bytes 1540
  0.7 20.6 %copy-start.3 = (f32[8,125,125]{2,0,1:T(8,128)S(1)}, f32[8,125,125]{2,0,1:T(8,128)}, u32[]{:S(2)}) copy-start(f32[8,125,125]{2,0,1:T(8,128)} %param.17) | copy-start | bytes 1500004
  3.7 26.2 %collective-permute-start.4 = (f32[5,224,128]{2,1,0:T(8,128)S(1)}, f32[5,224,128]{2,1,0:T(8,128)S(1)}, u32[]{:S(2)}, u32[]{:S(2)}) collective-permute-start(f32[5,224,128]{2,1,0:T(8,128)S(1)} %get-tuple-element.31.back), channel_id=1, source_target_pairs={{0,248},{8,0},{16,8},{24,16},{32,24},{40,32},{48,40},{56,48},{64,5... | collective-permute-start | bytes 1720328 | tf_op jit(solution)/shard_map/ppermute | solution.py:650
  12.4 17.5 %collective-permute-start.3 = (f32[160,128]{1,0:T(8,128)S(1)}, f32[160,128]{1,0:T(8,128)S(1)}, u32[]{:S(2)}, u32[]{:S(2)}) collective-permute-start(f32[160,128]{1,0:T(8,128)S(1)} %get-tuple-element.35.axial), channel_id=1, source_target_pairs={{0,1},{1,0},{2,3},{3,2},{4,5},{5,4},{6,7},{7,6},{8,9},{9,8},{10,11... | collective-permute-start | bytes 245768 | tf_op jit(solution)/shard_map/ppermute | solution.py:654
  13.7 16.2 %collective-permute-start = (f32[5,96,128]{2,1,0:T(8,128)S(1)}, f32[5,96,128]{2,1,0:T(8,128)S(1)}, u32[]{:S(2)}, u32[]{:S(2)}) collective-permute-start(f32[5,96,128]{2,1,0:T(8,128)S(1)} %get-tuple-element.32.fwd), channel_id=1, source_target_pairs={{0,8},{8,16},{16,24},{24,32},{32,40},{40,48},{48,56},{56,64},{64,7... | collective-permute-start | bytes 737288 | tf_op jit(solution)/shard_map/ppermute | solution.py:651
  13.7 16.2 %collective-permute-start.2 = (f32[5,96,128]{2,1,0:T(8,128)S(1)}, f32[5,96,128]{2,1,0:T(8,128)S(1)}, u32[]{:S(2)}, u32[]{:S(2)}) collective-permute-start(f32[5,96,128]{2,1,0:T(8,128)S(1)} %get-tuple-element.33.low), channel_id=1, source_target_pairs={{2,0},{4,2},{6,4},{3,1},{5,3},{7,5},{10,8},{12,10},{14,12},{11,9},... | collective-permute-start | bytes 737288 | tf_op jit(solution)/shard_map/ppermute | solution.py:652
  16.8 13.1 %collective-permute-start.1 = (f32[5,96,128]{2,1,0:T(8,128)S(1)}, f32[5,96,128]{2,1,0:T(8,128)S(1)}, u32[]{:S(2)}, u32[]{:S(2)}) collective-permute-start(f32[5,96,128]{2,1,0:T(8,128)S(1)} %get-tuple-element.34.high), channel_id=1, source_target_pairs={{0,2},{2,4},{4,6},{1,3},{3,5},{5,7},{8,10},{10,12},{12,14},{9,11},... | collective-permute-start | bytes 737288 | tf_op jit(solution)/shard_map/ppermute | solution.py:653
  21.3 8.6 %copy-start.1 = (bf16[640,640]{1,0:T(8,128)(2,1)S(1)}, bf16[640,640]{1,0:T(8,128)(2,1)}, u32[]{:S(2)}) copy-start(bf16[640,640]{1,0:T(8,128)(2,1)} %constant.7.clone.perm_t) | copy-start | bytes 2457604

commit v3 on v2

--- a/solution.py
+++ b/solution.py
@@ -94,9 +94,7 @@
 
 
 def relane(x, matrix):
-    rows = x.shape[0]
-    y = dot(jnp.concatenate(split(x), axis=0), matrix)
-    return y[:rows] + y[rows:]
+    return dot(jnp.concatenate(split(x), axis=1), matrix)
 
 
 def les_prims(q):
@@ -154,14 +152,29 @@
 
 
 def pack_kernel(
-    les_h, ac_h, den_h, snd_h, mv_h, back, fwd, low, high, axial, les, ac, den, snd, mv, sems,
+    les_h, ac_h, den_h, snd_h, mv_h, back, fwd, inner, outer, axial, les, ac, den, snd, mv, sems,
 ):
-    copies = [pltpu.make_async_copy(les_h.at[c], les.at[c], sems.at[c]) for c in range(5)]
+    halves = [slice(0, 5), slice(5, 10)]
+    copies = [[], [], []]
+    for h in range(2):
+        for c in range(5):
+            copies[h].append(pltpu.make_async_copy(les_h.at[c, halves[h]], les.at[c, halves[h]], sems.at[5 * h + c]))
     for i, (src, dst) in enumerate(((ac_h, ac), (den_h, den), (snd_h, snd), (mv_h, mv))):
-        copies.append(pltpu.make_async_copy(src, dst, sems.at[5 + i]))
-    for copy in copies:
-        copy.start()
-    for copy in copies:
+        copies[2].append(pltpu.make_async_copy(src, dst, sems.at[10 + i]))
+    for group in (0, 2, 1):
+        for copy in copies[group]:
+            copy.start()
+    even = lax.rem(lax.axis_index("rad"), 2) == 0
+
+    def radial_faces(layers):
+        for j in range(5):
+            for c in range(5):
+                for a in layers:
+                    first, last = les[c, a, 0:1, tile(j)], les[c, a, 9:10, tile(j)]
+                    inner[j, c * 10 + a : c * 10 + a + 1, :] = jnp.where(even, last, first)
+                    outer[j, c * 10 + a : c * 10 + a + 1, :] = jnp.where(even, first, last)
+
+    for copy in copies[0]:
         copy.wait()
     for a in range(5):
         rec = 1.0 / les[0, a]
@@ -174,25 +187,34 @@
         back[j, 160:170, :] = les[4, 0, :, tile(j)]
         back[j, 170:176, :] = jnp.zeros((6, 128), F32)
         back[j, 221:224, :] = jnp.zeros((3, 128), F32)
+        for buf in (fwd, inner, outer):
+            buf[j, 95:96, :] = jnp.zeros((1, 128), F32)
+    radial_faces(range(5))
+    for copy in copies[2]:
+        copy.wait()
+    for j in range(5):
         for buf, a, base in ((back, 0, B_APE), (fwd, 4, F_APE)):
             for r in range(5):
                 buf[j, pl.ds(base + r, 4, stride=5), :] = ac[a, r, :, tile(j)]
                 buf[j, pl.ds(base + 30 + r, 3, stride=5), :] = mv[a, r, :, tile(j)]
             buf[j, base + 20 : base + 25, :] = den[a, :, tile(j)]
             buf[j, base + 25 : base + 30, :] = snd[a, :, tile(j)]
+        for a in range(5):
+            for src, base in ((ac, F_APE), (mv, F_APE + 30)):
+                first, last = src[a, 0, :, tile(j)], src[a, 4, :, tile(j)]
+                at = pl.ds(base + a, first.shape[0], stride=5)
+                inner[j, at, :] = jnp.where(even, last, first)
+                outer[j, at, :] = jnp.where(even, first, last)
+            for src, base in ((den, F_APE + 20), (snd, F_APE + 25)):
+                first, last = src[a, 0:1, tile(j)], src[a, 4:5, tile(j)]
+                inner[j, base + a : base + a + 1, :] = jnp.where(even, last, first)
+                outer[j, base + a : base + a + 1, :] = jnp.where(even, first, last)
+    for copy in copies[1]:
+        copy.wait()
+    for j in range(5):
         for c in range(5):
             fwd[j, c * 10 : c * 10 + 10, :] = les[c, 9, :, tile(j)]
-        for buf, r, ra in ((low, 0, 0), (high, 9, 4)):
-            for c in range(5):
-                for a in range(10):
-                    buf[j, c * 10 + a : c * 10 + a + 1, :] = les[c, a, r : r + 1, tile(j)]
-            for a in range(5):
-                buf[j, pl.ds(F_APE + a, 4, stride=5), :] = ac[a, ra, :, tile(j)]
-                buf[j, pl.ds(F_APE + 30 + a, 3, stride=5), :] = mv[a, ra, :, tile(j)]
-                buf[j, F_APE + 20 + a : F_APE + 21 + a, :] = den[a, ra : ra + 1, tile(j)]
-                buf[j, F_APE + 25 + a : F_APE + 26 + a, :] = snd[a, ra : ra + 1, tile(j)]
-        for buf in (fwd, low, high):
-            buf[j, 95:96, :] = jnp.zeros((1, 128), F32)
+    radial_faces(range(5, 10))
     first = lax.axis_index("group") == 0
 
     def end(ref, *at):
@@ -271,7 +293,7 @@
     def les_rows_pass():
         lane = lax.broadcasted_iota(jnp.int32, (8, 128), 1)
 
-        @pl.loop(0, 20)
+        @pl.loop(0, 20, unroll=5)
         def _(t):
             er = t // 10
             base = (t - er * 10) * 10 + er * 5
@@ -438,49 +460,60 @@
     return common(fl, fr, les_speed(rl, vl, pl_, k), les_speed(rr, vr, pr, k), ql, qr), fl, fr
 
 
+def les_change(own, nbr, k, side):
+    ro, vo, po = les_prims(own)
+    rn, vn, pn = les_prims(nbr)
+    fo, fn = les_flux(own, vo, po, k), les_flux(nbr, vn, pn, k)
+    half = 0.5 * LIFT * jnp.maximum(les_speed(ro, vo, po, k), les_speed(rn, vn, pn, k))
+    return [(0.5 * LIFT * side) * (fo[n] - fn[n]) + half * (nbr[n] - own[n]) for n in range(5)]
+
+
+def ape_change(own, nbr, k, side):
+    half = 0.5 * LIFT * jnp.maximum(jnp.abs(own[6 + k]) + own[5], jnp.abs(nbr[6 + k]) + nbr[5])
+    out = [half * (nbr[n] - own[n]) for n in range(4)]
+    out[0] = out[0] + (0.5 * LIFT * side) * (ape_leading(own, k) - ape_leading(nbr, k))
+    out[1 + k] = out[1 + k] + (0.5 * LIFT * side) * (ape_carried(own) - ape_carried(nbr))
+    return out
+
+
 def finish_kernel(
-    les, ac, acc, da_in, lamb_own, m, pp_hi, pp_lo, back, fwd, low, high, axial,
-    fwd_in, low_in, high_in, axial_in, back_in, perm, perm_t, coef,
+    les, ac, acc, da_in, lamb_own, m, pp_hi, pp_lo, back, fwd, inner, outer, axial,
+    fwd_in, inner_in, outer_in, axial_in, back_in, perm, perm_t, coef,
     les_out, ac_out, delta, result, yn, rt, rhs_hi, rhs_lo, osc, da, sem,
 ):
     rad = lax.axis_index("rad")
+    even = lax.rem(rad, 2) == 0
     first_half = lax.axis_index("group") == 0
-    at_low, at_high = rad == 0, rad == lax.axis_size("rad") - 1
+    inner_side, axis_side = jnp.where(even, 1.0, -1.0), jnp.where(first_half, 1.0, -1.0)
+    inner_row = jnp.where(even, 9, 0)
+    at_end = (rad == 0) | (rad == lax.axis_size("rad") - 1)
 
     def les_faces():
         value = relane(wide(acc), perm_t[...])
         for j in range(5):
             delta[j] = value[:, tile(j)]
         for j in range(5):
-            own_low, own_high = les_rows(low, j), les_rows(high, j)
-            nbr_low = [jnp.where(at_low, o, n) for o, n in zip(own_low, les_rows(low_in, j))]
-            nbr_high = [jnp.where(at_high, o, n) for o, n in zip(own_high, les_rows(high_in, j))]
-            h, _, fr = les_common(nbr_low, own_low, 1)
-            g, fl, _ = les_common(own_high, nbr_high, 1)
-            for n in range(5):
-                at = pl.ds(n * 100, 10, stride=10)
-                delta[j, at, :] = delta[j, at, :] + LIFT * (h[n] - fr[n])
-                at = pl.ds(n * 100 + 9, 10, stride=10)
-                delta[j, at, :] = delta[j, at, :] + LIFT * (fl[n] - g[n])
-            h, _, fr = les_common(les_rows(fwd_in, j), back_face(back, j), 0)
-            g, fl, _ = les_common(les_rows(fwd, j), back_face(back_in, j), 0)
-            for n in range(5):
-                at = slice(n * 100, n * 100 + 10)
-                delta[j, at, :] = delta[j, at, :] + LIFT * (h[n] - fr[n])
-                at = slice(n * 100 + 90, n * 100 + 100)
-                delta[j, at, :] = delta[j, at, :] + LIFT * (fl[n] - g[n])
+
+            def add(start, stride, change):
+                for n in range(5):
+                    at = pl.ds(n * 100 + start, 10, stride=stride)
+                    delta[j, at, :] = delta[j, at, :] + change[n]
+
+            add(inner_row, 10, les_change(les_rows(inner, j), les_rows(inner_in, j), 1, inner_side))
+            own = les_rows(outer, j)
+            nbr = [jnp.where(at_end, o, n) for o, n in zip(own, les_rows(outer_in, j))]
+            add(9 - inner_row, 10, les_change(own, nbr, 1, -inner_side))
+            add(0, 1, les_change(back_face(back, j), les_rows(fwd_in, j), 0, -1.0))
+            add(90, 1, les_change(les_rows(fwd, j), back_face(back_in, j), 0, 1.0))
         own = [axial[16 * c : 16 * c + 16, :] for c in range(5)]
         nbr = [axial_in[16 * c : 16 * c + 16, :] for c in range(5)]
-        ql = [jnp.where(first_half, o, n) for o, n in zip(own, nbr)]
-        qr = [jnp.where(first_half, n, o) for o, n in zip(own, nbr)]
-        h, fl, fr = les_common(ql, qr, 2)
+        change = les_change(own, nbr, 2, axis_side)
         lane = lax.broadcasted_iota(jnp.int32, (10, 128), 1)
         on_last = (lane == 127) & first_half
         on_first = (lane == 0) & jnp.logical_not(first_half)
         for n in range(5):
-            axis = LIFT * jnp.where(first_half, fl[n] - h[n], h[n] - fr[n])
             for a in range(10):
-                column = jnp.broadcast_to(axis[0:10, a : a + 1], (10, 128))
+                column = jnp.broadcast_to(change[n][0:10, a : a + 1], (10, 128))
                 at = slice(n * 100 + a * 10, n * 100 + a * 10 + 10)
                 for j in range(5):
                     value = delta[j, at, :]
@@ -489,6 +522,8 @@
                     if j == 4:
                         value = value + jnp.where(on_last, column, 0.0)
                     result[n, a, :, tile(j)] = les[n, a, :, tile(j)] + DT * value
+
+    def send_les():
         pltpu.make_async_copy(result, les_out, sem).start()
 
     def sources():
@@ -562,38 +597,25 @@
             )
 
         own, nbr = axial_state(axial), axial_state(axial_in)
-        ql = [jnp.where(first_half, o, n) for o, n in zip(own, nbr)]
-        qr = [jnp.where(first_half, n, o) for o, n in zip(own, nbr)]
-        h, fl, fr = ape_common(ql, qr, 2)
-        rows = []
-        for n in range(4):
-            fl_n = fl[0] if n == 0 else fl[1] if n == 3 else 0.0
-            fr_n = fr[0] if n == 0 else fr[1] if n == 3 else 0.0
-            rows.append(LIFT * jnp.where(first_half, fl_n - h[n], h[n] - fr_n))
-        axis = jnp.concatenate(rows, axis=0)
+        axis = jnp.concatenate(ape_change(own, nbr, 2, axis_side), axis=0)
         lane4 = lax.broadcasted_iota(jnp.int32, (4, 128), 1)
         on_last = (lane4 == 127) & first_half
         on_first = (lane4 == 0) & jnp.logical_not(first_half)
         for j in range(5):
             da[j] = value[:, tile(j)]
 
-            def add(start, stride, h, own, k, sign):
+            def add(start, stride, change):
                 for n in range(4):
-                    own_n = own[0] if n == 0 else own[1] if n == 1 + k else 0.0
                     at = pl.ds(start + n, 5, stride=stride)
-                    da[j, at, :] = da[j, at, :] + sign * LIFT * (h[n] - own_n)
-
-            h, _, fr = ape_common(ape_face(fwd_in, F_APE, j), ape_face(back, B_APE, j), 0)
-            add(0, 4, h, fr, 0, 1.0)
-            h, fl, _ = ape_common(ape_face(fwd, F_APE, j), ape_face(back_in, B_APE, j), 0)
-            add(80, 4, h, fl, 0, -1.0)
-            own_l, own_h = ape_face(low, F_APE, j), ape_face(high, F_APE, j)
-            nbr_l = [jnp.where(at_low, o, n) for o, n in zip(own_l, ape_face(low_in, F_APE, j))]
-            nbr_h = [jnp.where(at_high, o, n) for o, n in zip(own_h, ape_face(high_in, F_APE, j))]
-            h, _, fr = ape_common(nbr_l, own_l, 1)
-            add(0, 20, h, fr, 1, 1.0)
-            h, fl, _ = ape_common(own_h, nbr_h, 1)
-            add(16, 20, h, fl, 1, -1.0)
+                    da[j, at, :] = da[j, at, :] + change[n]
+
+            add(0, 4, ape_change(ape_face(back, B_APE, j), ape_face(fwd_in, F_APE, j), 0, -1.0))
+            add(80, 4, ape_change(ape_face(fwd, F_APE, j), ape_face(back_in, B_APE, j), 0, 1.0))
+            own, nbr = ape_face(inner, F_APE, j), ape_face(inner_in, F_APE, j)
+            add(jnp.where(even, 16, 0), 20, ape_change(own, nbr, 1, inner_side))
+            own = ape_face(outer, F_APE, j)
+            nbr = [jnp.where(at_end, o, n) for o, n in zip(own, ape_face(outer_in, F_APE, j))]
+            add(jnp.where(even, 0, 16), 20, ape_change(own, nbr, 1, -inner_side))
             for a in range(5):
                 for r in range(5):
                     i = a * 5 + r
@@ -603,9 +625,8 @@
                         change = change + jnp.where(on_last if j == 4 else on_first, column, 0.0)
                     ac_out[a, r, :, tile(j)] = ac[a, r, :, tile(j)] + DT * change
 
-    les_faces()
-    sources()
-    acoustic()
+    for part in (les_faces, send_les, sources, acoustic):
+        part()
     pltpu.make_async_copy(result, les_out, sem).wait()
 
 
@@ -627,20 +648,20 @@
     mv = jnp.transpose(mv, (1, 2, 0, 3))
     proj = jnp.transpose(proj, (1, 0, 2)).reshape(1000, 125)
     counts, elem, pattern = counts.reshape(1, 128), elem.reshape(1, 768), pattern.reshape(1, 768)
-    perm = jnp.asarray(lane_split(), BF16)
-    perm_t = jnp.asarray(lane_split().T, BF16)
+    perm = jnp.asarray(np.tile(lane_split(), (2, 1)), BF16)
+    perm_t = jnp.asarray(np.tile(lane_split().T, (2, 1)), BF16)
     coef = jnp.asarray(radial_coefs(), F32)
 
     hbm = pl.BlockSpec(memory_space=pltpu.HBM)
     held = [pltpu.VMEM(a.shape, F32) for a in (les, ac, den, snd, mv)]
-    back, fwd, low, high, axial, les, ac, den, snd, mv = pl.pallas_call(
+    back, fwd, inner, outer, axial, les, ac, den, snd, mv = pl.pallas_call(
         pack_kernel,
         out_shape=[pltpu.VMEM((5, n, 128), F32) for n in (B_ROWS, F_ROWS, F_ROWS, F_ROWS)]
         + [pltpu.VMEM((G_ROWS, 128), F32)]
         + held,
         in_specs=[hbm] * 5,
         out_specs=[vmem] * 10,
-        scratch_shapes=[pltpu.SemaphoreType.DMA((9,))],
+        scratch_shapes=[pltpu.SemaphoreType.DMA((14,))],
         compiler_params=params(),
         cost_estimate=cost(1_000_000, 5_000_000),
         name="pack",
@@ -649,8 +670,8 @@
     azim, radc = lax.axis_size("azim"), lax.axis_size("rad")
     back_in = lax.ppermute(back, "azim", [(i, (i - 1) % azim) for i in range(azim)])
     fwd_in = lax.ppermute(fwd, "azim", [(i, (i + 1) % azim) for i in range(azim)])
-    high_in = lax.ppermute(low, "rad", [(i, i - 1) for i in range(1, radc)])
-    low_in = lax.ppermute(high, "rad", [(i, i + 1) for i in range(radc - 1)])
+    inner_in = lax.ppermute(inner, "rad", [(i, i ^ 1) for i in range(radc)])
+    outer_in = lax.ppermute(outer, "rad", [p for i in range(1, radc - 1, 2) for p in ((i, i + 1), (i + 1, i))])
     axial_in = lax.ppermute(axial, "group", [(0, 1), (1, 0)])
 
     acc, da, lamb, m, pp_hi, pp_lo = pl.pallas_call(
@@ -696,8 +717,8 @@
         cost_estimate=cost(500_000_000, 4_000_000),
         name="finish",
     )(
-        les, ac, acc, da, lamb, m, pp_hi, pp_lo, back, fwd, low, high, axial,
-        fwd_in, low_in, high_in, axial_in, back_in, perm, perm_t, coef,
+        les, ac, acc, da, lamb, m, pp_hi, pp_lo, back, fwd, inner, outer, axial,
+        fwd_in, inner_in, outer_in, axial_in, back_in, perm, perm_t, coef,
     )
     return les_next, jnp.transpose(ac_next, (2, 0, 1, 3))
 

time: 35.6 us -> 32.8 us (0.921)
  starting transfers between devices: 17.5 us -> 15.8 us
  Pallas kernels: 17.1 us -> 15.9 us
    ppermute x2, starting transfers between devices: 7.56 us -> 5.82 us  [the longest x1 4.59 us: body(): lax.ppermute(outer, 'rad', [p for i in range(1, radc - 1, 2) for p in ((i...]
    pallas_call x1, Pallas kernels: 8.55 us -> 7.56 us  [body(): pl.pallas_call(interior_kernel, out_shape=[shape(5, 512, 128), shape(5, 1...]
  transfers between devices with their start and end apart: 5 -> 5, of which waited for: 0 -> 0; matrix products, arithmetic and copies ran while one was open for 0% -> 0% of each run, Pallas kernels for 24% -> 23%
where the time goes in v3:
time: 32.8 us; the launch traced here: 32.7 us
  Pallas kernels  15.9 us (48%)
  starting transfers between devices  15.8 us (48%)
  between operations  0.97 us (3%)
    ppermute x1, starting transfers between devices, body(): lax.ppermute(back, 'azim', [(i, (i - 1) % azim) for i in range(azim)])  8.68 us
    pallas_call x1, Pallas kernels, body(): pl.pallas_call(interior_kernel, out_shape=[shape(5, 512, 128), shape(5, 1...  7.56 us
    pallas_call x1, Pallas kernels, body(): pl.pallas_call(finish_kernel, out_shape=[shape(5, 10, 10, NX), shape(5, 5...  5.45 us
    ppermute x1, starting transfers between devices, body(): lax.ppermute(outer, 'rad', [p for i in range(1, radc - 1, 2) for p in ((i...  4.59 us
    pallas_call x1, Pallas kernels, body(): pl.pallas_call(pack_kernel, out_shape=[pltpu.VMEM((5, n, 128), F32) for n...  2.89 us
    ppermute x1, starting transfers between devices, body(): axial_in = lax.ppermute(axial, 'group', [(0, 1), (1, 0)])  1.3 us
    ppermute x1, starting transfers between devices, body(): inner_in = lax.ppermute(inner, 'rad', [(i, i ^ 1) for i in range(radc)])  1.24 us
  transfers between devices with their start and end apart: 5, of which 0 were waited for; matrix products, arithmetic and copies ran while one was open for 0% of the time, Pallas kernels for 23%

profile of v3, /device:TPU:1, one launch (start us, length us, event | category | flops | bytes accessed | tf_op | source)
XLA Modules:
  0.0 32.7 jit_solution(16928900408234063827)
XLA Ops:
  0.6 0.0 copy-start.2
  0.6 0.0 copy-start
  0.7 0.0 copy-start.5
  0.7 0.0 copy-start.4
  0.7 0.0 copy-start.6
  0.7 0.0 copy-start.3
  0.7 2.9 %pack.1 = (f32[5,224,128]{2,1,0:T(8,128)S(1)}, f32[5,96,128]{2,1,0:T(8,128)S(1)}, f32[5,96,128]{2,1,0:T(8,128)S(1)}, f32[5,96,128]{2,1,0:T(8,128)S(1)}, f32[160,...) custom-call(f32[5,10,10,640]{3,2,1,0:T(8,128)} %les_h.1, ...), custom_call_target="tpu_custom_call" | custom-call | flops 1000000 | bytes 5000000 | tf_op jit(solution)/shard_map/pack/pallas_call | solution.py:657
  3.6 8.7 %collective-permute-start.4 = (f32[5,224,128]{2,1,0:T(8,128)S(1)}, f32[5,224,128]{2,1,0:T(8,128)S(1)}, u32[]{:S(2)}, u32[]{:S(2)}) collective-permute-start(f32[5,224,128]{2,1,0:T(8,128)S(1)} %get-tuple-element.31.back), channel_id=1, source_target_pairs={{0,248},{8,0},{16,8},{24,16},{32,24},{40,32},{48,40},{56,48},{64,5... | collective-permute-start | bytes 1720328 | tf_op jit(solution)/shard_map/ppermute | solution.py:671
  12.3 1.3 %collective-permute-start.3 = (f32[160,128]{1,0:T(8,128)S(1)}, f32[160,128]{1,0:T(8,128)S(1)}, u32[]{:S(2)}, u32[]{:S(2)}) collective-permute-start(f32[160,128]{1,0:T(8,128)S(1)} %get-tuple-element.35.axial), channel_id=1, source_target_pairs={{0,1},{1,0},{2,3},{3,2},{4,5},{5,4},{6,7},{7,6},{8,9},{9,8},{10,11... | collective-permute-start | bytes 245768 | tf_op jit(solution)/shard_map/ppermute | solution.py:675
  13.6 0.0 collective-permute-start
  13.6 1.2 %collective-permute-start.1 = (f32[5,96,128]{2,1,0:T(8,128)S(1)}, f32[5,96,128]{2,1,0:T(8,128)S(1)}, u32[]{:S(2)}, u32[]{:S(2)}) collective-permute-start(f32[5,96,128]{2,1,0:T(8,128)S(1)} %get-tuple-element.33.inner), channel_id=1, source_target_pairs={{0,2},{2,0},{4,6},{6,4},{1,3},{3,1},{5,7},{7,5},{8,10},{10,8},{12,... | collective-permute-start | bytes 737288 | tf_op jit(solution)/shard_map/ppermute | solution.py:673
  14.8 4.6 %collective-permute-start.2 = (f32[5,96,128]{2,1,0:T(8,128)S(1)}, f32[5,96,128]{2,1,0:T(8,128)S(1)}, u32[]{:S(2)}, u32[]{:S(2)}) collective-permute-start(f32[5,96,128]{2,1,0:T(8,128)S(1)} %get-tuple-element.34.outer), channel_id=1, source_target_pairs={{2,4},{4,2},{3,5},{5,3},{10,12},{12,10},{11,13},{13,11},{18,20},{2... | collective-permute-start | bytes 737288 | tf_op jit(solution)/shard_map/ppermute | solution.py:674
  19.4 0.0 copy-done.2
  19.4 0.0 copy-done
  19.4 0.0 copy-done.5
  19.4 0.0 copy-done.4
  19.4 0.0 copy-done.6
  19.4 0.0 copy-done.3
  19.5 0.0 copy-start.1
  19.5 7.6 %interior.1 = (f32[5,512,128]{2,1,0:T(8,128)S(1)}, f32[5,104,128]{2,1,0:T(8,128)S(1)}, bf16[768,512]{1,0:T(8,128)(2,1)S(1)}, bf16[768,1024]{1,0:T(8,128)(2,1)S(1...) custom-call(f32[5,10,10,640]{3,2,1,0:T(8,128)S(1)} %get-tuple-element.20.les, ...), custom_call_target="tpu_custom_call" | custom-call | flops 5000000000 | bytes 10000000 | tf_op jit(solution)/shard_map/interior/pallas_call | solution.py:677
  27.0 0.0 collective-permute-done.3.axial_in
  27.1 0.0 collective-permute-done.fwd_in
  27.1 0.0 collective-permute-done.1.inner_in
  27.1 0.0 collective-permute-done.2.outer_in
  27.1 0.0 collective-permute-done.4.back_in
  27.1 0.0 copy-done.1
  27.1 5.5 %finish.1 = (f32[5,10,10,640]{3,2,1,0:T(8,128)}, f32[5,5,4,640]{3,2,1,0:T(4,128)}) custom-call(f32[5,10,10,640]{3,2,1,0:T(8,128)S(1)} %get-tuple-element.20.les, f32[5,5,4,640]{3,2,1,0:T(4,128)S(1)} %get-tuple-element.21.ac, f32[5,512,128]{2,1,0:T(8,128)S(1)} %get-tuple-element.25.acc, f32[5,104,128]{2,1,0:T(8,128)S(1)} %get-tuple-element.26.da_in, ...), custom_call_target="tpu_custom_call" | custom-call | flops 500000000 | bytes 4000000 | tf_op jit(solution)/shard_map/finish/pallas_call | solution.py:700
Async XLA Ops:
  0.6 18.8 %copy-start.2 = (f32[4,5,8,128]{3,2,1,0:T(8,128)S(1)}, f32[4,5,8,128]{3,2,1,0:T(8,128)}, u32[]{:S(2)}) copy-start(f32[4,5,8,128]{3,2,1,0:T(8,128)} %constant.8.clone.coef) | copy-start | bytes 245764
  0.6 18.8 %copy-start = (bf16[1280,640]{1,0:T(8,128)(2,1)S(1)}, bf16[1280,640]{1,0:T(8,128)(2,1)}, u32[]{:S(2)}) copy-start(bf16[1280,640]{1,0:T(8,128)(2,1)} %constant.6.clone.perm) | copy-start | bytes 4915204
  0.7 18.8 %copy-start.5 = (s32[1,1,1,768]{3,2,1,0:T(1,128)S(1)}, s32[1,1,1,768]{3,2,1,0:T(1,128)}, u32[]{:S(2)}) copy-start(s32[1,1,1,768]{3,2,1,0:T(1,128)} %param.20) | copy-start | bytes 9220
  0.7 18.8 %copy-start.4 = (s32[1,1,1,768]{3,2,1,0:T(1,128)S(1)}, s32[1,1,1,768]{3,2,1,0:T(1,128)}, u32[]{:S(2)}) copy-start(s32[1,1,1,768]{3,2,1,0:T(1,128)} %param.19) | copy-start | bytes 9220
  0.7 18.8 %copy-start.6 = (s32[1,1,1,128]{3,2,1,0:T(1,128)S(1)}, s32[1,1,1,128]{3,2,1,0:T(1,128)}, u32[]{:S(2)}) copy-start(s32[1,1,1,128]{3,2,1,0:T(1,128)} %param.18) | copy-start | bytes 1540
  0.7 18.8 %copy-start.3 = (f32[8,125,125]{2,0,1:T(8,128)S(1)}, f32[8,125,125]{2,0,1:T(8,128)}, u32[]{:S(2)}) copy-start(f32[8,125,125]{2,0,1:T(8,128)} %param.17) | copy-start | bytes 1500004
  3.6 23.5 %collective-permute-start.4 = (f32[5,224,128]{2,1,0:T(8,128)S(1)}, f32[5,224,128]{2,1,0:T(8,128)S(1)}, u32[]{:S(2)}, u32[]{:S(2)}) collective-permute-start(f32[5,224,128]{2,1,0:T(8,128)S(1)} %get-tuple-element.31.back), channel_id=1, source_target_pairs={{0,248},{8,0},{16,8},{24,16},{32,24},{40,32},{48,40},{56,48},{64,5... | collective-permute-start | bytes 1720328 | tf_op jit(solution)/shard_map/ppermute | solution.py:671
  12.3 14.8 %collective-permute-start.3 = (f32[160,128]{1,0:T(8,128)S(1)}, f32[160,128]{1,0:T(8,128)S(1)}, u32[]{:S(2)}, u32[]{:S(2)}) collective-permute-start(f32[160,128]{1,0:T(8,128)S(1)} %get-tuple-element.35.axial), channel_id=1, source_target_pairs={{0,1},{1,0},{2,3},{3,2},{4,5},{5,4},{6,7},{7,6},{8,9},{9,8},{10,11... | collective-permute-start | bytes 245768 | tf_op jit(solution)/shard_map/ppermute | solution.py:675
  13.6 13.5 %collective-permute-start = (f32[5,96,128]{2,1,0:T(8,128)S(1)}, f32[5,96,128]{2,1,0:T(8,128)S(1)}, u32[]{:S(2)}, u32[]{:S(2)}) collective-permute-start(f32[5,96,128]{2,1,0:T(8,128)S(1)} %get-tuple-element.32.fwd), channel_id=1, source_target_pairs={{0,8},{8,16},{16,24},{24,32},{32,40},{40,48},{48,56},{56,64},{64,7... | collective-permute-start | bytes 737288 | tf_op jit(solution)/shard_map/ppermute | solution.py:672
  13.6 13.5 %collective-permute-start.1 = (f32[5,96,128]{2,1,0:T(8,128)S(1)}, f32[5,96,128]{2,1,0:T(8,128)S(1)}, u32[]{:S(2)}, u32[]{:S(2)}) collective-permute-start(f32[5,96,128]{2,1,0:T(8,128)S(1)} %get-tuple-element.33.inner), channel_id=1, source_target_pairs={{0,2},{2,0},{4,6},{6,4},{1,3},{3,1},{5,7},{7,5},{8,10},{10,8},{12,... | collective-permute-start | bytes 737288 | tf_op jit(solution)/shard_map/ppermute | solution.py:673
  14.8 12.3 %collective-permute-start.2 = (f32[5,96,128]{2,1,0:T(8,128)S(1)}, f32[5,96,128]{2,1,0:T(8,128)S(1)}, u32[]{:S(2)}, u32[]{:S(2)}) collective-permute-start(f32[5,96,128]{2,1,0:T(8,128)S(1)} %get-tuple-element.34.outer), channel_id=1, source_target_pairs={{2,4},{4,2},{3,5},{5,3},{10,12},{12,10},{11,13},{13,11},{18,20},{2... | collective-permute-start | bytes 737288 | tf_op jit(solution)/shard_map/ppermute | solution.py:674
  19.5 7.6 %copy-start.1 = (bf16[1280,640]{1,0:T(8,128)(2,1)S(1)}, bf16[1280,640]{1,0:T(8,128)(2,1)}, u32[]{:S(2)}) copy-start(bf16[1280,640]{1,0:T(8,128)(2,1)} %constant.7.clone.perm_t) | copy-start | bytes 4915204

commit v4 on v3

--- a/solution.py
+++ b/solution.py
@@ -95,6 +95,19 @@
 
 def relane(x, matrix):
     return dot(jnp.concatenate(split(x), axis=1), matrix)
+
+
+def split_tiles(x):
+    lane = lax.broadcasted_iota(jnp.int32, (8, 128), 1)
+    out = []
+    for j in range(5):
+        element = ((lane - j) * 77) & 127
+        source = (5 * element + j) >> 7
+        merged = x[0]
+        for t in range(1, 5):
+            merged = jnp.where(source == t, x[t], merged)
+        out.append(jnp.take_along_axis(merged, (5 * lane + j) & 127, axis=1, mode="promise_in_bounds"))
+    return out
 
 
 def les_prims(q):
@@ -245,7 +258,7 @@
 
 def interior_kernel(
     les, ac, den, snd, mv, proj, counts, elem, pattern, perm, coef,
-    acc, da, lamb_out, m_out, pp_hi, pp_lo,
+    acc, da, lamb_out, m_out, pp,
     x, y, vel, omega, rt, one_hot, owned, flat,
 ):
     def list_matrices():
@@ -271,8 +284,9 @@
         flat[0:1000, 0:125] = proj[...]
         for p in range(8):
             hi, lo = split(flat[pl.ds(p, 128, stride=8), :])
-            pp_hi[:, tile(p)] = hi
-            pp_lo[:, tile(p)] = lo
+            pp[:, tile(p)] = hi
+            pp[:, tile(8 + p)] = lo
+            pp[:, tile(16 + p)] = hi
 
     def lane_splitting():
         for j in range(5):
@@ -286,9 +300,12 @@
                     x[j, APE_MV + 3 * i : APE_MV + 3 * i + 3, :] = mv[a, r, :, tile(j)]
                 x[j, APE_DEN + 8 * a : APE_DEN + 8 * a + 5, :] = den[a, :, tile(j)]
                 x[j, APE_SND + 8 * a : APE_SND + 8 * a + 5, :] = snd[a, :, tile(j)]
-        value = relane(wide(x), perm[...])
-        for j in range(5):
-            y[j] = value[:, tile(j)]
+        value = relane(jnp.concatenate([x[j, 0:512, :] for j in range(5)], axis=1), perm[...])
+        for j in range(5):
+            y[j, 0:504, :] = value[0:504, tile(j)]
+        for i in range(63, 96):
+            for j, part in enumerate(split_tiles([x[j, 8 * i : 8 * i + 8, :] for j in range(5)])):
+                y[j, 8 * i : 8 * i + 8, :] = part
 
     def les_rows_pass():
         lane = lax.broadcasted_iota(jnp.int32, (8, 128), 1)
@@ -477,9 +494,9 @@
 
 
 def finish_kernel(
-    les, ac, acc, da_in, lamb_own, m, pp_hi, pp_lo, back, fwd, inner, outer, axial,
+    les, ac, acc, da_in, lamb_own, m, pp, back, fwd, inner, outer, axial,
     fwd_in, inner_in, outer_in, axial_in, back_in, perm, perm_t, coef,
-    les_out, ac_out, delta, result, yn, rt, rhs_hi, rhs_lo, osc, da, sem,
+    les_out, ac_out, delta, result, yn, rt, rhs, osc, da, sem,
 ):
     rad = lax.axis_index("rad")
     even = lax.rem(rad, 2) == 0
@@ -562,10 +579,10 @@
         for p in range(8):
             for c in range(3):
                 hi, lo = split(s[c * 128 : c * 128 + 128, tile(p)])
-                rhs_hi[p * 128 : p * 128 + 128, tile(c)] = hi
-                rhs_lo[p * 128 : p * 128 + 128, tile(c)] = lo
-        hi = rhs_hi[...]
-        out = dot(pp_hi[...], hi) + (dot(pp_lo[...], hi) + dot(pp_hi[...], rhs_lo[...]))
+                rhs[p * 128 : p * 128 + 128, tile(c)] = hi
+                rhs[1024 + p * 128 : 1152 + p * 128, tile(c)] = hi
+                rhs[2048 + p * 128 : 2176 + p * 128, tile(c)] = lo
+        out = dot(pp[...], rhs[...])
         for c in range(3):
             osc[c] = out[:, tile(c)]
 
@@ -674,14 +691,14 @@
     outer_in = lax.ppermute(outer, "rad", [p for i in range(1, radc - 1, 2) for p in ((i, i + 1), (i + 1, i))])
     axial_in = lax.ppermute(axial, "group", [(0, 1), (1, 0)])
 
-    acc, da, lamb, m, pp_hi, pp_lo = pl.pallas_call(
+    acc, da, lamb, m, pp = pl.pallas_call(
         interior_kernel,
         out_shape=[
             shape(5, 512, 128), shape(5, 104, 128), shape(768, 512, dtype=BF16), shape(768, 1024, dtype=BF16),
-            shape(128, 1024, dtype=BF16), shape(128, 1024, dtype=BF16),
+            shape(128, 3072, dtype=BF16),
         ],
         in_specs=[vmem] * 11,
-        out_specs=[vmem] * 6,
+        out_specs=[vmem] * 5,
         scratch_shapes=[
             pltpu.VMEM((5, ROWS, 128), F32),
             pltpu.VMEM((5, ROWS, 128), F32),
@@ -700,15 +717,14 @@
     les_next, ac_next = pl.pallas_call(
         finish_kernel,
         out_shape=[shape(5, 10, 10, NX), shape(5, 5, 4, NX)],
-        in_specs=[vmem] * 21,
+        in_specs=[vmem] * 20,
         out_specs=[hbm, vmem],
         scratch_shapes=[
             pltpu.VMEM((5, 512, 128), F32),
             pltpu.VMEM((5, 10, 10, NX), F32),
             pltpu.VMEM((5, 160, 128), F32),
             pltpu.VMEM((2, 384, 128), F32),
-            pltpu.VMEM((1024, 384), BF16),
-            pltpu.VMEM((1024, 384), BF16),
+            pltpu.VMEM((3072, 384), BF16),
             pltpu.VMEM((3, 128, 128), F32),
             pltpu.VMEM((5, 104, 128), F32),
             pltpu.SemaphoreType.DMA(()),
@@ -717,7 +733,7 @@
         cost_estimate=cost(500_000_000, 4_000_000),
         name="finish",
     )(
-        les, ac, acc, da, lamb, m, pp_hi, pp_lo, back, fwd, inner, outer, axial,
+        les, ac, acc, da, lamb, m, pp, back, fwd, inner, outer, axial,
         fwd_in, inner_in, outer_in, axial_in, back_in, perm, perm_t, coef,
     )
     return les_next, jnp.transpose(ac_next, (2, 0, 1, 3))

time: 32.8 us -> 32.4 us (0.988)
  Pallas kernels: 15.9 us -> 15.5 us
    pallas_call x1, Pallas kernels: 7.56 us -> 7.06 us  [body(): pl.pallas_call(interior_kernel, out_shape=[shape(5, 512, 128), shape(5, 1...]
  transfers between devices with their start and end apart: 5 -> 5, of which waited for: 0 -> 0; matrix products, arithmetic and copies ran while one was open for 0% -> 0% of each run, Pallas kernels for 23% -> 22%
where the time goes in v4:
time: 32.4 us; the launch traced here: 32.3 us
  starting transfers between devices  15.8 us (49%)
  Pallas kernels  15.5 us (48%)
  between operations  0.97 us (3%)
    ppermute x1, starting transfers between devices, body(): lax.ppermute(back, 'azim', [(i, (i - 1) % azim) for i in range(azim)])  8.68 us
    pallas_call x1, Pallas kernels, body(): pl.pallas_call(interior_kernel, out_shape=[shape(5, 512, 128), shape(5, 1...  7.06 us
    pallas_call x1, Pallas kernels, body(): pl.pallas_call(finish_kernel, out_shape=[shape(5, 10, 10, NX), shape(5, 5...  5.52 us
    ppermute x1, starting transfers between devices, body(): lax.ppermute(outer, 'rad', [p for i in range(1, radc - 1, 2) for p in ((i...  4.59 us
    pallas_call x1, Pallas kernels, body(): pl.pallas_call(pack_kernel, out_shape=[pltpu.VMEM((5, n, 128), F32) for n...  2.89 us
    ppermute x1, starting transfers between devices, body(): axial_in = lax.ppermute(axial, 'group', [(0, 1), (1, 0)])  1.3 us
    ppermute x1, starting transfers between devices, body(): inner_in = lax.ppermute(inner, 'rad', [(i, i ^ 1) for i in range(radc)])  1.24 us
  transfers between devices with their start and end apart: 5, of which 0 were waited for; matrix products, arithmetic and copies ran while one was open for 0% of the time, Pallas kernels for 22%

profile of v4, /device:TPU:1, one launch (start us, length us, event | category | flops | bytes accessed | tf_op | source)
XLA Modules:
  0.0 32.3 jit_solution(8139115387508814264)
XLA Ops:
  0.6 0.0 copy-start.2
  0.6 0.0 copy-start
  0.7 0.0 copy-start.5
  0.7 0.0 copy-start.4
  0.7 0.0 copy-start.6
  0.7 0.0 copy-start.3
  0.7 2.9 %pack.1 = (f32[5,224,128]{2,1,0:T(8,128)S(1)}, f32[5,96,128]{2,1,0:T(8,128)S(1)}, f32[5,96,128]{2,1,0:T(8,128)S(1)}, f32[5,96,128]{2,1,0:T(8,128)S(1)}, f32[160,...) custom-call(f32[5,10,10,640]{3,2,1,0:T(8,128)} %les_h.1, ...), custom_call_target="tpu_custom_call" | custom-call | flops 1000000 | bytes 5000000 | tf_op jit(solution)/shard_map/pack/pallas_call | solution.py:674
  3.6 8.7 %collective-permute-start.4 = (f32[5,224,128]{2,1,0:T(8,128)S(1)}, f32[5,224,128]{2,1,0:T(8,128)S(1)}, u32[]{:S(2)}, u32[]{:S(2)}) collective-permute-start(f32[5,224,128]{2,1,0:T(8,128)S(1)} %get-tuple-element.29.back), channel_id=1, source_target_pairs={{0,248},{8,0},{16,8},{24,16},{32,24},{40,32},{48,40},{56,48},{64,5... | collective-permute-start | bytes 1720328 | tf_op jit(solution)/shard_map/ppermute | solution.py:688
  12.3 1.3 %collective-permute-start.3 = (f32[160,128]{1,0:T(8,128)S(1)}, f32[160,128]{1,0:T(8,128)S(1)}, u32[]{:S(2)}, u32[]{:S(2)}) collective-permute-start(f32[160,128]{1,0:T(8,128)S(1)} %get-tuple-element.33.axial), channel_id=1, source_target_pairs={{0,1},{1,0},{2,3},{3,2},{4,5},{5,4},{6,7},{7,6},{8,9},{9,8},{10,11... | collective-permute-start | bytes 245768 | tf_op jit(solution)/shard_map/ppermute | solution.py:692
  13.6 0.0 collective-permute-start
  13.6 1.2 %collective-permute-start.1 = (f32[5,96,128]{2,1,0:T(8,128)S(1)}, f32[5,96,128]{2,1,0:T(8,128)S(1)}, u32[]{:S(2)}, u32[]{:S(2)}) collective-permute-start(f32[5,96,128]{2,1,0:T(8,128)S(1)} %get-tuple-element.31.inner), channel_id=1, source_target_pairs={{0,2},{2,0},{4,6},{6,4},{1,3},{3,1},{5,7},{7,5},{8,10},{10,8},{12,... | collective-permute-start | bytes 737288 | tf_op jit(solution)/shard_map/ppermute | solution.py:690
  14.8 4.6 %collective-permute-start.2 = (f32[5,96,128]{2,1,0:T(8,128)S(1)}, f32[5,96,128]{2,1,0:T(8,128)S(1)}, u32[]{:S(2)}, u32[]{:S(2)}) collective-permute-start(f32[5,96,128]{2,1,0:T(8,128)S(1)} %get-tuple-element.32.outer), channel_id=1, source_target_pairs={{2,4},{4,2},{3,5},{5,3},{10,12},{12,10},{11,13},{13,11},{18,20},{2... | collective-permute-start | bytes 737288 | tf_op jit(solution)/shard_map/ppermute | solution.py:691
  19.4 0.0 copy-done.2
  19.4 0.0 copy-done
  19.4 0.0 copy-done.5
  19.4 0.0 copy-done.4
  19.4 0.0 copy-done.6
  19.4 0.0 copy-done.3
  19.5 0.0 copy-start.1
  19.5 7.1 %interior.1 = (f32[5,512,128]{2,1,0:T(8,128)S(1)}, f32[5,104,128]{2,1,0:T(8,128)S(1)}, bf16[768,512]{1,0:T(8,128)(2,1)S(1)}, bf16[768,1024]{1,0:T(8,128)(2,1)S(1)}, bf16[128,3072]{1,0:T(8,128)(2,1)S(1)}) custom-call(f32[5,10,10,640]{3,2,1,0:T(8,128)S(1)} %get-tuple-element.19.les, f32[5,5,4,640]{3,2,1,0:T(4,128)S(1)} %get-tuple-element.20.ac, ...), custom_call_target="tpu_custom_call" | custom-call | flops 5000000000 | bytes 10000000 | tf_op jit(solution)/shard_map/interior/pallas_call | solution.py:694
  26.5 0.0 collective-permute-done.3.axial_in
  26.5 0.0 collective-permute-done.fwd_in
  26.6 0.0 collective-permute-done.1.inner_in
  26.6 0.0 collective-permute-done.2.outer_in
  26.6 0.0 collective-permute-done.4.back_in
  26.6 0.0 copy-done.1
  26.6 5.5 %finish.1 = (f32[5,10,10,640]{3,2,1,0:T(8,128)}, f32[5,5,4,640]{3,2,1,0:T(4,128)}) custom-call(f32[5,10,10,640]{3,2,1,0:T(8,128)S(1)} %get-tuple-element.19.les, f32[5,5,4,640]{3,2,1,0:T(4,128)S(1)} %get-tuple-element.20.ac, f32[5,512,128]{2,1,0:T(8,128)S(1)} %get-tuple-element.24.acc, f32[5,104,128]{2,1,0:T(8,128)S(1)} %get-tuple-element.25.da_in, ...), custom_call_target="tpu_custom_call" | custom-call | flops 500000000 | bytes 4000000 | tf_op jit(solution)/shard_map/finish/pallas_call | solution.py:717
Async XLA Ops:
  0.6 18.8 %copy-start.2 = (f32[4,5,8,128]{3,2,1,0:T(8,128)S(1)}, f32[4,5,8,128]{3,2,1,0:T(8,128)}, u32[]{:S(2)}) copy-start(f32[4,5,8,128]{3,2,1,0:T(8,128)} %constant.8.clone.coef) | copy-start | bytes 245764
  0.6 18.8 %copy-start = (bf16[1280,640]{1,0:T(8,128)(2,1)S(1)}, bf16[1280,640]{1,0:T(8,128)(2,1)}, u32[]{:S(2)}) copy-start(bf16[1280,640]{1,0:T(8,128)(2,1)} %constant.6.clone.perm) | copy-start | bytes 4915204
  0.7 18.8 %copy-start.5 = (s32[1,1,1,768]{3,2,1,0:T(1,128)S(1)}, s32[1,1,1,768]{3,2,1,0:T(1,128)}, u32[]{:S(2)}) copy-start(s32[1,1,1,768]{3,2,1,0:T(1,128)} %param.20) | copy-start | bytes 9220
  0.7 18.8 %copy-start.4 = (s32[1,1,1,768]{3,2,1,0:T(1,128)S(1)}, s32[1,1,1,768]{3,2,1,0:T(1,128)}, u32[]{:S(2)}) copy-start(s32[1,1,1,768]{3,2,1,0:T(1,128)} %param.19) | copy-start | bytes 9220
  0.7 18.8 %copy-start.6 = (s32[1,1,1,128]{3,2,1,0:T(1,128)S(1)}, s32[1,1,1,128]{3,2,1,0:T(1,128)}, u32[]{:S(2)}) copy-start(s32[1,1,1,128]{3,2,1,0:T(1,128)} %param.18) | copy-start | bytes 1540
  0.7 18.8 %copy-start.3 = (f32[8,125,125]{2,0,1:T(8,128)S(1)}, f32[8,125,125]{2,0,1:T(8,128)}, u32[]{:S(2)}) copy-start(f32[8,125,125]{2,0,1:T(8,128)} %param.17) | copy-start | bytes 1500004
  3.6 23.0 %collective-permute-start.4 = (f32[5,224,128]{2,1,0:T(8,128)S(1)}, f32[5,224,128]{2,1,0:T(8,128)S(1)}, u32[]{:S(2)}, u32[]{:S(2)}) collective-permute-start(f32[5,224,128]{2,1,0:T(8,128)S(1)} %get-tuple-element.29.back), channel_id=1, source_target_pairs={{0,248},{8,0},{16,8},{24,16},{32,24},{40,32},{48,40},{56,48},{64,5... | collective-permute-start | bytes 1720328 | tf_op jit(solution)/shard_map/ppermute | solution.py:688
  12.3 14.3 %collective-permute-start.3 = (f32[160,128]{1,0:T(8,128)S(1)}, f32[160,128]{1,0:T(8,128)S(1)}, u32[]{:S(2)}, u32[]{:S(2)}) collective-permute-start(f32[160,128]{1,0:T(8,128)S(1)} %get-tuple-element.33.axial), channel_id=1, source_target_pairs={{0,1},{1,0},{2,3},{3,2},{4,5},{5,4},{6,7},{7,6},{8,9},{9,8},{10,11... | collective-permute-start | bytes 245768 | tf_op jit(solution)/shard_map/ppermute | solution.py:692
  13.6 13.0 %collective-permute-start = (f32[5,96,128]{2,1,0:T(8,128)S(1)}, f32[5,96,128]{2,1,0:T(8,128)S(1)}, u32[]{:S(2)}, u32[]{:S(2)}) collective-permute-start(f32[5,96,128]{2,1,0:T(8,128)S(1)} %get-tuple-element.30.fwd), channel_id=1, source_target_pairs={{0,8},{8,16},{16,24},{24,32},{32,40},{40,48},{48,56},{56,64},{64,7... | collective-permute-start | bytes 737288 | tf_op jit(solution)/shard_map/ppermute | solution.py:689
  13.6 13.0 %collective-permute-start.1 = (f32[5,96,128]{2,1,0:T(8,128)S(1)}, f32[5,96,128]{2,1,0:T(8,128)S(1)}, u32[]{:S(2)}, u32[]{:S(2)}) collective-permute-start(f32[5,96,128]{2,1,0:T(8,128)S(1)} %get-tuple-element.31.inner), channel_id=1, source_target_pairs={{0,2},{2,0},{4,6},{6,4},{1,3},{3,1},{5,7},{7,5},{8,10},{10,8},{12,... | collective-permute-start | bytes 737288 | tf_op jit(solution)/shard_map/ppermute | solution.py:690
  14.8 11.8 %collective-permute-start.2 = (f32[5,96,128]{2,1,0:T(8,128)S(1)}, f32[5,96,128]{2,1,0:T(8,128)S(1)}, u32[]{:S(2)}, u32[]{:S(2)}) collective-permute-start(f32[5,96,128]{2,1,0:T(8,128)S(1)} %get-tuple-element.32.outer), channel_id=1, source_target_pairs={{2,4},{4,2},{3,5},{5,3},{10,12},{12,10},{11,13},{13,11},{18,20},{2... | collective-permute-start | bytes 737288 | tf_op jit(solution)/shard_map/ppermute | solution.py:691
  19.5 7.1 %copy-start.1 = (bf16[1280,640]{1,0:T(8,128)(2,1)S(1)}, bf16[1280,640]{1,0:T(8,128)(2,1)}, u32[]{:S(2)}) copy-start(bf16[1280,640]{1,0:T(8,128)(2,1)} %constant.7.clone.perm_t) | copy-start | bytes 4915204

commit v5 on v4

--- a/solution.py
+++ b/solution.py
@@ -496,7 +496,7 @@
 def finish_kernel(
     les, ac, acc, da_in, lamb_own, m, pp, back, fwd, inner, outer, axial,
     fwd_in, inner_in, outer_in, axial_in, back_in, perm, perm_t, coef,
-    les_out, ac_out, delta, result, yn, rt, rhs, osc, da, sem,
+    les_out, ac_out, delta, result, yn, rt, rhs, osc, da, corr, sem,
 ):
     rad = lax.axis_index("rad")
     even = lax.rem(rad, 2) == 0
@@ -586,14 +586,24 @@
         for c in range(3):
             osc[c] = out[:, tile(c)]
 
-    def acoustic():
-        for j in range(5):
-            da[j] = da_in[j]
-            for a in range(5):
-                for n in range(1, 4):
-                    at = pl.ds(a * 20 + n, 5, stride=4)
-                    da[j, at, :] = da[j, at, :] - osc[n - 1, pl.ds(a * 25 + j, 5, stride=5), :]
-        value = relane(wide(da), perm_t[...])
+    axial_change = []
+
+    def acoustic_faces():
+        for j in range(5):
+            corr[j] = jnp.zeros((104, 128), F32)
+
+            def add(start, stride, change):
+                for n in range(4):
+                    at = pl.ds(start + n, 5, stride=stride)
+                    corr[j, at, :] = corr[j, at, :] + change[n]
+
+            add(0, 4, ape_change(ape_face(back, B_APE, j), ape_face(fwd_in, F_APE, j), 0, -1.0))
+            add(80, 4, ape_change(ape_face(fwd, F_APE, j), ape_face(back_in, B_APE, j), 0, 1.0))
+            own, nbr = ape_face(inner, F_APE, j), ape_face(inner_in, F_APE, j)
+            add(jnp.where(even, 16, 0), 20, ape_change(own, nbr, 1, inner_side))
+            own = ape_face(outer, F_APE, j)
+            nbr = [jnp.where(at_end, o, n) for o, n in zip(own, ape_face(outer_in, F_APE, j))]
+            add(jnp.where(even, 0, 16), 20, ape_change(own, nbr, 1, -inner_side))
 
         def axial_state(buf):
             def spread(base):
@@ -615,24 +625,24 @@
 
         own, nbr = axial_state(axial), axial_state(axial_in)
         axis = jnp.concatenate(ape_change(own, nbr, 2, axis_side), axis=0)
+        axial_change.append(axis)
+
+    def acoustic():
+        for j in range(5):
+            da[j] = da_in[j]
+            for a in range(5):
+                for n in range(1, 4):
+                    at = pl.ds(a * 20 + n, 5, stride=4)
+                    da[j, at, :] = da[j, at, :] - osc[n - 1, pl.ds(a * 25 + j, 5, stride=5), :]
+        value = relane(wide(da), perm_t[...])
+
+        axis = axial_change[0]
         lane4 = lax.broadcasted_iota(jnp.int32, (4, 128), 1)
         on_last = (lane4 == 127) & first_half
         on_first = (lane4 == 0) & jnp.logical_not(first_half)
         for j in range(5):
-            da[j] = value[:, tile(j)]
-
-            def add(start, stride, change):
-                for n in range(4):
-                    at = pl.ds(start + n, 5, stride=stride)
-                    da[j, at, :] = da[j, at, :] + change[n]
-
-            add(0, 4, ape_change(ape_face(back, B_APE, j), ape_face(fwd_in, F_APE, j), 0, -1.0))
-            add(80, 4, ape_change(ape_face(fwd, F_APE, j), ape_face(back_in, B_APE, j), 0, 1.0))
-            own, nbr = ape_face(inner, F_APE, j), ape_face(inner_in, F_APE, j)
-            add(jnp.where(even, 16, 0), 20, ape_change(own, nbr, 1, inner_side))
-            own = ape_face(outer, F_APE, j)
-            nbr = [jnp.where(at_end, o, n) for o, n in zip(own, ape_face(outer_in, F_APE, j))]
-            add(jnp.where(even, 0, 16), 20, ape_change(own, nbr, 1, -inner_side))
+            da[j] = value[:, tile(j)] + corr[j]
+
             for a in range(5):
                 for r in range(5):
                     i = a * 5 + r
@@ -642,7 +652,7 @@
                         change = change + jnp.where(on_last if j == 4 else on_first, column, 0.0)
                     ac_out[a, r, :, tile(j)] = ac[a, r, :, tile(j)] + DT * change
 
-    for part in (les_faces, send_les, sources, acoustic):
+    for part in (les_faces, send_les, sources, acoustic_faces, acoustic):
         part()
     pltpu.make_async_copy(result, les_out, sem).wait()
 
@@ -727,6 +737,7 @@
             pltpu.VMEM((3072, 384), BF16),
             pltpu.VMEM((3, 128, 128), F32),
             pltpu.VMEM((5, 104, 128), F32),
+            pltpu.VMEM((5, 104, 128), F32),
             pltpu.SemaphoreType.DMA(()),
         ],
         compiler_params=params(),

time: 32.4 us -> 32.4 us (level)
  no operation moved by 1% of the time
where the time goes in v5:
time: 32.4 us; the launch traced here: 32.3 us
  starting transfers between devices  15.8 us (49%)
  Pallas kernels  15.5 us (48%)
  between operations  0.97 us (3%)
    ppermute x1, starting transfers between devices, body(): lax.ppermute(back, 'azim', [(i, (i - 1) % azim) for i in range(azim)])  8.68 us
    pallas_call x1, Pallas kernels, body(): pl.pallas_call(interior_kernel, out_shape=[shape(5, 512, 128), shape(5, 1...  7.06 us
    pallas_call x1, Pallas kernels, body(): pl.pallas_call(finish_kernel, out_shape=[shape(5, 10, 10, NX), shape(5, 5...  5.52 us
    ppermute x1, starting transfers between devices, body(): lax.ppermute(outer, 'rad', [p for i in range(1, radc - 1, 2) for p in ((i...  4.59 us
    pallas_call x1, Pallas kernels, body(): pl.pallas_call(pack_kernel, out_shape=[pltpu.VMEM((5, n, 128), F32) for n...  2.89 us
    ppermute x1, starting transfers between devices, body(): axial_in = lax.ppermute(axial, 'group', [(0, 1), (1, 0)])  1.3 us
    ppermute x1, starting transfers between devices, body(): inner_in = lax.ppermute(inner, 'rad', [(i, i ^ 1) for i in range(radc)])  1.24 us
  transfers between devices with their start and end apart: 5, of which 0 were waited for; matrix products, arithmetic and copies ran while one was open for 0% of the time, Pallas kernels for 22%

profile of v5, /device:TPU:1, one launch (start us, length us, event | category | flops | bytes accessed | tf_op | source)
XLA Modules:
  0.0 32.3 jit_solution(12945782158205357919)
XLA Ops:
  0.6 0.0 copy-start.2
  0.6 0.0 copy-start
  0.7 0.0 copy-start.5
  0.7 0.0 copy-start.4
  0.7 0.0 copy-start.6
  0.7 0.0 copy-start.3
  0.7 2.9 %pack.1 = (f32[5,224,128]{2,1,0:T(8,128)S(1)}, f32[5,96,128]{2,1,0:T(8,128)S(1)}, f32[5,96,128]{2,1,0:T(8,128)S(1)}, f32[5,96,128]{2,1,0:T(8,128)S(1)}, f32[160,...) custom-call(f32[5,10,10,640]{3,2,1,0:T(8,128)} %les_h.1, ...), custom_call_target="tpu_custom_call" | custom-call | flops 1000000 | bytes 5000000 | tf_op jit(solution)/shard_map/pack/pallas_call | solution.py:684
  3.6 8.7 %collective-permute-start.4 = (f32[5,224,128]{2,1,0:T(8,128)S(1)}, f32[5,224,128]{2,1,0:T(8,128)S(1)}, u32[]{:S(2)}, u32[]{:S(2)}) collective-permute-start(f32[5,224,128]{2,1,0:T(8,128)S(1)} %get-tuple-element.29.back), channel_id=1, source_target_pairs={{0,248},{8,0},{16,8},{24,16},{32,24},{40,32},{48,40},{56,48},{64,5... | collective-permute-start | bytes 1720328 | tf_op jit(solution)/shard_map/ppermute | solution.py:698
  12.3 1.3 %collective-permute-start.3 = (f32[160,128]{1,0:T(8,128)S(1)}, f32[160,128]{1,0:T(8,128)S(1)}, u32[]{:S(2)}, u32[]{:S(2)}) collective-permute-start(f32[160,128]{1,0:T(8,128)S(1)} %get-tuple-element.33.axial), channel_id=1, source_target_pairs={{0,1},{1,0},{2,3},{3,2},{4,5},{5,4},{6,7},{7,6},{8,9},{9,8},{10,11... | collective-permute-start | bytes 245768 | tf_op jit(solution)/shard_map/ppermute | solution.py:702
  13.6 0.0 collective-permute-start
  13.6 1.2 %collective-permute-start.1 = (f32[5,96,128]{2,1,0:T(8,128)S(1)}, f32[5,96,128]{2,1,0:T(8,128)S(1)}, u32[]{:S(2)}, u32[]{:S(2)}) collective-permute-start(f32[5,96,128]{2,1,0:T(8,128)S(1)} %get-tuple-element.31.inner), channel_id=1, source_target_pairs={{0,2},{2,0},{4,6},{6,4},{1,3},{3,1},{5,7},{7,5},{8,10},{10,8},{12,... | collective-permute-start | bytes 737288 | tf_op jit(solution)/shard_map/ppermute | solution.py:700
  14.8 4.6 %collective-permute-start.2 = (f32[5,96,128]{2,1,0:T(8,128)S(1)}, f32[5,96,128]{2,1,0:T(8,128)S(1)}, u32[]{:S(2)}, u32[]{:S(2)}) collective-permute-start(f32[5,96,128]{2,1,0:T(8,128)S(1)} %get-tuple-element.32.outer), channel_id=1, source_target_pairs={{2,4},{4,2},{3,5},{5,3},{10,12},{12,10},{11,13},{13,11},{18,20},{2... | collective-permute-start | bytes 737288 | tf_op jit(solution)/shard_map/ppermute | solution.py:701
  19.4 0.0 copy-done.2
  19.4 0.0 copy-done
  19.4 0.0 copy-done.5
  19.4 0.0 copy-done.4
  19.4 0.0 copy-done.6
  19.4 0.0 copy-done.3
  19.5 0.0 copy-start.1
  19.5 7.1 %interior.1 = (f32[5,512,128]{2,1,0:T(8,128)S(1)}, f32[5,104,128]{2,1,0:T(8,128)S(1)}, bf16[768,512]{1,0:T(8,128)(2,1)S(1)}, bf16[768,1024]{1,0:T(8,128)(2,1)S(1)}, bf16[128,3072]{1,0:T(8,128)(2,1)S(1)}) custom-call(f32[5,10,10,640]{3,2,1,0:T(8,128)S(1)} %get-tuple-element.19.les, f32[5,5,4,640]{3,2,1,0:T(4,128)S(1)} %get-tuple-element.20.ac, ...), custom_call_target="tpu_custom_call" | custom-call | flops 5000000000 | bytes 10000000 | tf_op jit(solution)/shard_map/interior/pallas_call | solution.py:704
  26.5 0.0 collective-permute-done.3.axial_in
  26.5 0.0 collective-permute-done.fwd_in
  26.6 0.0 collective-permute-done.1.inner_in
  26.6 0.0 collective-permute-done.2.outer_in
  26.6 0.0 collective-permute-done.4.back_in
  26.6 0.0 copy-done.1
  26.6 5.5 %finish.1 = (f32[5,10,10,640]{3,2,1,0:T(8,128)}, f32[5,5,4,640]{3,2,1,0:T(4,128)}) custom-call(f32[5,10,10,640]{3,2,1,0:T(8,128)S(1)} %get-tuple-element.19.les, f32[5,5,4,640]{3,2,1,0:T(4,128)S(1)} %get-tuple-element.20.ac, f32[5,512,128]{2,1,0:T(8,128)S(1)} %get-tuple-element.24.acc, f32[5,104,128]{2,1,0:T(8,128)S(1)} %get-tuple-element.25.da_in, ...), custom_call_target="tpu_custom_call" | custom-call | flops 500000000 | bytes 4000000 | tf_op jit(solution)/shard_map/finish/pallas_call | solution.py:727
Async XLA Ops:
  0.6 18.8 %copy-start.2 = (f32[4,5,8,128]{3,2,1,0:T(8,128)S(1)}, f32[4,5,8,128]{3,2,1,0:T(8,128)}, u32[]{:S(2)}) copy-start(f32[4,5,8,128]{3,2,1,0:T(8,128)} %constant.8.clone.coef) | copy-start | bytes 245764
  0.6 18.8 %copy-start = (bf16[1280,640]{1,0:T(8,128)(2,1)S(1)}, bf16[1280,640]{1,0:T(8,128)(2,1)}, u32[]{:S(2)}) copy-start(bf16[1280,640]{1,0:T(8,128)(2,1)} %constant.6.clone.perm) | copy-start | bytes 4915204
  0.7 18.8 %copy-start.5 = (s32[1,1,1,768]{3,2,1,0:T(1,128)S(1)}, s32[1,1,1,768]{3,2,1,0:T(1,128)}, u32[]{:S(2)}) copy-start(s32[1,1,1,768]{3,2,1,0:T(1,128)} %param.20) | copy-start | bytes 9220
  0.7 18.8 %copy-start.4 = (s32[1,1,1,768]{3,2,1,0:T(1,128)S(1)}, s32[1,1,1,768]{3,2,1,0:T(1,128)}, u32[]{:S(2)}) copy-start(s32[1,1,1,768]{3,2,1,0:T(1,128)} %param.19) | copy-start | bytes 9220
  0.7 18.8 %copy-start.6 = (s32[1,1,1,128]{3,2,1,0:T(1,128)S(1)}, s32[1,1,1,128]{3,2,1,0:T(1,128)}, u32[]{:S(2)}) copy-start(s32[1,1,1,128]{3,2,1,0:T(1,128)} %param.18) | copy-start | bytes 1540
  0.7 18.8 %copy-start.3 = (f32[8,125,125]{2,0,1:T(8,128)S(1)}, f32[8,125,125]{2,0,1:T(8,128)}, u32[]{:S(2)}) copy-start(f32[8,125,125]{2,0,1:T(8,128)} %param.17) | copy-start | bytes 1500004
  3.6 23.0 %collective-permute-start.4 = (f32[5,224,128]{2,1,0:T(8,128)S(1)}, f32[5,224,128]{2,1,0:T(8,128)S(1)}, u32[]{:S(2)}, u32[]{:S(2)}) collective-permute-start(f32[5,224,128]{2,1,0:T(8,128)S(1)} %get-tuple-element.29.back), channel_id=1, source_target_pairs={{0,248},{8,0},{16,8},{24,16},{32,24},{40,32},{48,40},{56,48},{64,5... | collective-permute-start | bytes 1720328 | tf_op jit(solution)/shard_map/ppermute | solution.py:698
  12.3 14.3 %collective-permute-start.3 = (f32[160,128]{1,0:T(8,128)S(1)}, f32[160,128]{1,0:T(8,128)S(1)}, u32[]{:S(2)}, u32[]{:S(2)}) collective-permute-start(f32[160,128]{1,0:T(8,128)S(1)} %get-tuple-element.33.axial), channel_id=1, source_target_pairs={{0,1},{1,0},{2,3},{3,2},{4,5},{5,4},{6,7},{7,6},{8,9},{9,8},{10,11... | collective-permute-start | bytes 245768 | tf_op jit(solution)/shard_map/ppermute | solution.py:702
  13.6 13.0 %collective-permute-start = (f32[5,96,128]{2,1,0:T(8,128)S(1)}, f32[5,96,128]{2,1,0:T(8,128)S(1)}, u32[]{:S(2)}, u32[]{:S(2)}) collective-permute-start(f32[5,96,128]{2,1,0:T(8,128)S(1)} %get-tuple-element.30.fwd), channel_id=1, source_target_pairs={{0,8},{8,16},{16,24},{24,32},{32,40},{40,48},{48,56},{56,64},{64,7... | collective-permute-start | bytes 737288 | tf_op jit(solution)/shard_map/ppermute | solution.py:699
  13.6 13.0 %collective-permute-start.1 = (f32[5,96,128]{2,1,0:T(8,128)S(1)}, f32[5,96,128]{2,1,0:T(8,128)S(1)}, u32[]{:S(2)}, u32[]{:S(2)}) collective-permute-start(f32[5,96,128]{2,1,0:T(8,128)S(1)} %get-tuple-element.31.inner), channel_id=1, source_target_pairs={{0,2},{2,0},{4,6},{6,4},{1,3},{3,1},{5,7},{7,5},{8,10},{10,8},{12,... | collective-permute-start | bytes 737288 | tf_op jit(solution)/shard_map/ppermute | solution.py:700
  14.8 11.8 %collective-permute-start.2 = (f32[5,96,128]{2,1,0:T(8,128)S(1)}, f32[5,96,128]{2,1,0:T(8,128)S(1)}, u32[]{:S(2)}, u32[]{:S(2)}) collective-permute-start(f32[5,96,128]{2,1,0:T(8,128)S(1)} %get-tuple-element.32.outer), channel_id=1, source_target_pairs={{2,4},{4,2},{3,5},{5,3},{10,12},{12,10},{11,13},{13,11},{18,20},{2... | collective-permute-start | bytes 737288 | tf_op jit(solution)/shard_map/ppermute | solution.py:701
  19.5 7.1 %copy-start.1 = (bf16[1280,640]{1,0:T(8,128)(2,1)S(1)}, bf16[1280,640]{1,0:T(8,128)(2,1)}, u32[]{:S(2)}) copy-start(bf16[1280,640]{1,0:T(8,128)(2,1)} %constant.7.clone.perm_t) | copy-start | bytes 4915204
